TPU v7x, 32 devices: a whole 2x2x4 slice. The times are simulated.
32 devices in a mesh: ctx: 8 (over z, x), tp: 4 (over y, core).
Axes of the slice: x: 2, y: 2, z: 4, core: 2. Of those that a mesh axis runs over, the one named last changes fastest.
Arguments:
- tokens_in: bfloat16 [2048, 2048], P('ctx'), may hold values from -6 to 6
- block_order: int32 [2, 8], replicated, may hold values from 0 to 7, each once within a row
- routes: int32 [2048, 8], P('ctx'), may hold values from 0 to 31, all different within a row; in each aligned block of 256 rows (0 to 255, 256 to 511, ...) at most 128 rows name the same one
- norm1_gain: float32 [2048], replicated, may hold values from 0.5 to 1.5
- w_query: bfloat16 [2048, 4096], P(None, 'tp'), may hold values from -0.125 to 0.125
- key_weight: bfloat16 [2048, 512], P(None, 'tp'), may hold values from -0.125 to 0.125
- value_weight: bfloat16 [2048, 512], P(None, 'tp'), may hold values from -0.125 to 0.125
- query_gain: float32 [128], replicated, may hold values from 0.5 to 1.5
- key_gain: float32 [128], replicated, may hold values from 0.5 to 1.5
- w_out: bfloat16 [4096, 2048], P('tp'), may hold values from -1.5 to 1.5
- norm2_gain: float32 [2048], replicated, may hold values from 0.5 to 1.5
- w_router: bfloat16 [2048, 32], replicated, may hold values from -0.0625 to 0.0625
- w_gate: bfloat16 [32, 2048, 768], P('ctx', None, 'tp'), may hold values from -0.125 to 0.125
- w_up: bfloat16 [32, 2048, 768], P('ctx', None, 'tp'), may hold values from -0.125 to 0.125
- w_down: bfloat16 [32, 768, 2048], P('ctx', 'tp'), may hold values from -0.875 to 0.875
- cotangent: bfloat16 [2048, 2048], P('ctx'), may hold values from -6 to 6
Outputs:
- layer_out: bfloat16 [2048, 2048], P('ctx')
- grad_input: bfloat16 [2048, 2048], P('ctx')
- grad_norm1: float32 [2048], P('ctx')
- grad_query: float32 [2048, 4096], P('ctx', 'tp')
- grad_key: float32 [2048, 512], P('ctx', 'tp')
- grad_value: float32 [2048, 512], P('ctx', 'tp')
- grad_qgain: float32 [128], P('ctx')
- grad_kgain: float32 [128], P('ctx')
- grad_out: float32 [4096, 2048], P('tp', 'ctx')
- grad_norm2: float32 [2048], P('ctx')
- grad_router: float32 [2048, 32], P('ctx')
- grad_gate: float32 [32, 2048, 768], P('ctx', None, 'tp')
- grad_up: float32 [32, 2048, 768], P('ctx', None, 'tp')
- grad_down: float32 [32, 768, 2048], P('ctx', 'tp')
Inputs may be any that keep to these rules, and one draw needn't show every extreme that they name: `block_order`: each row is a permutation: the ctx indices hold different block pairs of each sequence. `routes`: A token's 8 experts differ; among the rows of one ctx index no expert is named more than 128 times, a bound that some block reaches.
All inputs are finite; a program needn't handle non-finite values.
Results may differ from a plain program's by a relative error of at most 0.03.
Values may be sent and summed in bfloat16 or wider, within the bound.
A program may use at most 320 MiB of HBM per device.

v0:
```python
import math

import jax
import jax.numpy as jnp
from jax import lax
from jax.sharding import PartitionSpec as P

EPSILON = 1e-06
ROPE_BASE = 1000000.0
MASKED_SCORE = -1000000000.0


def rms_norm(values, gain_vec):
    factor = lax.rsqrt(jnp.mean(values * values, axis=-1, keepdims=True) + EPSILON)
    return values * factor * gain_vec


def soft_rows(scores):
    row_top = jnp.max(scores, axis=-1, keepdims=True)
    exp_scores = jnp.exp(scores - row_top)
    return exp_scores / jnp.sum(exp_scores, axis=-1, keepdims=True)


def silu_mix(gate_pre, up_pre):
    return gate_pre / (1.0 + jnp.exp(-gate_pre)) * up_pre


def rotate(values, rotary_angles):
    half_size = values.shape[-1] // 2
    first_half = values[..., :half_size]
    second_half = values[..., half_size:]
    cosine = jnp.cos(rotary_angles)
    sine_part = jnp.sin(rotary_angles)
    return jnp.concatenate(
        [
            first_half * cosine - second_half * sine_part,
            second_half * cosine + first_half * sine_part,
        ],
        axis=-1,
    )


def angles_of(token_positions, head_width):
    freq_steps = jnp.arange(head_width // 2).astype(jnp.float32) * (2.0 / head_width)
    frequency = jnp.exp(-math.log(ROPE_BASE) * freq_steps)
    return token_positions.astype(jnp.float32)[..., None] * frequency


def positions_of(block_order, dev_count, block_len):
    first_block = jnp.transpose(block_order)
    block_pair = jnp.stack([first_block, 2 * dev_count - 1 - first_block], axis=-1)
    spread = block_pair[..., None] * block_len + jnp.arange(block_len, dtype=jnp.int32)
    return spread.reshape(dev_count, block_order.shape[0], 2 * block_len)


def head_route_path(raw_heads, gain_vec, rotary_angles, head_count):
    shaped = raw_heads.reshape(raw_heads.shape[0], head_count, -1)
    return rotate(rms_norm(shaped, gain_vec), rotary_angles[:, None, :])


def dispatch(buffer):
    return lax.all_to_all(buffer, "ctx", split_axis=0, concat_axis=1, tiled=True)


def send_back(buffer):
    return lax.all_to_all(buffer, "ctx", split_axis=1, concat_axis=0, tiled=True)


def attend_forward(seq_item):
    query_matrix, every_key_row, every_value_row, query_pos, key_pos = seq_item
    score_scale = 1.0 / math.sqrt(query_matrix.shape[-1])
    unscaled_scores = jnp.einsum(
        "upnj,apj->upna", query_matrix, every_key_row, preferred_element_type=jnp.float32
    )
    allowed = query_pos[:, None, None, None] >= key_pos[None, None, None, :]
    scores = jnp.where(allowed, unscaled_scores * score_scale, MASKED_SCORE)
    row_top = jnp.max(scores, axis=-1, keepdims=True)
    exp_scores = jnp.exp(scores - row_top)
    totals = jnp.sum(exp_scores, axis=-1, keepdims=True)
    lower_attention_probs = (exp_scores / totals).astype(jnp.bfloat16)
    attended_mix = jnp.einsum(
        "jzfq,qzx->jzfx", lower_attention_probs, every_value_row, preferred_element_type=jnp.float32
    )
    return (attended_mix, (row_top + jnp.log(totals))[..., 0])


def attend_backward(seq_item):
    (
        query_matrix,
        every_key_row,
        every_value_row,
        query_pos,
        key_pos,
        grad_attended_mix,
        log_total,
    ) = seq_item
    score_scale = 1.0 / math.sqrt(query_matrix.shape[-1])
    unscaled_scores = jnp.einsum(
        "upnj,apj->upna", query_matrix, every_key_row, preferred_element_type=jnp.float32
    )
    allowed = query_pos[:, None, None, None] >= key_pos[None, None, None, :]
    scores = jnp.where(allowed, unscaled_scores * score_scale, MASKED_SCORE)
    attention_probs = jnp.exp(scores - log_total[..., None])
    grad_probs = jnp.einsum(
        "upnj,apj->upna", grad_attended_mix, every_value_row, preferred_element_type=jnp.float32
    )
    row_inner = jnp.sum(attention_probs * grad_probs, axis=-1, keepdims=True)
    grad_score_dots = (attention_probs * (grad_probs - row_inner) * score_scale).astype(
        jnp.bfloat16
    )
    grad_queries = jnp.einsum(
        "jzfq,qzx->jzfx", grad_score_dots, every_key_row, preferred_element_type=jnp.float32
    )
    grad_key_rows = jnp.einsum(
        "axfv,axfz->vxz", grad_score_dots, query_matrix, preferred_element_type=jnp.float32
    )
    grad_values = jnp.einsum(
        "axfv,axfz->vxz",
        attention_probs.astype(jnp.bfloat16),
        grad_attended_mix,
        preferred_element_type=jnp.float32,
    )
    return (grad_queries, grad_key_rows, grad_values)


def shards(
    tokens_in,
    block_order,
    routes,
    norm1_gain,
    w_query,
    key_weight,
    value_weight,
    query_gain,
    key_gain,
    w_out,
    norm2_gain,
    w_router,
    w_gate,
    w_up,
    w_down,
    cotangent,
):
    tok_count = tokens_in.shape[0]
    model_width = tokens_in.shape[1]
    head_size = query_gain.shape[0]
    local_heads = w_query.shape[1] // head_size
    local_kv = key_weight.shape[1] // head_size
    query_group_width = local_heads // local_kv
    seq_count = block_order.shape[0]
    devices = lax.axis_size("ctx")
    block_len = tok_count // (2 * seq_count)
    top_count = routes.shape[1]
    experts = w_router.shape[1]
    capacity = 2 * tok_count * top_count // experts
    assigned = tok_count * top_count
    token_positions = positions_of(block_order, devices, block_len)
    query_pos = lax.dynamic_index_in_dim(token_positions, lax.axis_index("ctx"), 0, keepdims=False)
    key_pos = jnp.transpose(token_positions, (1, 0, 2)).reshape(seq_count, devices * 2 * block_len)
    rotary_angles = angles_of(query_pos.reshape(-1), head_size)
    inputs = tokens_in.astype(jnp.float32)
    first_normed, first_back = jax.vjp(rms_norm, inputs, norm1_gain)
    first_in = first_normed.astype(jnp.bfloat16)
    query_raw = jnp.dot(first_in, w_query, preferred_element_type=jnp.float32)
    unrotated_key = jnp.dot(first_in, key_weight, preferred_element_type=jnp.float32)
    value_input_rows = jnp.dot(first_in, value_weight, preferred_element_type=jnp.float32).astype(
        jnp.bfloat16
    )

    def rope_heads(raw_query, raw_key, gain_query, key_norm_gain):
        return (
            head_route_path(raw_query, gain_query, rotary_angles, local_heads),
            head_route_path(raw_key, key_norm_gain, rotary_angles, local_kv),
        )

    (query_rot, key_rot), rope_back = jax.vjp(
        rope_heads, query_raw, unrotated_key, query_gain, key_gain
    )
    query_input_rows = query_rot.astype(jnp.bfloat16).reshape(
        seq_count, 2 * block_len, local_kv, query_group_width, head_size
    )
    key_flat = key_rot.astype(jnp.bfloat16).reshape(seq_count, 2 * block_len * local_kv * head_size)
    value_flat = value_input_rows.reshape(seq_count, 2 * block_len * local_kv * head_size)
    key_seen, value_seen = (
        lax.all_gather(key_flat, "ctx", axis=1, tiled=True),
        lax.all_gather(value_flat, "ctx", axis=1, tiled=True),
    )
    seen_shape = (seq_count, devices * 2 * block_len, local_kv, head_size)
    key_full = key_seen.reshape(seen_shape)
    value_full = value_seen.reshape(seen_shape)
    attended_mix, log_total = lax.map(
        attend_forward, (query_input_rows, key_full, value_full, query_pos, key_pos)
    )
    attended = attended_mix.reshape(tok_count, local_heads * head_size).astype(jnp.bfloat16)
    attn_part = jnp.dot(attended, w_out, preferred_element_type=jnp.float32)
    residual = inputs + lax.psum(attn_part.astype(jnp.bfloat16), "tp").astype(jnp.float32)
    second_normed, second_back = jax.vjp(rms_norm, residual, norm2_gain)
    second_in = second_normed.astype(jnp.bfloat16)
    logits = jnp.dot(second_in, w_router, preferred_element_type=jnp.float32)
    choose = (routes[:, :, None] == jnp.arange(experts, dtype=jnp.int32)).astype(jnp.float32)
    picked = jnp.sum(choose * logits[:, None, :], axis=2)
    gate_weights, gate_back = jax.vjp(soft_rows, picked)
    flat_routes = routes.reshape(-1)
    route_hits = (flat_routes[:, None] == jnp.arange(experts, dtype=jnp.int32)).astype(jnp.int32)
    slot_index = jnp.sum((jnp.cumsum(route_hits, axis=0) - route_hits) * route_hits, axis=1)
    target = flat_routes * capacity + slot_index
    slot_table = (
        jnp.full((experts * capacity,), assigned, jnp.int32)
        .at[target]
        .set(jnp.arange(assigned, dtype=jnp.int32))
    )
    source_rows = slot_table // top_count
    padded_in = jnp.concatenate([second_in, jnp.zeros((1, model_width), jnp.bfloat16)], axis=0)
    received = dispatch(padded_in[source_rows].reshape(experts, capacity, model_width))
    gate_pre = jnp.einsum("erd,edf->erf", received, w_gate, preferred_element_type=jnp.float32)
    up_pre = jnp.einsum("erd,edf->erf", received, w_up, preferred_element_type=jnp.float32)
    hidden, hidden_back = jax.vjp(silu_mix, gate_pre, up_pre)
    hidden_in = hidden.astype(jnp.bfloat16)
    expert_out = jnp.einsum(
        "erf,efd->erd", hidden_in, w_down, preferred_element_type=jnp.float32
    ).astype(jnp.bfloat16)
    returned = send_back(expert_out)
    col_width = returned.shape[2]
    route_out = returned.reshape(experts * capacity, col_width)[target].reshape(
        tok_count, top_count, col_width
    )
    moe_part = jnp.einsum("tk,tkd->td", gate_weights, route_out, preferred_element_type=jnp.float32)
    grad_layer = cotangent.astype(jnp.float32)
    moe_total = lax.psum(moe_part.astype(jnp.bfloat16), "tp").astype(jnp.float32)
    layer_sum = residual + moe_total
    layer_out = layer_sum.astype(jnp.bfloat16)
    gate_part = jnp.einsum("td,tkd->tk", grad_layer, route_out, preferred_element_type=jnp.float32)
    grad_routed = (
        (gate_weights[:, :, None] * grad_layer[:, None, :])
        .astype(jnp.bfloat16)
        .reshape(assigned, model_width)
    )
    padded_grad = jnp.concatenate([grad_routed, jnp.zeros((1, model_width), jnp.bfloat16)], axis=0)
    grad_received = dispatch(padded_grad[slot_table].reshape(experts, capacity, model_width))
    grad_down = jnp.einsum(
        "erf,erd->efd", hidden_in, grad_received, preferred_element_type=jnp.float32
    )
    grad_hidden = jnp.einsum(
        "erd,efd->erf", grad_received, w_down, preferred_element_type=jnp.float32
    )
    grad_gate_pre, grad_up_pre = hidden_back(grad_hidden)
    gate_low = grad_gate_pre.astype(jnp.bfloat16)
    up_low = grad_up_pre.astype(jnp.bfloat16)
    grad_gate = jnp.einsum("erd,erf->edf", received, gate_low, preferred_element_type=jnp.float32)
    grad_up = jnp.einsum("erd,erf->edf", received, up_low, preferred_element_type=jnp.float32)
    grad_entry = jnp.einsum("erf,edf->erd", gate_low, w_gate, preferred_element_type=jnp.float32)
    grad_entry = (
        grad_entry + jnp.einsum("erf,edf->erd", up_low, w_up, preferred_element_type=jnp.float32)
    ).astype(jnp.bfloat16)
    grad_returned = send_back(grad_entry).reshape(experts * capacity, col_width)
    second_part = jnp.sum(
        grad_returned[target].reshape(tok_count, top_count, col_width), axis=1, dtype=jnp.float32
    )
    grad_second_exp, gate_total = (
        lax.psum(second_part.astype(jnp.bfloat16), "tp").astype(jnp.float32),
        lax.psum(gate_part.astype(jnp.bfloat16), "tp").astype(jnp.float32),
    )
    (grad_picked,) = gate_back(gate_total)
    grad_logits = jnp.einsum("tk,tke->te", grad_picked, choose).astype(jnp.bfloat16)
    grad_router = jnp.einsum(
        "td,te->de", second_in, grad_logits, preferred_element_type=jnp.float32
    )
    grad_second = grad_second_exp + jnp.einsum(
        "te,de->td", grad_logits, w_router, preferred_element_type=jnp.float32
    )
    grad_resid_norm, grad_norm2 = second_back(grad_second)
    grad_residual = grad_layer + grad_resid_norm
    grad_attn_low = grad_residual.astype(jnp.bfloat16)
    grad_out = jnp.einsum("tc,td->cd", attended, grad_attn_low, preferred_element_type=jnp.float32)
    grad_attended_mix = jnp.einsum(
        "td,cd->tc", grad_attn_low, w_out, preferred_element_type=jnp.float32
    ).astype(jnp.bfloat16)
    grad_attended_mix = grad_attended_mix.reshape(
        seq_count, 2 * block_len, local_kv, query_group_width, head_size
    )
    grad_query_seq, grad_key_seq, grad_value_seq = lax.map(
        attend_backward,
        (query_input_rows, key_full, value_full, query_pos, key_pos, grad_attended_mix, log_total),
    )
    grad_key_own, grad_value_own = (
        lax.psum_scatter(
            grad_key_seq.reshape(seq_count, -1).astype(jnp.bfloat16),
            "ctx",
            scatter_dimension=1,
            tiled=True,
        ).astype(jnp.float32),
        lax.psum_scatter(
            grad_value_seq.reshape(seq_count, -1).astype(jnp.bfloat16),
            "ctx",
            scatter_dimension=1,
            tiled=True,
        ).astype(jnp.float32),
    )
    grad_query_rot = grad_query_seq.reshape(tok_count, local_heads, head_size)
    grad_key_rot = grad_key_own.reshape(tok_count, local_kv, head_size)
    grad_query_raw, grad_key_raw, grad_qgain_part, grad_kgain_part = rope_back(
        (grad_query_rot, grad_key_rot)
    )
    query_low = grad_query_raw.astype(jnp.bfloat16)
    key_low = grad_key_raw.astype(jnp.bfloat16)
    value_low = grad_value_own.reshape(tok_count, local_kv * head_size).astype(jnp.bfloat16)
    grad_query = jnp.einsum("td,tc->dc", first_in, query_low, preferred_element_type=jnp.float32)
    grad_key = jnp.einsum("td,tc->dc", first_in, key_low, preferred_element_type=jnp.float32)
    grad_value = jnp.einsum("td,tc->dc", first_in, value_low, preferred_element_type=jnp.float32)
    first_part = jnp.einsum("tc,dc->td", query_low, w_query, preferred_element_type=jnp.float32)
    first_part = first_part + jnp.einsum(
        "tc,dc->td", key_low, key_weight, preferred_element_type=jnp.float32
    )
    first_part = first_part + jnp.einsum(
        "tc,dc->td", value_low, value_weight, preferred_element_type=jnp.float32
    )
    grad_first, qgain_total, kgain_total = (
        lax.psum(first_part.astype(jnp.bfloat16), "tp").astype(jnp.float32),
        lax.psum(grad_qgain_part.astype(jnp.bfloat16), "tp").astype(jnp.float32),
        lax.psum(grad_kgain_part.astype(jnp.bfloat16), "tp").astype(jnp.float32),
    )
    grad_input_norm, grad_norm1 = first_back(grad_first)
    grad_input = (grad_residual + grad_input_norm).astype(jnp.bfloat16)
    summed_grads = (
        lax.psum_scatter(
            grad_norm1.astype(jnp.bfloat16), "ctx", scatter_dimension=0, tiled=True
        ).astype(jnp.float32),
        lax.psum_scatter(
            grad_query.astype(jnp.bfloat16), "ctx", scatter_dimension=0, tiled=True
        ).astype(jnp.float32),
        lax.psum_scatter(
            grad_key.astype(jnp.bfloat16), "ctx", scatter_dimension=0, tiled=True
        ).astype(jnp.float32),
        lax.psum_scatter(
            grad_value.astype(jnp.bfloat16), "ctx", scatter_dimension=0, tiled=True
        ).astype(jnp.float32),
        lax.psum_scatter(
            qgain_total.astype(jnp.bfloat16), "ctx", scatter_dimension=0, tiled=True
        ).astype(jnp.float32),
        lax.psum_scatter(
            kgain_total.astype(jnp.bfloat16), "ctx", scatter_dimension=0, tiled=True
        ).astype(jnp.float32),
        lax.psum_scatter(
            grad_out.astype(jnp.bfloat16), "ctx", scatter_dimension=1, tiled=True
        ).astype(jnp.float32),
        lax.psum_scatter(
            grad_norm2.astype(jnp.bfloat16), "ctx", scatter_dimension=0, tiled=True
        ).astype(jnp.float32),
        lax.psum_scatter(
            grad_router.astype(jnp.bfloat16), "ctx", scatter_dimension=0, tiled=True
        ).astype(jnp.float32),
    )
    return (
        layer_out,
        grad_input,
        summed_grads[0],
        summed_grads[1],
        summed_grads[2],
        summed_grads[3],
        summed_grads[4],
        summed_grads[5],
        summed_grads[6],
        summed_grads[7],
        summed_grads[8],
        grad_gate,
        grad_up,
        grad_down,
    )


def solution(mesh):
    in_specs = (
        P("ctx", None),
        P(),
        P("ctx", None),
        P(),
        P(None, "tp"),
        P(None, "tp"),
        P(None, "tp"),
        P(),
        P(),
        P("tp", None),
        P(),
        P(),
        P("ctx", None, "tp"),
        P("ctx", None, "tp"),
        P("ctx", "tp", None),
        P("ctx", None),
    )
    out_specs = (
        P("ctx", None),
        P("ctx", None),
        P("ctx"),
        P("ctx", "tp"),
        P("ctx", "tp"),
        P("ctx", "tp"),
        P("ctx"),
        P("ctx"),
        P("tp", "ctx"),
        P("ctx"),
        P("ctx", None),
        P("ctx", None, "tp"),
        P("ctx", None, "tp"),
        P("ctx", "tp", None),
    )
    return jax.shard_map(shards, mesh=mesh, in_specs=in_specs, out_specs=out_specs, check_vma=False)
```

profile of v0, /device:TPU:0, one launch (start us, length us, event | category | flops | bytes accessed | tf_op | source)
XLA Modules:
  0.0 3493.5 jit_solution(18350877095937985611)
XLA Ops:
  24.2 33.3 all_gather.7
  58.4 31.7 all_gather.6
  187.5 35.8 %gather_fusion.2 = bf16[4096,2048]{1,0:T(8,128)(2,1)} fusion(bf16[2049,2048]{1,0:T(8,128)(2,1)} %concatenate.36, s32[4096]{0:T(1024)S(1)} %get-tuple-element.312), kind=kCustom, calls=%fused_computation.2 | custom fusion | bytes 33570816 | tf_op jit(solution)/shard_map/gather | solution.py:239
  231.4 32.7 gather_fusion
  264.1 327.9 %all-to-all-done.2 = bf16[32,128,2048]{2,1,0:T(8,128)(2,1)} async-done(((bf16[32,128,2048]{2,1,0:T(8,128)(2,1)}), bf16[32,128,2048]{2,1,0:T(8,128)(2,1)}, u32[]{:S(2)}, u32[]{:S(2)}) %all-to-all-start.2) | async-done | bytes 16777248 | tf_op jit(solution)/shard_map/all_to_all | solution.py:62
  612.3 347.8 %all-to-all-done = bf16[32,128,2048]{2,1,0:T(8,128)(2,1)} async-done(((bf16[32,128,2048]{2,1,0:T(8,128)(2,1)}), bf16[32,128,2048]{2,1,0:T(8,128)(2,1)}, u32[]{:S(2)}, u32[]{:S(2)}) %all-to-all-start) | async-done | bytes 16777248 | tf_op jit(solution)/shard_map/all_to_all | solution.py:62
  1018.7 22.1 copy.209
  1078.6 22.1 copy.213
  1100.7 307.4 %all-to-all-done.1 = bf16[4,1024,2048]{2,0,1:T(4,128)(2,1)} async-done(((bf16[4,1024,2048]{2,0,1:T(4,128)(2,1)}), bf16[4,1024,2048]{2,0,1:T(4,128)(2,1)}, u32[]{:S(2)}, u32[]{:S(2)}) %all-to-all-start.1) | async-done | bytes 16777248 | tf_op jit(solution)/shard_map/all_to_all | solution.py:66
  1432.6 24.3 gather_fusion.1
  1472.0 303.7 %all-to-all-done.3 = bf16[4,1024,2048]{2,0,1:T(4,128)(2,1)} async-done(((bf16[4,1024,2048]{2,0,1:T(4,128)(2,1)}), bf16[4,1024,2048]{2,0,1:T(4,128)(2,1)}, u32[]{:S(2)}, u32[]{:S(2)}) %all-to-all-start.3) | async-done | bytes 16777248 | tf_op jit(solution)/shard_map/all_to_all | solution.py:66
  1794.3 24.7 gather_fusion.3
  1830.5 35.6 %all-reduce.19.cloned.1.call-done = bf16[256,2048]{1,0:T(8,128)(2,1)} async-done(((bf16[256,2048]{1,0:T(8,128)(2,1)}), bf16[256,2048]{1,0:T(8,128)(2,1)}) %all-reduce.19.cloned.1.call-update) | async-done | bytes 1048592 | tf_op jit(solution)/shard_map/psum | solution.py:260
  1874.0 27.7 while.27
  1901.7 53.0 %copy.250 = bf16[2,1024,1,128]{0,3,1,2:T(8,128)(2,1)} copy(bf16[2,1024,1,128]{1,3,2,0:T(8,128)(2,1)} %get-tuple-element.120) | data formatting | bytes 1048576
  1962.2 53.0 %copy.249 = bf16[2,1024,1,128]{0,3,1,2:T(8,128)(2,1)} copy(bf16[2,1024,1,128]{1,3,2,0:T(8,128)(2,1)} %get-tuple-element.119) | data formatting | bytes 1048576
  2027.2 470.9 %reduce-scatter.24.cloned.1.call-done = bf16[16384,2]{1,0:T(8,128)(2,1)} async-done(((bf16[131072,2]{1,0:T(8,128)(2,1)}), bf16[16384,2]{1,0:T(8,128)(2,1)}) %reduce-scatter.24.cloned.1.call-update) | async-done | bytes 65552
  2502.6 541.5 %reduce-scatter.22.cloned.1.call-done = bf16[16384,2]{1,0:T(8,128)(2,1)} async-done(((bf16[131072,2]{1,0:T(8,128)(2,1)}), bf16[16384,2]{1,0:T(8,128)(2,1)}) %reduce-scatter.22.cloned.1.call-update) | async-done | bytes 65552
  3108.7 21.9 all-reduce.10
  3130.8 41.1 %reduce-scatter.20.cloned.1.call-done = bf16[256,32]{0,1:T(8,128)(2,1)} async-done(((bf16[2048,32]{0,1:T(8,128)(2,1)}), bf16[256,32]{0,1:T(8,128)(2,1)}) %reduce-scatter.20.cloned.1.call-update) | async-done | bytes 16400 | tf_op jit(solution)/shard_map/reduce_scatter | solution.py:349
  3179.9 56.7 %reduce-scatter.16.cloned.1.call-done = bf16[256,128]{1,0:T(8,128)(2,1)} async-done(((bf16[2048,128]{1,0:T(8,128)(2,1)}), bf16[256,128]{1,0:T(8,128)(2,1)}) %reduce-scatter.16.cloned.1.call-update) | async-done | bytes 65552 | tf_op jit(solution)/shard_map/reduce_scatter | solution.py:334
  3238.1 63.4 %reduce-scatter.14.cloned.1.call-done = bf16[256,128]{1,0:T(8,128)(2,1)} async-done(((bf16[2048,128]{1,0:T(8,128)(2,1)}), bf16[256,128]{1,0:T(8,128)(2,1)}) %reduce-scatter.14.cloned.1.call-update) | async-done | bytes 65552 | tf_op jit(solution)/shard_map/reduce_scatter | solution.py:331
  3309.1 83.4 %reduce-scatter.12.cloned.1.call-done = bf16[256,1024]{1,0:T(8,128)(2,1)} async-done(((bf16[2048,1024]{1,0:T(8,128)(2,1)}), bf16[256,1024]{1,0:T(8,128)(2,1)}) %reduce-scatter.12.cloned.1.call-update) | async-done | bytes 524304 | tf_op jit(solution)/shard_map/reduce_scatter | solution.py:328
  3394.7 89.6 %reduce-scatter.18.cloned.1.call-done = bf16[1024,256]{1,0:T(8,128)(2,1)} async-done(((bf16[1024,2048]{1,0:T(8,128)(2,1)}), bf16[1024,256]{1,0:T(8,128)(2,1)}) %reduce-scatter.18.cloned.1.call-update) | async-done | bytes 524304 | tf_op jit(solution)/shard_map/reduce_scatter | solution.py:343
  (421 shorter events, 465.4 us)
Async XLA Ops:
  7.2 989.3 %copy-start = (bf16[4,192,2048]{2,1,0:T(8,128)(2,1)S(1)}, bf16[4,192,2048]{2,1,0:T(8,128)(2,1)}, u32[]{:S(2)}) copy-start(bf16[4,192,2048]{2,1,0:T(8,128)(2,1)} %param.34) | copy-start | bytes 9437188
  7.2 159.0 %all-reduce.17.cloned.1.call-start = ((), (), s32[]{:S(2)}) async-start(), calls=%async_computation.11 | async-start | bytes 2097152 | tf_op jit(solution)/shard_map/psum | solution.py:196
  223.3 368.7 %all-to-all-start.2 = ((bf16[32,128,2048]{2,1,0:T(8,128)(2,1)}), bf16[32,128,2048]{2,1,0:T(8,128)(2,1)}, u32[]{:S(2)}, u32[]{:S(2)}) async-start(bf16[32,128,2048]{2,1,0:T(8,128)(2,1)} %bitcast.423), calls=%async_computation.2 | async-start | bytes 33554432 | tf_op jit(solution)/shard_map/all_to_all | solution.py:62
  591.9 368.2 %all-to-all-start = ((bf16[32,128,2048]{2,1,0:T(8,128)(2,1)}), bf16[32,128,2048]{2,1,0:T(8,128)(2,1)}, u32[]{:S(2)}, u32[]{:S(2)}) async-start(bf16[32,128,2048]{2,1,0:T(8,128)(2,1)} %bitcast.422), calls=%async_computation | async-start | bytes 33554432 | tf_op jit(solution)/shard_map/all_to_all | solution.py:62
  1040.8 367.3 %all-to-all-start.1 = ((bf16[4,1024,2048]{2,0,1:T(4,128)(2,1)}), bf16[4,1024,2048]{2,0,1:T(4,128)(2,1)}, u32[]{:S(2)}, u32[]{:S(2)}) async-start(bf16[4,1024,2048]{2,0,1:T(4,128)(2,1)} %copy.209), calls=%async_computation.1 | async-start | bytes 33554432 | tf_op jit(solution)/shard_map/all_to_all | solution.py:66
  1100.7 313.3 %copy-start.65 = (s32[2048,1]{0,1:T(1,128)S(1)}, s32[2048,1]{0,1:T(1,128)}, u32[]{:S(2)}) copy-start(s32[2048,1]{0,1:T(1,128)} %copy-done.64) | copy-start | bytes 24580
  1100.7 313.3 %copy-start.61 = (f32[256]{0:T(256)S(1)}, f32[256]{0:T(256)}, u32[]{:S(2)}) copy-start(f32[256]{0:T(256)} %copy-done.60) | copy-start | bytes 3076
  1408.1 367.6 %all-to-all-start.3 = ((bf16[4,1024,2048]{2,0,1:T(4,128)(2,1)}), bf16[4,1024,2048]{2,0,1:T(4,128)(2,1)}, u32[]{:S(2)}, u32[]{:S(2)}) async-start(bf16[4,1024,2048]{2,0,1:T(4,128)(2,1)} %copy.213), calls=%async_computation.3 | async-start | bytes 33554432 | tf_op jit(solution)/shard_map/all_to_all | solution.py:66
  1413.9 452.2 %all-reduce.19.cloned.1.call-start = ((), (), s32[]{:S(2)}) async-start(), calls=%async_computation.12 | async-start | bytes 2097152 | tf_op jit(solution)/shard_map/psum | solution.py:260
  1830.2 667.8 %reduce-scatter.24.cloned.1.call-start = ((), (), s32[]{:S(2)}) async-start(), calls=%async_computation.19 | async-start | bytes 37748736
  1954.7 1089.4 %reduce-scatter.22.cloned.1.call-start = ((), (), s32[]{:S(2)}) async-start(), calls=%async_computation.18 | async-start | bytes 37748736
  2016.6 1089.8 %all-reduce.21.cloned.1.call-start = ((), (), s32[]{:S(2)}) async-start(), calls=%async_computation.20 | async-start | bytes 4194304 | tf_op jit(solution)/shard_map/psum | solution.py:229
  2501.8 548.5 %copy-start.70 = (f32[1,2,128]{2,0,1:T(1,128)S(1)}, f32[1,2,128]{2,0,1:T(1,128)}, u32[]{:S(2)}) copy-start(f32[1,2,128]{2,0,1:T(1,128)} %copy-done.69) | copy-start | bytes 3076
  2501.9 548.5 %copy-start.80 = (f32[64]{0:T(128)S(1)}, f32[64]{0:T(128)}, u32[]{:S(2)}) copy-start(f32[64]{0:T(128)} %multiply_exponential_fusion) | copy-start | bytes 772
  2501.9 549.7 %copy-start.28 = (f32[256,128]{0,1:T(8,128)S(1)}, f32[256,128]{0,1:T(8,128)}, u32[]{:S(2)}) copy-start(f32[256,128]{0,1:T(8,128)} %copy-done.27) | copy-start | bytes 393220
  2501.9 549.7 %copy-start.71 = (f32[256]{0:T(256)S(1)}, f32[256]{0:T(256)}, u32[]{:S(2)}) copy-start(f32[256]{0:T(256)} %fusion.128) | copy-start | bytes 3076
  2501.9 549.7 %copy-start.79 = (f32[128]{0:T(128)S(1)}, f32[128]{0:T(128)}, u32[]{:S(2)}) copy-start(f32[128]{0:T(128)} %param.28) | copy-start | bytes 1540
  3055.6 116.3 %reduce-scatter.20.cloned.1.call-start = ((), (), s32[]{:S(2)}) async-start(), calls=%async_computation.17 | async-start | bytes 147456 | tf_op jit(solution)/shard_map/reduce_scatter | solution.py:349
  3056.6 179.9 %reduce-scatter.16.cloned.1.call-start = ((), (), s32[]{:S(2)}) async-start(), calls=%async_computation.15 | async-start | bytes 589824 | tf_op jit(solution)/shard_map/reduce_scatter | solution.py:334
  3058.1 243.3 %reduce-scatter.14.cloned.1.call-start = ((), (), s32[]{:S(2)}) async-start(), calls=%async_computation.14 | async-start | bytes 589824 | tf_op jit(solution)/shard_map/reduce_scatter | solution.py:331
  3059.6 333.0 %reduce-scatter.12.cloned.1.call-start = ((), (), s32[]{:S(2)}) async-start(), calls=%async_computation.13 | async-start | bytes 4718592 | tf_op jit(solution)/shard_map/reduce_scatter | solution.py:328
  3063.1 421.2 %reduce-scatter.18.cloned.1.call-start = ((), (), s32[]{:S(2)}) async-start(), calls=%async_computation.16 | async-start | bytes 4718592 | tf_op jit(solution)/shard_map/reduce_scatter | solution.py:343
  3096.5 207.0 %copy-start.75 = (f32[256]{0:T(256)S(1)}, f32[256]{0:T(256)}, u32[]{:S(2)}) copy-start(f32[256]{0:T(256)} %copy-done.74) | copy-start | bytes 3076
  3303.6 182.8 %copy-start.1 = (bf16[4,192,2048]{2,1,0:T(8,128)(2,1)S(1)}, bf16[4,192,2048]{2,1,0:T(8,128)(2,1)}, u32[]{:S(2)}) copy-start(bf16[4,192,2048]{2,1,0:T(8,128)(2,1)} %param.34) | copy-start | bytes 9437188
  (91 other events, 1292.4 us)
Sparse Core Ops, SparseCore 0:
  128.8 37.3 all-reduce.16
  1830.4 35.7 all-reduce.18
  1954.8 543.2 reduce-scatter.23
  2501.7 542.3 reduce-scatter.21
  3055.7 50.6 all-reduce.20
  3110.5 61.2 reduce-scatter.19
  3175.6 60.9 reduce-scatter.15
  3240.5 60.8 reduce-scatter.13
  3305.5 87.0 reduce-scatter.11
  3396.0 88.2 reduce-scatter.17
where the time goes:
time: 3500 us; the launch traced here: 3490 us
  waiting for transfers between devices  2680 us (77%)
  local copies, waits for them, and re-layouts  405 us (12%)
  matrix products  177 us (5%)
  blocking collectives  98.6 us (3%)
  other arithmetic  90.3 us (3%)
    unnamed x12, waiting for transfers between devices  1010 us
    all_to_all x2, waiting for transfers between devices, dispatch(): lax.all_to_all(buffer, 'ctx', split_axis=0, concat_axis=1, tiled=True)  676 us
    all_to_all x2, waiting for transfers between devices, send_back(): lax.all_to_all(buffer, 'ctx', split_axis=1, concat_axis=0, tiled=True)  611 us
    unnamed x177, local copies, waits for them, and re-layouts  127 us
    reduce_scatter x1, waiting for transfers between devices, shards(): lax.psum_scatter(grad_out.astype(jnp.bfloat16), 'ctx', scatter_dimension=...  89.6 us
    reduce_scatter x1, waiting for transfers between devices, shards(): lax.psum_scatter(grad_query.astype(jnp.bfloat16), 'ctx', scatter_dimensio...  83.4 us
  transfers between devices with their start and end apart: 14, of which 14 were waited for; matrix products, arithmetic and copies ran while one was open for 9% of the time, Pallas kernels for 0%

commit v1 on v0

v1 whole, which is shorter than its diff:
```python
import math
import jax
import jax.numpy as jnp
from jax import lax
from jax.sharding import PartitionSpec as P
from jax.experimental import pallas as pl
from jax.experimental.pallas import tpu as pltpu
MESH=pl.DeviceIdType.MESH

def coords():
    ctx=lax.axis_index("ctx"); tp=lax.axis_index("tp")
    return ctx//2, ctx%2, tp//2, tp%2
def dev(z,x,y,c): return (z*2+x, y*2+c)
def pid(z,x,y,c): return (z*2+x)*4+y*2+c

def neighbours():
    z,x,y,c=coords()
    ax=x+(1-c)*(1-2*x); ay=y+c*(1-2*y)
    bx=x+c*(1-2*x); by=y+(1-c)*(1-2*y)
    return z,x,y,c,ax,ay,bx,by

def barrier_all():
    z,x,y,c=coords()
    b=pltpu.get_barrier_semaphore()
    def sig(d): pl.semaphore_signal(b,inc=1,device_id=d,device_id_type=MESH)
    sig(dev(z,1-x,y,c)); sig(dev(z,x,1-y,c)); sig(dev(z,x,y,1-c))
    @pl.when(z<3)
    def _(): sig(dev(z+1,x,y,c))
    @pl.when(z>0)
    def _(): sig(dev(z-1,x,y,c))
    pl.semaphore_wait(b,5-(3-z)//3-z//3)

def ag32_kernel(x_ref,out_ref,lsem,send,recv):
    rows=x_ref.shape[0]
    z,x,y,c,ax,ay,bx,by=neighbours()
    barrier_all()
    me=pid(z,x,y,c)
    def at(p): return out_ref.at[pl.ds(pl.multiple_of(p*rows,rows),rows)]
    def cp(p,d,k,own=False):
        return pltpu.make_async_remote_copy(src_ref=x_ref if own else at(p),dst_ref=at(p),send_sem=send.at[k,p],recv_sem=recv.at[p],device_id=d,device_id_type=MESH)
    up,down,A,B,C=dev(z+1,x,y,c),dev(z-1,x,y,c),dev(z,ax,ay,c),dev(z,bx,by,c),dev(z,x,y,1-c)
    def wait(p):
        cp(p,C,4).wait_recv()
    loc=pltpu.make_async_copy(x_ref,at(me),lsem); loc.start()
    @pl.when(z<3)
    def _(): cp(me,up,0,True).start()
    @pl.when(z>0)
    def _(): cp(me,down,1,True).start()
    cp(me,A,2,True).start(); cp(me,B,3,True).start(); cp(me,C,4,True).start()
    def zlow(d):
        @pl.when(z-d>=0)
        def _():
            p=pid(z-d,x,y,c); wait(p)
            @pl.when(z<3)
            def _(): cp(p,up,0).start()
            cp(p,A,2).start(); cp(p,B,3).start(); cp(p,C,4).start()
    def zhigh(d):
        @pl.when(z+d<=3)
        def _():
            p=pid(z+d,x,y,c); wait(p)
            @pl.when(z>0)
            def _(): cp(p,down,1).start()
            cp(p,A,2).start(); cp(p,B,3).start(); cp(p,C,4).start()
    def fa(zz):
        @pl.when((zz>=0)&(zz<=3))
        def _():
            p=pid(zz,ax,ay,c); wait(p)
            cp(p,B,3).start(); cp(p,C,4).start()
    def fb(zz,xx,yy):
        @pl.when((zz>=0)&(zz<=3))
        def _():
            p=pid(zz,xx,yy,c); wait(p); cp(p,C,4).start()
    zlow(1); zhigh(1); fa(z); zlow(2); zhigh(2); fa(z-1); fa(z+1); fb(z,bx,by); zlow(3); zhigh(3)
    fa(z-2); fa(z+2); fb(z-1,bx,by); fb(z+1,bx,by); fa(z-3); fa(z+3)
    dx,dy=1-x,1-y
    fb(z,dx,dy); fb(z-2,bx,by); fb(z+2,bx,by); fb(z-1,dx,dy); fb(z+1,dx,dy); fb(z-3,bx,by); fb(z+3,bx,by); fb(z-2,dx,dy); fb(z+2,dx,dy); fb(z-3,dx,dy); fb(z+3,dx,dy)
    for zz in range(4):
        for xx in range(2):
            for yy in range(2):
                wait(pid(zz,xx,yy,1-c))
    loc.wait()
    for zz in range(4):
        p=pid(zz,x,y,c)
        @pl.when((z<3)&(zz<=z))
        def _(): cp(p,up,0).wait_send()
        @pl.when((z>0)&(zz>=z))
        def _(): cp(p,down,1).wait_send()
        cp(p,A,2).wait_send(); cp(p,B,3).wait_send(); cp(p,C,4).wait_send()
        q=pid(zz,ax,ay,c)
        cp(q,B,3).wait_send(); cp(q,C,4).wait_send()
        cp(pid(zz,bx,by,c),C,4).wait_send(); cp(pid(zz,dx,dy,c),C,4).wait_send()

def ag32(piece,cid=0):
    rows,w=piece.shape
    return pl.pallas_call(ag32_kernel,out_shape=jax.ShapeDtypeStruct((rows*32,w),piece.dtype),
        in_specs=[pl.BlockSpec(memory_space=pl.ANY)],out_specs=pl.BlockSpec(memory_space=pl.ANY),
        scratch_shapes=[pltpu.SemaphoreType.DMA,pltpu.SemaphoreType.DMA((5,32)),pltpu.SemaphoreType.DMA((32,))],
        compiler_params=pltpu.CompilerParams(collective_id=cid,has_side_effects=True))(piece)

def zmask(z):
    return (3-z)//3, (z%3)%2, (z%3)//2, z//3
def zfar(z,k):
    m0,m1,m2,m3=zmask(z)
    t=((3,2,1,0),(3,0,2,1),(0,3,1,2),(0,1,2,3))
    return m0*t[0][k]+m1*t[1][k]+m2*t[2][k]+m3*t[3][k]

def zreduce(z,x,y,c,load,zup,zdn,stage,zsend,zrecv,out_store):
    def cp(buf,zz,d,k,r):
        return pltpu.make_async_remote_copy(src_ref=stage.at[zz],dst_ref=buf.at[zz],send_sem=zsend.at[zz],recv_sem=zrecv.at[r,zz],device_id=d,device_id_type=MESH)
    up,down=dev(z+1,x,y,c),dev(z-1,x,y,c)
    for k in range(3):
        zz=zfar(z,k)
        @pl.when(zz>z)
        def _():
            stage[zz]=load(zz).astype(stage.dtype)
            @pl.when(z>0)
            def _():
                cp(zup,zz,up,0,0).wait_recv()
                stage[zz]=(stage[zz].astype(jnp.float32)+zup[zz].astype(jnp.float32)).astype(stage.dtype)
            cp(zup,zz,up,0,0).start()
        @pl.when(zz<z)
        def _():
            stage[zz]=load(zz).astype(stage.dtype)
            @pl.when(z<3)
            def _():
                cp(zdn,zz,down,1,1).wait_recv()
                stage[zz]=(stage[zz].astype(jnp.float32)+zdn[zz].astype(jnp.float32)).astype(stage.dtype)
            cp(zdn,zz,down,1,1).start()
    out_store(load(z),True)
    @pl.when(z>0)
    def _():
        cp(zup,z,up,0,0).wait_recv()
        out_store(zup[z].astype(jnp.float32),False)
    @pl.when(z<3)
    def _():
        cp(zdn,z,down,1,1).wait_recv()
        out_store(zdn[z].astype(jnp.float32),False)
    for k in range(3):
        zz=zfar(z,k)
        cp(zup,zz,up,0,0).wait_send()

def rs32_kernel(in_ref,out_ref,acc,cbuf,bbuf,abuf,zup,zdn,stage,lsem,csend,crecv,bsend,brecv,asend,arecv,zsend,zrecv):
    rows=out_ref.shape[0]
    z,x,y,c,ax,ay,bx,by=neighbours()
    dx,dy=1-x,1-y
    barrier_all()
    f32=jnp.float32
    A,B,C=dev(z,ax,ay,c),dev(z,bx,by,c),dev(z,x,y,1-c)
    def q(zz,xx,yy): return zz*4+xx*2+yy
    def at(p): return in_ref.at[pl.ds(pl.multiple_of(p*rows,rows),rows)]
    def ccopy(zz,xx,yy,cc):
        return pltpu.make_async_remote_copy(src_ref=at(pid(zz,xx,yy,cc)),dst_ref=cbuf.at[q(zz,xx,yy)],send_sem=csend.at[q(zz,xx,yy)],recv_sem=crecv.at[q(zz,xx,yy)],device_id=C,device_id_type=MESH)
    def lcopy(zz,xx,yy):
        return pltpu.make_async_copy(at(pid(zz,xx,yy,c)),acc.at[q(zz,xx,yy)],lsem.at[q(zz,xx,yy)])
    sides=[(dx,dy),(bx,by),(ax,ay),(x,y)]
    for (xx,yy) in sides:
        for k in range(4):
            zz=zfar(z,k)
            lcopy(zz,xx,yy).start()
    for (xx,yy) in [(dx,dy),(ax,ay),(bx,by),(x,y)]:
        for k in range(4):
            zz=zfar(z,k)
            ccopy(zz,xx,yy,1-c).start()
    def have_c(zz,xx,yy):
        lcopy(zz,xx,yy).wait(); ccopy(zz,xx,yy,1-c).wait_recv()
        i=q(zz,xx,yy)
        return acc[i].astype(f32)+cbuf[i].astype(f32)
    def bcopy(zz,far):
        xx,yy=(dx,dy) if far else (bx,by)
        i=zz+4*far
        return pltpu.make_async_remote_copy(src_ref=acc.at[q(zz,xx,yy)],dst_ref=bbuf.at[i],send_sem=bsend.at[i],recv_sem=brecv.at[i],device_id=B,device_id_type=MESH)
    for far in (1,0):
        xx,yy=(dx,dy) if far else (bx,by)
        for k in range(4):
            zz=zfar(z,k)
            acc[q(zz,xx,yy)]=have_c(zz,xx,yy).astype(acc.dtype)
            bcopy(zz,far).start()
    def acopy(zz):
        return pltpu.make_async_remote_copy(src_ref=acc.at[q(zz,ax,ay)],dst_ref=abuf.at[zz],send_sem=asend.at[zz],recv_sem=arecv.at[zz],device_id=A,device_id_type=MESH)
    for k in range(4):
        zz=zfar(z,k)
        v=have_c(zz,ax,ay)
        bcopy(zz,1).wait_recv()
        acc[q(zz,ax,ay)]=(v+bbuf[zz+4].astype(f32)).astype(acc.dtype)
        acopy(zz).start()
    def load(zz):
        v=have_c(zz,x,y)
        bcopy(zz,0).wait_recv(); acopy(zz).wait_recv()
        return v+bbuf[zz].astype(f32)+abuf[zz].astype(f32)
    def store(v,first):
        out_ref[...]=v if first else out_ref[...]+v
    zreduce(z,x,y,c,load,zup,zdn,stage,zsend,zrecv,store)
    for zz in range(4):
        for (xx,yy) in sides: ccopy(zz,xx,yy,1-c).wait_send()
        bcopy(zz,1).wait_send(); bcopy(zz,0).wait_send(); acopy(zz).wait_send()

def rs32(part,cid=1):
    n,w=part.shape; rows=n//32
    S=pltpu.SemaphoreType.DMA
    def V(k): return pltpu.VMEM((k,rows,w),part.dtype)
    return pl.pallas_call(rs32_kernel,out_shape=jax.ShapeDtypeStruct((rows,w),jnp.float32),
        in_specs=[pl.BlockSpec(memory_space=pl.ANY)],out_specs=pl.BlockSpec(memory_space=pltpu.VMEM),
        scratch_shapes=[V(16),V(16),V(8),V(4),V(4),V(4),V(4),S((16,)),S((16,)),S((16,)),S((8,)),S((8,)),S((4,)),S((4,)),S((4,)),S((2,4))],
        compiler_params=pltpu.CompilerParams(collective_id=cid,has_side_effects=True,vmem_limit_bytes=48*2**20))(part)

def barrier_plane():
    z,x,y,c=coords()
    b=pltpu.get_barrier_semaphore()
    def sig(d): pl.semaphore_signal(b,inc=1,device_id=d,device_id_type=MESH)
    sig(dev(z,1-x,y,c))
    @pl.when(z<3)
    def _(): sig(dev(z+1,x,y,c))
    @pl.when(z>0)
    def _(): sig(dev(z-1,x,y,c))
    pl.semaphore_wait(b,3-(3-z)//3-z//3)

def barrier_tp():
    z,x,y,c=coords()
    b=pltpu.get_barrier_semaphore()
    for d in (dev(z,x,1-y,c),dev(z,x,y,1-c)):
        pl.semaphore_signal(b,inc=1,device_id=d,device_id_type=MESH)
    pl.semaphore_wait(b,2)

def agctx_kernel(x_ref,out_ref,lsem,send,recv):
    rows=x_ref.shape[0]
    z,x,y,c=coords()
    barrier_plane()
    def at(p): return out_ref.at[pl.ds(pl.multiple_of(p*rows,rows),rows)]
    def cp(p,d,k,own=False):
        return pltpu.make_async_remote_copy(src_ref=x_ref if own else at(p),dst_ref=at(p),send_sem=send.at[k,p],recv_sem=recv.at[p],device_id=d,device_id_type=MESH)
    up,down,X=dev(z+1,x,y,c),dev(z-1,x,y,c),dev(z,1-x,y,c)
    me=z*2+x
    loc=pltpu.make_async_copy(x_ref,at(me),lsem); loc.start()
    @pl.when(z<3)
    def _(): cp(me,up,0,True).start()
    @pl.when(z>0)
    def _(): cp(me,down,1,True).start()
    cp(me,X,2,True).start()
    for d in (1,2,3):
        @pl.when(z-d>=0)
        def _():
            p=(z-d)*2+x; cp(p,X,2).wait_recv()
            @pl.when(z<3)
            def _(): cp(p,up,0).start()
            cp(p,X,2).start()
        @pl.when(z+d<=3)
        def _():
            p=(z+d)*2+x; cp(p,X,2).wait_recv()
            @pl.when(z>0)
            def _(): cp(p,down,1).start()
            cp(p,X,2).start()
    loc.wait()
    for zz in range(4):
        cp(zz*2+1-x,X,2).wait_recv()
        p=zz*2+x
        @pl.when((z<3)&(zz<=z))
        def _(): cp(p,up,0).wait_send()
        @pl.when((z>0)&(zz>=z))
        def _(): cp(p,down,1).wait_send()
        cp(p,X,2).wait_send()

def agctx(piece,cid=2):
    rows,w=piece.shape
    S=pltpu.SemaphoreType.DMA
    return pl.pallas_call(agctx_kernel,out_shape=jax.ShapeDtypeStruct((rows*8,w),piece.dtype),
        in_specs=[pl.BlockSpec(memory_space=pl.ANY)],out_specs=pl.BlockSpec(memory_space=pl.ANY),
        scratch_shapes=[S,S((3,8)),S((8,))],
        compiler_params=pltpu.CompilerParams(collective_id=cid,has_side_effects=True))(piece)

def rsctx_kernel(in_ref,out_ref,xbuf,zup,zdn,stage,xsend,xrecv,zsend,zrecv):
    rows=out_ref.shape[0]
    z,x,y,c=coords()
    barrier_plane()
    f32=jnp.float32
    X=dev(z,1-x,y,c)
    def at(p): return in_ref.at[pl.ds(pl.multiple_of(p*rows,rows),rows)]
    def xcopy(zz):
        return pltpu.make_async_remote_copy(src_ref=at(zz*2+1-x),dst_ref=xbuf.at[zz],send_sem=xsend.at[zz],recv_sem=xrecv.at[zz],device_id=X,device_id_type=MESH)
    for k in range(4): xcopy(zfar(z,k)).start()
    def load(zz):
        xcopy(zz).wait_recv()
        return at(zz*2+x)[...].astype(f32)+xbuf[zz].astype(f32)
    def store(v,first):
        out_ref[...]=v if first else out_ref[...]+v
    zreduce(z,x,y,c,load,zup,zdn,stage,zsend,zrecv,store)
    for zz in range(4): xcopy(zz).wait_send()

def rsctx(part,cid=3):
    n,w=part.shape; rows=n//8
    S=pltpu.SemaphoreType.DMA
    def V(k): return pltpu.VMEM((k,rows,w),part.dtype)
    return pl.pallas_call(rsctx_kernel,out_shape=jax.ShapeDtypeStruct((rows,w),jnp.float32),
        in_specs=[pl.BlockSpec(memory_space=pltpu.VMEM)],out_specs=pl.BlockSpec(memory_space=pltpu.VMEM),
        scratch_shapes=[V(4),V(4),V(4),V(4),S((4,)),S((4,)),S((4,)),S((2,4))],
        compiler_params=pltpu.CompilerParams(collective_id=cid,has_side_effects=True,vmem_limit_bytes=32*2**20))(part)

def rstp_kernel(in_ref,out_ref,cbuf,ybuf,stage,csend,crecv,ysend,yrecv):
    rows=out_ref.shape[0]
    z,x,y,c=coords()
    barrier_tp()
    f32=jnp.float32
    def at(yy,cc): return in_ref.at[pl.ds(pl.multiple_of((yy*2+cc)*rows,rows),rows)]
    def ccopy(yy):
        return pltpu.make_async_remote_copy(src_ref=at(yy,1-c),dst_ref=cbuf.at[yy],send_sem=csend.at[yy],recv_sem=crecv.at[yy],device_id=dev(z,x,y,1-c),device_id_type=MESH)
    ccopy(1-y).start(); ccopy(y).start()
    ccopy(1-y).wait_recv()
    stage[...]=(at(1-y,c)[...].astype(f32)+cbuf[1-y].astype(f32)).astype(stage.dtype)
    yc=pltpu.make_async_remote_copy(src_ref=stage,dst_ref=ybuf,send_sem=ysend,recv_sem=yrecv,device_id=dev(z,x,1-y,c),device_id_type=MESH)
    yc.start()
    ccopy(y).wait_recv()
    out_ref[...]=at(y,c)[...].astype(f32)+cbuf[y].astype(f32)
    yc.wait_recv()
    out_ref[...]+=ybuf[...].astype(f32)
    yc.wait_send(); ccopy(0).wait_send(); ccopy(1).wait_send()

def rstp(part,cid=4):
    n,w=part.shape; rows=n//4
    S=pltpu.SemaphoreType.DMA
    return pl.pallas_call(rstp_kernel,out_shape=jax.ShapeDtypeStruct((rows,w),jnp.float32),
        in_specs=[pl.BlockSpec(memory_space=pltpu.VMEM)],out_specs=pl.BlockSpec(memory_space=pltpu.VMEM),
        scratch_shapes=[pltpu.VMEM((2,rows,w),part.dtype),pltpu.VMEM((rows,w),part.dtype),pltpu.VMEM((rows,w),part.dtype),S((2,)),S((2,)),S,S],
        compiler_params=pltpu.CompilerParams(collective_id=cid,has_side_effects=True,vmem_limit_bytes=32*2**20))(part)

def agtp_kernel(x_ref,out_ref,lsem,send,recv):
    rows=x_ref.shape[0]
    z,x,y,c=coords()
    barrier_tp()
    def at(yy,cc): return out_ref.at[pl.ds(pl.multiple_of((yy*2+cc)*rows,rows),rows)]
    def cp(src,yy,cc,d,k):
        return pltpu.make_async_remote_copy(src_ref=src,dst_ref=at(yy,cc),send_sem=send.at[k],recv_sem=recv.at[yy*2+cc],device_id=d,device_id_type=MESH)
    Y,C=dev(z,x,1-y,c),dev(z,x,y,1-c)
    loc=pltpu.make_async_copy(x_ref,at(y,c),lsem); loc.start()
    cp(x_ref,y,c,Y,0).start(); cp(x_ref,y,c,C,1).start()
    cp(x_ref,1-y,c,Y,0).wait_recv()
    cp(at(1-y,c),1-y,c,C,2).start()
    cp(x_ref,y,1-c,C,1).wait_recv(); cp(x_ref,1-y,1-c,C,2).wait_recv()
    loc.wait()
    cp(x_ref,y,c,Y,0).wait_send(); cp(x_ref,y,c,C,1).wait_send(); cp(at(1-y,c),1-y,c,C,2).wait_send()

def agtp(piece,cid=5):
    rows,w=piece.shape
    S=pltpu.SemaphoreType.DMA
    return pl.pallas_call(agtp_kernel,out_shape=jax.ShapeDtypeStruct((rows*4,w),piece.dtype),
        in_specs=[pl.BlockSpec(memory_space=pl.ANY)],out_specs=pl.BlockSpec(memory_space=pl.ANY),
        scratch_shapes=[S,S((3,)),S((4,))],
        compiler_params=pltpu.CompilerParams(collective_id=cid,has_side_effects=True))(piece)


EPSILON = 1e-06
ROPE_BASE = 1000000.0
MASKED_SCORE = -1000000000.0
BF = jnp.bfloat16
F32 = jnp.float32


def dotf(a, b, dims):
    return lax.dot_general(a, b, (dims, ((), ())), preferred_element_type=F32)


class Links:
    def __init__(self, own):
        self.own = own

    def ag_all(self, piece, cid):
        if self.own:
            return ag32(piece, cid)
        return lax.all_gather(piece, ("ctx", "tp"), axis=0, tiled=True)

    def rs_all(self, part, cid):
        if self.own:
            return rs32(part, cid)
        return lax.psum_scatter(part, ("ctx", "tp"), scatter_dimension=0, tiled=True).astype(F32)

    def ag_ctx(self, piece, cid):
        if self.own:
            return agctx(piece, cid)
        return lax.all_gather(piece, "ctx", axis=0, tiled=True)

    def rs_ctx(self, part, cid):
        if self.own:
            return rsctx(part, cid)
        return lax.psum_scatter(part, "ctx", scatter_dimension=0, tiled=True).astype(F32)

    def rs_tp(self, part, cid):
        if self.own:
            return rstp(part, cid)
        return lax.psum_scatter(part, "tp", scatter_dimension=0, tiled=True).astype(F32)

    def ag_tp(self, piece, cid):
        if self.own:
            return agtp(piece, cid)
        return lax.all_gather(piece, "tp", axis=0, tiled=True)


def rms_norm(values, gain_vec):
    factor = lax.rsqrt(jnp.mean(values * values, axis=-1, keepdims=True) + EPSILON)
    return values * factor * gain_vec


def rotate(values, rotary_angles):
    half_size = values.shape[-1] // 2
    first_half = values[..., :half_size]
    second_half = values[..., half_size:]
    cosine = jnp.cos(rotary_angles)
    sine_part = jnp.sin(rotary_angles)
    return jnp.concatenate(
        [
            first_half * cosine - second_half * sine_part,
            second_half * cosine + first_half * sine_part,
        ],
        axis=-1,
    )


def angles_of(token_positions, head_width):
    freq_steps = jnp.arange(head_width // 2).astype(F32) * (2.0 / head_width)
    frequency = jnp.exp(-math.log(ROPE_BASE) * freq_steps)
    return token_positions.astype(F32)[..., None] * frequency


def positions_of(block_order, dev_count, block_len):
    first_block = jnp.transpose(block_order)
    block_pair = jnp.stack([first_block, 2 * dev_count - 1 - first_block], axis=-1)
    spread = block_pair[..., None] * block_len + jnp.arange(block_len, dtype=jnp.int32)
    return spread.reshape(dev_count, block_order.shape[0], 2 * block_len)


def head_route_path(raw_heads, gain_vec, rotary_angles, head_count):
    shaped = raw_heads.reshape(raw_heads.shape[0], head_count, -1)
    return rotate(rms_norm(shaped, gain_vec), rotary_angles[:, None, :])


def attend_forward(seq_item):
    query_matrix, every_key_row, every_value_row, query_pos, key_pos = seq_item
    score_scale = 1.0 / math.sqrt(query_matrix.shape[-1])
    unscaled_scores = jnp.einsum(
        "upnj,apj->upna", query_matrix, every_key_row, preferred_element_type=F32
    )
    allowed = query_pos[:, None, None, None] >= key_pos[None, None, None, :]
    scores = jnp.where(allowed, unscaled_scores * score_scale, MASKED_SCORE)
    row_top = jnp.max(scores, axis=-1, keepdims=True)
    exp_scores = jnp.exp(scores - row_top)
    totals = jnp.sum(exp_scores, axis=-1, keepdims=True)
    lower_attention_probs = (exp_scores / totals).astype(BF)
    attended_mix = jnp.einsum(
        "jzfq,qzx->jzfx", lower_attention_probs, every_value_row, preferred_element_type=F32
    )
    return (attended_mix, (row_top + jnp.log(totals))[..., 0])


def attend_backward(seq_item):
    (
        query_matrix,
        every_key_row,
        every_value_row,
        query_pos,
        key_pos,
        grad_attended_mix,
        log_total,
    ) = seq_item
    score_scale = 1.0 / math.sqrt(query_matrix.shape[-1])
    unscaled_scores = jnp.einsum(
        "upnj,apj->upna", query_matrix, every_key_row, preferred_element_type=F32
    )
    allowed = query_pos[:, None, None, None] >= key_pos[None, None, None, :]
    scores = jnp.where(allowed, unscaled_scores * score_scale, MASKED_SCORE)
    attention_probs = jnp.exp(scores - log_total[..., None])
    grad_probs = jnp.einsum(
        "upnj,apj->upna", grad_attended_mix, every_value_row, preferred_element_type=F32
    )
    row_inner = jnp.sum(attention_probs * grad_probs, axis=-1, keepdims=True)
    grad_score_dots = (attention_probs * (grad_probs - row_inner) * score_scale).astype(BF)
    grad_queries = jnp.einsum(
        "jzfq,qzx->jzfx", grad_score_dots, every_key_row, preferred_element_type=F32
    )
    grad_key_rows = jnp.einsum(
        "axfv,axfz->vxz", grad_score_dots, query_matrix, preferred_element_type=F32
    )
    grad_values = jnp.einsum(
        "axfv,axfz->vxz", attention_probs.astype(BF), grad_attended_mix, preferred_element_type=F32
    )
    return (grad_queries, grad_key_rows, grad_values)


def gates_of(logits, routes):
    experts = logits.shape[1]
    named = jnp.any(routes[:, :, None] == jnp.arange(experts, dtype=jnp.int32), axis=1)
    masked = jnp.where(named, logits, -jnp.inf)
    top = jnp.max(masked, axis=1, keepdims=True)
    weights = jnp.where(named, jnp.exp(masked - top), 0.0)
    return weights / jnp.sum(weights, axis=1, keepdims=True)


def shards(
    tokens_in,
    block_order,
    routes,
    norm1_gain,
    w_query,
    key_weight,
    value_weight,
    query_gain,
    key_gain,
    w_out,
    norm2_gain,
    w_router,
    w_gate,
    w_up,
    w_down,
    cotangent,
):
    tok_count, model_width = tokens_in.shape
    head_size = query_gain.shape[0]
    local_heads = w_query.shape[1] // head_size
    local_kv = key_weight.shape[1] // head_size
    query_group_width = local_heads // local_kv
    seq_count = block_order.shape[0]
    devices, tp_size = lax.axis_size("ctx"), lax.axis_size("tp")
    links = Links(devices == 8 and tp_size == 4)
    me, tp_me = lax.axis_index("ctx"), lax.axis_index("tp")
    rows = tok_count // tp_size
    block_len = tok_count // (2 * seq_count)
    experts = w_router.shape[1]
    own_experts, _, units = w_gate.shape
    hid = own_experts * units
    all_tok = devices * tok_count

    def own_rows(v):
        return lax.dynamic_slice_in_dim(v, tp_me * rows, rows, axis=0)

    cot_own = own_rows(cotangent)
    cot_all = links.ag_all(cot_own, 0)
    routes_all = lax.all_gather(routes, "ctx", axis=0, tiled=True)

    token_positions = positions_of(block_order, devices, block_len)
    query_pos = lax.dynamic_index_in_dim(token_positions, me, 0, keepdims=False)
    key_pos = jnp.transpose(token_positions, (1, 0, 2)).reshape(seq_count, devices * 2 * block_len)
    rotary_angles = angles_of(query_pos.reshape(-1), head_size)
    inputs = tokens_in.astype(F32)
    first_in = rms_norm(inputs, norm1_gain).astype(BF)
    query_raw = jnp.dot(first_in, w_query, preferred_element_type=F32)
    unrotated_key = jnp.dot(first_in, key_weight, preferred_element_type=F32)
    value_rows = jnp.dot(first_in, value_weight, preferred_element_type=F32).astype(BF)

    def rope_heads(raw_query, raw_key, gain_query, key_norm_gain):
        return (
            head_route_path(raw_query, gain_query, rotary_angles, local_heads),
            head_route_path(raw_key, key_norm_gain, rotary_angles, local_kv),
        )

    (query_rot, key_rot), rope_back = jax.vjp(
        rope_heads, query_raw, unrotated_key, query_gain, key_gain
    )
    query_rows = query_rot.astype(BF).reshape(
        seq_count, 2 * block_len, local_kv, query_group_width, head_size
    )
    kv_width = local_kv * head_size
    kv_own = jnp.concatenate([key_rot.astype(BF).reshape(tok_count, kv_width), value_rows], axis=1)
    kv_all = links.ag_ctx(kv_own, 1)
    kv_seq = kv_all.reshape(devices, seq_count, 2 * block_len, 2, local_kv, head_size)
    kv_seq = kv_seq.transpose(3, 1, 0, 2, 4, 5).reshape(
        2, seq_count, devices * 2 * block_len, local_kv, head_size
    )
    key_full, value_full = kv_seq[0], kv_seq[1]
    attended_mix, log_total = lax.map(
        attend_forward, (query_rows, key_full, value_full, query_pos, key_pos)
    )
    attended = attended_mix.reshape(tok_count, local_heads * head_size).astype(BF)
    attn_part = jnp.dot(attended, w_out, preferred_element_type=F32).astype(BF)
    residual = own_rows(inputs) + links.rs_tp(attn_part, 2)
    second_normed, second_back = jax.vjp(rms_norm, residual, norm2_gain)
    second_in = second_normed.astype(BF)
    second_all = links.ag_all(second_in, 3)

    gates_all = gates_of(jnp.dot(second_all, w_router, preferred_element_type=F32), routes_all)
    gates_mine = lax.dynamic_slice_in_dim(gates_all, me * own_experts, own_experts, axis=1)
    gates_own = lax.dynamic_slice_in_dim(
        gates_all, (me * tp_size + tp_me) * rows, rows, axis=0
    )
    spread = jnp.repeat(gates_mine, units, axis=1)
    gate_mat = w_gate.transpose(1, 0, 2).reshape(model_width, hid)
    up_mat = w_up.transpose(1, 0, 2).reshape(model_width, hid)
    down_mat = w_down.reshape(hid, model_width)
    def expert_block(block):
        rows_in, cots, weights, own = block
        gate_pre = jnp.dot(rows_in, gate_mat, preferred_element_type=F32)
        up_pre = jnp.dot(rows_in, up_mat, preferred_element_type=F32)
        sig = 1.0 / (1.0 + jnp.exp(-gate_pre))
        silu = gate_pre * sig
        hidden = silu * up_pre
        hidden_low = (hidden * weights).astype(BF)
        out_part = jnp.dot(hidden_low, down_mat, preferred_element_type=F32).astype(BF)
        back = dotf(cots, down_mat, ((1,), (1,)))
        gate_grad = jnp.sum((hidden * back).reshape(-1, own_experts, units), axis=2)
        grad_hidden = back * weights
        gate_low = (grad_hidden * up_pre * sig * (1.0 + gate_pre * (1.0 - sig))).astype(BF)
        up_low = (grad_hidden * silu).astype(BF)
        entry = dotf(gate_low, gate_mat, ((1,), (1,))) + dotf(up_low, up_mat, ((1,), (1,)))
        gate_wide = lax.dynamic_update_slice(
            jnp.zeros((rows_in.shape[0], extra), F32), gate_grad, (0, me * own_experts)
        )
        entry = jnp.concatenate([entry.astype(BF), gate_wide.astype(BF)], axis=1)
        sums = (
            dotf(rows_in, gate_low, ((0,), (0,))),
            dotf(rows_in, up_low, ((0,), (0,))),
            dotf(hidden_low, cots, ((0,), (0,))),
        )
        return out_part, entry, sums

    extra = -(-experts // 128) * 128
    steps = max(1, all_tok // 2048)
    if steps == 1:
        out_part, entry, sums = expert_block((second_all, cot_all, spread, gates_mine))
    else:

        def step(total, block):
            out_part, entry, sums = expert_block(block)
            return tuple(a + b for a, b in zip(total, sums)), (out_part, entry)

        def cut(v):
            return v.reshape(steps, -1, v.shape[1])

        zero = jnp.zeros((model_width, hid), F32)
        sums, (out_part, entry) = lax.scan(
            step, (zero, zero, zero.T), (cut(second_all), cut(cot_all), cut(spread), cut(gates_mine))
        )
        out_part = out_part.reshape(all_tok, model_width)
        entry = entry.reshape(all_tok, model_width + extra)
    out_own = links.rs_all(out_part, 4)
    layer_out = links.ag_tp((residual + out_own).astype(BF), 5)
    grad_gate = sums[0].reshape(model_width, own_experts, units).transpose(1, 0, 2)
    grad_up = sums[1].reshape(model_width, own_experts, units).transpose(1, 0, 2)
    grad_down = sums[2].reshape(own_experts, units, model_width)
    entry_own = links.rs_all(entry, 6)
    gate_total = entry_own[:, model_width : model_width + experts]
    grad_logits = (
        gates_own * (gate_total - jnp.sum(gates_own * gate_total, axis=1, keepdims=True))
    ).astype(BF)
    logits_all = lax.all_gather(grad_logits, ("ctx", "tp"), axis=0, tiled=True)
    width_part = model_width // devices
    second_cols = lax.dynamic_slice_in_dim(second_all, me * width_part, width_part, axis=1)
    grad_router = dotf(second_cols, logits_all, ((0,), (0,)))
    grad_second = entry_own[:, :model_width] + dotf(grad_logits, w_router, ((1,), (1,)))
    grad_resid_norm, grad_norm2 = second_back(grad_second)
    grad_residual = cot_own.astype(F32) + grad_resid_norm
    grad_attn_low = links.ag_tp(grad_residual.astype(BF), 7)
    grad_out = dotf(attended, grad_attn_low, ((0,), (0,)))
    grad_mixed = dotf(grad_attn_low, w_out, ((1,), (1,))).astype(BF)
    grad_mixed = grad_mixed.reshape(
        seq_count, 2 * block_len, local_kv, query_group_width, head_size
    )
    grad_query_seq, grad_key_seq, grad_value_seq = lax.map(
        attend_backward,
        (query_rows, key_full, value_full, query_pos, key_pos, grad_mixed, log_total),
    )
    grad_kv = jnp.stack([grad_key_seq, grad_value_seq]).astype(BF)
    grad_kv = grad_kv.reshape(2, seq_count, devices, 2 * block_len, kv_width)
    grad_kv = grad_kv.transpose(2, 1, 3, 0, 4).reshape(all_tok, 2 * kv_width)
    grad_kv_own = links.rs_ctx(grad_kv, 8)
    grad_query_rot = grad_query_seq.reshape(tok_count, local_heads, head_size)
    grad_key_rot = grad_kv_own[:, :kv_width].reshape(tok_count, local_kv, head_size)
    grad_query_raw, grad_key_raw, grad_qgain, grad_kgain = rope_back(
        (grad_query_rot, grad_key_rot)
    )
    query_low = grad_query_raw.astype(BF)
    key_low = grad_key_raw.astype(BF)
    value_low = grad_kv_own[:, kv_width:].astype(BF)
    first_part = dotf(query_low, w_query, ((1,), (1,)))
    first_part = first_part + dotf(key_low, key_weight, ((1,), (1,)))
    first_part = first_part + dotf(value_low, value_weight, ((1,), (1,)))
    grad_first = links.rs_tp(first_part.astype(BF), 9)
    _, first_back = jax.vjp(rms_norm, own_rows(inputs), norm1_gain)
    grad_input_norm, grad_norm1 = first_back(grad_first)
    grad_input = links.ag_tp((grad_residual + grad_input_norm).astype(BF), 10)

    def over_ctx(v, dim):
        return lax.psum_scatter(v.astype(BF), "ctx", scatter_dimension=dim, tiled=True).astype(F32)

    low_all = jnp.concatenate([query_low, key_low, value_low], axis=1)
    weight_grads = over_ctx(dotf(first_in, low_all, ((0,), (0,))), 0)
    wide = query_low.shape[1]
    grad_query = weight_grads[:, :wide]
    grad_key = weight_grads[:, wide : wide + kv_width]
    grad_value = weight_grads[:, wide + kv_width :]
    grad_out = over_ctx(grad_out, 1)
    vectors = lax.psum(
        jnp.concatenate([grad_norm1, grad_norm2, grad_qgain, grad_kgain]), ("ctx", "tp")
    )

    def piece_of(start, size):
        part = size // devices
        return lax.dynamic_slice_in_dim(vectors, start + me * part, part, axis=0)

    return (
        layer_out,
        grad_input,
        piece_of(0, model_width),
        grad_query,
        grad_key,
        grad_value,
        piece_of(2 * model_width, head_size),
        piece_of(2 * model_width + head_size, head_size),
        grad_out,
        piece_of(model_width, model_width),
        grad_router,
        grad_gate,
        grad_up,
        grad_down,
    )


def solution(mesh):
    in_specs = (
        P("ctx", None),
        P(),
        P("ctx", None),
        P(),
        P(None, "tp"),
        P(None, "tp"),
        P(None, "tp"),
        P(),
        P(),
        P("tp", None),
        P(),
        P(),
        P("ctx", None, "tp"),
        P("ctx", None, "tp"),
        P("ctx", "tp", None),
        P("ctx", None),
    )
    out_specs = (
        P("ctx", None),
        P("ctx", None),
        P("ctx"),
        P("ctx", "tp"),
        P("ctx", "tp"),
        P("ctx", "tp"),
        P("ctx"),
        P("ctx"),
        P("tp", "ctx"),
        P("ctx"),
        P("ctx", None),
        P("ctx", None, "tp"),
        P("ctx", None, "tp"),
        P("ctx", "tp", None),
    )
    return jax.shard_map(shards, mesh=mesh, in_specs=in_specs, out_specs=out_specs, check_vma=False)
```

time: 3500 us -> 707 us (0.20)
  waiting for transfers between devices: 2680 us -> 0.04 us
  local copies, waits for them, and re-layouts: 405 us -> 51.7 us
  Pallas kernels: 0 us -> 300 us
    all_to_all x4 -> x0, waiting for transfers between devices: 1290 us -> none  [the longest x2 676 us: dispatch(): lax.all_to_all(buffer, 'ctx', split_axis=0, concat_axis=1, tiled=True)]
    unnamed x12 -> x2, waiting for transfers between devices: 1010 us -> 0.03 us
    reduce_scatter x5 -> x2, waiting for transfers between devices: 334 us -> 0.01 us  [over_ctx(): lax.psum_scatter(v.astype(BF), 'ctx', scatter_dimension=dim, tiled=True)]
    pallas_call x0 -> x11, Pallas kernels: none -> 300 us  [the longest x2 109 us: rs32(): pl.pallas_call(rs32_kernel, out_shape=jax.ShapeDtypeStruct((rows, w), jnp...]
    gather x4 -> x0, local copies, waits for them, and re-layouts: 118 us -> none  [the longest x1 35.8 us: shards(): padded_grad[slot_table].reshape(experts, capacity, model_width)]
    unnamed x177 -> x143, local copies, waits for them, and re-layouts: 127 us -> 10.3 us
    all_to_all x4 -> x0, local copies, waits for them, and re-layouts: 65.8 us -> none  [the longest x2 37.2 us: send_back(): lax.all_to_all(buffer, 'ctx', split_axis=1, concat_axis=0, tiled=True)]
    psum x3 -> x0, waiting for transfers between devices: 46.8 us -> none  [the longest x1 35.6 us: shards(): lax.psum(second_part.astype(jnp.bfloat16), 'tp').astype(jnp.float32)]
  transfers between devices with their start and end apart: 14 -> 2, of which waited for: 14 -> 0; matrix products, arithmetic and copies ran while one was open for 9% -> 15% of each run, Pallas kernels for 0% -> 17%
where the time goes in v1:
time: 707 us; the launch traced here: 700 us
  Pallas kernels  300 us (42%)
  matrix products  168 us (24%)
  blocking collectives  107 us (15%)
  other arithmetic  57.1 us (8%)
  local copies, waits for them, and re-layouts  51.7 us (7%)
  between operations  15.6 us (2%)
    pallas_call x2, Pallas kernels, rs32(): pl.pallas_call(rs32_kernel, out_shape=jax.ShapeDtypeStruct((rows, w), jnp...  109 us
    dot_general x14, matrix products, dotf(): return lax.dot_general(a, b, (dims, ((), ())), preferred_element_type=F32)  87.3 us
    pallas_call x2, Pallas kernels, ag32(): pl.pallas_call(ag32_kernel, out_shape=jax.ShapeDtypeStruct((rows * 32, w)...  83.6 us
    pallas_call x3, Pallas kernels, agtp(): pl.pallas_call(agtp_kernel, out_shape=jax.ShapeDtypeStruct((rows * 4, w),...  45.4 us
    all_gather x1, blocking collectives, shards(): logits_all = lax.all_gather(grad_logits, ('ctx', 'tp'), axis=0, tiled=True)  38.9 us
    psum x1, blocking collectives, shards(): lax.psum(jnp.concatenate([grad_norm1, grad_norm2, grad_qgain, grad_kgain]...  37.1 us
    all_gather x1, blocking collectives, shards(): routes_all = lax.all_gather(routes, 'ctx', axis=0, tiled=True)  30.7 us
    pallas_call x1, Pallas kernels, agctx(): pl.pallas_call(agctx_kernel, out_shape=jax.ShapeDtypeStruct((rows * 8, w)...  22 us
  transfers between devices with their start and end apart: 2, of which 0 were waited for; matrix products, arithmetic and copies ran while one was open for 15% of the time, Pallas kernels for 17%

profile of v1, /device:TPU:0, one launch (start us, length us, event | category | flops | bytes accessed | tf_op | source)
XLA Modules:
  0.0 700.3 jit_solution(8816491679842888950)
XLA Ops:
  30.1 22.0 %shard_map.263 = bf16[2048,256]{1,0:T(8,128)(2,1)} custom-call(bf16[256,256]{1,0:T(8,128)(2,1)} %pad_maximum_fusion.3.x_ref), custom_call_target="tpu_custom_call" | custom-call | tf_op jit(solution)/shard_map/pallas_call | solution.py:265
  71.5 11.5 %while.26 = (s32[]{:T(128)}, bf16[2,128,1,8,128]{1,4,3,2,0:T(8,128)(2,1)}, f32[2,128,1,8]{1,3,2,0:T(8,128)}, bf16[2,1024,1,128]{3,1,2,0:T(8,128)(2,1)}, s32[2,12...) while((s32[]{:T(128)}, ...), condition=%wide.region_6.7_spmd, body=%wide.region_3.6_spmd.sunk | while | flops 549583872 | bytes 20758212 | solution.py:565
  88.8 10.2 %shard_map.264 = f32[64,2048]{1,0:T(8,128)S(1)} custom-call(bf16[256,2048]{1,0:T(8,128)(2,1)S(1)} %convolution_convert_fusion.3.in_ref), custom_call_target="tpu_custom_call" | custom-call | tf_op jit(solution)/shard_map/pallas_call | solution.py:319
  102.9 41.4 %shard_map.265 = bf16[2048,2048]{1,0:T(8,128)(2,1)} custom-call(bf16[64,2048]{1,0:T(8,128)(2,1)} %multiply_convert_fusion.3.x_ref), custom_call_target="tpu_custom_call" | custom-call | tf_op jit(solution)/shard_map/pallas_call | solution.py:95
  146.0 42.2 %shard_map.268 = bf16[2048,2048]{1,0:T(8,128)(2,1)} custom-call(bf16[64,2048]{1,0:T(8,128)(2,1)} %constant_dynamic-slice_fusion.5.x_ref), custom_call_target="tpu_custom_call" | custom-call | tf_op jit(solution)/shard_map/pallas_call | solution.py:95
  188.2 30.7 %all_gather.6 = s32[2048,8]{0,1:T(8,128)S(1)} all-gather(s32[256,8]{0,1:T(8,128)S(1)} %copy-done.55), channel_id=1, replica_groups=mesh['ctx'=8,'tp'=4] {'ctx'}, dimensions={0}, use_global_device_ids=true | all-gather | bytes 73728 | tf_op jit(solution)/shard_map/all_gather | solution.py:533
  219.5 11.9 %fusion.119 = f32[2048,768]{0,1:T(8,128)} fusion(bf16[2048,2048]{1,0:T(8,128)(2,1)} %shard_map.265, bf16[2048,768]{0,1:T(8,128)(2,1)} %bitcast.409), kind=kOutput, calls=%fused_computation.210 | convolution fusion | flops 6442450944 | bytes 17825792 | tf_op jit(solution)/shard_map/dot_general | solution.py:587
  240.2 10.1 %fusion.120 = f32[2048,768]{0,1:T(8,128)S(1)} fusion(bf16[2048,2048]{1,0:T(8,128)(2,1)} %shard_map.268, bf16[768,2048]{1,0:T(8,128)(2,1)} %bitcast.411), kind=kOutput, calls=%fused_computation.211 | convolution fusion | flops 6442450944 | bytes 17825792 | tf_op jit(solution)/shard_map/dot_general | solution.py:357
  250.3 16.5 %multiply_convert_fusion.1 = (bf16[2048,768]{0,1:T(8,128)(2,1)}, f32[2048,768]{0,1:T(8,128)}, bf16[2048,768]{0,1:T(8,128)(2,1)}, bf16[2048,768]{0,1:T(8,128)(2,1)}) fusion(f32[2048,768]{0,1:T(8,128)} %fusion.119, f32[2048,768]{0,1:T(8,128)S(1)} %fusion.120, f32[2048,4]{0,1:T(4,128)S(1)} %copy.235, bf16[2048,2048]{1,0:T(8,128)(2,1)} %shard_map.265, ...), kind=kOutput, calls=%fused_computation.78 | convolution fusion | flops 6470762496 | bytes 39878656 | tf_op jit(solution)/shard_map/dot_general | solution.py:586
  271.1 12.2 %fusion.121 = f32[2048,2048]{1,0:T(8,128)} fusion(bf16[2048,768]{0,1:T(8,128)(2,1)} %get-tuple-element.308, bf16[2048,768]{0,1:T(8,128)(2,1)S(1)} %bitcast.377), kind=kOutput, calls=%fused_computation.212 | convolution fusion | flops 6442450944 | bytes 23068672 | tf_op jit(solution)/shard_map/dot_general | solution.py:357
  283.3 12.7 %add_convert_fusion = bf16[2048,2048]{1,0:T(8,128)(2,1)} fusion(f32[2048,2048]{1,0:T(8,128)} %fusion.121, bf16[2048,768]{0,1:T(8,128)(2,1)S(1)} %copy-done.28, bf16[2048,768]{0,1:T(8,128)(2,1)S(1)} %bitcast.410), kind=kOutput, calls=%fused_computation.70 | convolution fusion | flops 6450839552 | bytes 31457280 | tf_op jit(solution)/shard_map/dot_general | solution.py:357
  306.4 53.2 %shard_map.269 = f32[64,2176]{1,0:T(8,128)S(1)} custom-call(bf16[2048,2176]{1,0:T(8,128)(2,1)} %pad_maximum_fusion.in_ref), custom_call_target="tpu_custom_call" | custom-call | tf_op jit(solution)/shard_map/pallas_call | solution.py:201
  364.6 10.3 %shard_map.270 = bf16[256,2048]{1,0:T(8,128)(2,1)} custom-call(bf16[64,2048]{1,0:T(8,128)(2,1)} %fusion.110.x_ref), custom_call_target="tpu_custom_call" | custom-call | tf_op jit(solution)/shard_map/pallas_call | solution.py:343
  383.5 30.9 %while.27 = (s32[]{:T(128)}, f32[2,128,1,8,128]{4,3,1,0,2:T(8,128)}, bf16[2,1024,1,128]{1,3,2,0:T(8,128)(2,1)}, bf16[2,1024,1,128]{1,3,2,0:T(8,128)(2,1)}, bf16[...) while((s32[]{:T(128)}, ...), condition=%wide.region_16.17_spmd, body=%wide.region_14.16_spmd.sunk | while | flops 1359084544 | bytes 61124372 | solution.py:652
  426.8 21.1 %shard_map.271 = f32[256,256]{1,0:T(8,128)S(1)} custom-call(bf16[2048,256]{1,0:T(8,128)(2,1)S(1)} %bitcast.378), custom_call_target="tpu_custom_call" | custom-call | tf_op jit(solution)/shard_map/pallas_call | solution.py:292
  461.2 9.5 %shard_map.272 = f32[64,2048]{1,0:T(8,128)S(1)} custom-call(bf16[256,2048]{1,0:T(8,128)(2,1)S(1)} %fusion.62.in_ref), custom_call_target="tpu_custom_call" | custom-call | tf_op jit(solution)/shard_map/pallas_call | solution.py:319
  470.7 9.2 %convolution_convert_fusion.1.in_ref = bf16[2048,2048]{1,0:T(8,128)(2,1)} fusion(bf16[2048,768]{0,1:T(8,128)(2,1)S(1)} %copy-done.26, bf16[768,2048]{1,0:T(8,128)(2,1)S(1)} %bitcast.412), kind=kOutput, calls=%fused_computation.75 | convolution fusion | flops 6446645248 | bytes 14680064 | tf_op jit(solution)/shard_map/dot_general | solution.py:592
  479.9 55.4 %shard_map.266 = f32[64,2048]{1,0:T(8,128)S(1)} custom-call(bf16[2048,2048]{1,0:T(8,128)(2,1)} %convolution_convert_fusion.1.in_ref), custom_call_target="tpu_custom_call" | custom-call | tf_op jit(solution)/shard_map/pallas_call | solution.py:201
  537.7 24.6 %shard_map.267 = bf16[256,2048]{1,0:T(8,128)(2,1)} custom-call(bf16[64,2048]{1,0:T(8,128)(2,1)} %get-tuple-element.322.x_ref), custom_call_target="tpu_custom_call" | custom-call | tf_op jit(solution)/shard_map/pallas_call | solution.py:343
  562.2 10.5 %shard_map.273 = bf16[256,2048]{1,0:T(8,128)(2,1)} custom-call(bf16[64,2048]{1,0:T(8,128)(2,1)} %get-tuple-element.321.x_ref), custom_call_target="tpu_custom_call" | custom-call | tf_op jit(solution)/shard_map/pallas_call | solution.py:343
  572.9 38.9 %all-gather = bf16[32,64,32]{1,2,0:T(8,128)(2,1)S(1)} all-gather(bf16[1,64,32]{1,2,0:T(8,128)(2,1)S(1)} %copy.248), channel_id=1, replica_groups=mesh['ctx'=8,'tp'=4] {'ctx','tp'}, dimensions={0}, use_global_device_ids=true | all-gather | bytes 135168 | tf_op jit(solution)/shard_map/all_gather | solution.py:639
  612.1 37.1 %psum.7 = f32[4352]{0:T(1024)S(1)} all-reduce(f32[4352]{0:T(1024)S(1)} %pad_maximum_fusion.4), channel_id=1, replica_groups=mesh['ctx'=8,'tp'=4] {'ctx','tp'}, use_global_device_ids=true, to_apply=%region_25.26 | all-reduce | flops 4352 | bytes 34816 | tf_op jit(solution)/shard_map/psum | solution.py:686
  652.6 11.8 %fusion.123 = f32[2048,768]{0,1:T(8,128)} fusion(bf16[2048,768]{0,1:T(8,128)(2,1)} %get-tuple-element.308, bf16[2048,2048]{1,0:T(8,128)(2,1)} %shard_map.265), kind=kOutput, calls=%fused_computation.214 | convolution fusion | flops 6442450944 | bytes 17825792 | tf_op jit(solution)/shard_map/dot_general | solution.py:357
  664.4 10.8 %fusion.124 = f32[2048,768]{0,1:T(8,128)} fusion(bf16[2048,768]{0,1:T(8,128)(2,1)S(1)} %copy-done.29, bf16[2048,2048]{1,0:T(8,128)(2,1)} %shard_map.265), kind=kOutput, calls=%fused_computation.215 | convolution fusion | flops 6442450944 | bytes 17825792 | tf_op jit(solution)/shard_map/dot_general | solution.py:357
  (316 shorter events, 181.9 us)
Async XLA Ops:
  7.2 243.2 %copy-start = (bf16[4,2048,192]{1,2,0:T(8,128)(2,1)S(1)}, bf16[4,2048,192]{1,2,0:T(8,128)(2,1)}, u32[]{:S(2)}) copy-start(bf16[4,2048,192]{1,2,0:T(8,128)(2,1)} %param.32) | copy-start | bytes 9437188
  7.2 676.6 %reduce-scatter.5.cloned.1.call-start = ((), (), s32[]{:S(2)}) async-start(), calls=%async_computation.3 | async-start | bytes 4718592 | tf_op jit(solution)/shard_map/reduce_scatter | solution.py:677
  19.5 39.9 %copy-start.30 = (f32[256,8]{1,0:T(8,128)}, f32[256,8]{1,0:T(8,128)S(1)}, u32[]{:S(2)}) copy-start(f32[256,8]{1,0:T(8,128)S(1)} %copy.226) | copy-start | bytes 24580
  24.6 33.9 %copy-start.33 = (f32[256,128]{1,0:T(8,128)}, f32[256,128]{1,0:T(8,128)S(1)}, u32[]{:S(2)}) copy-start(f32[256,128]{1,0:T(8,128)S(1)} %copy.220) | copy-start | bytes 393220
  25.4 33.2 %copy-start.53 = (f32[256]{0:T(256)}, f32[256]{0:T(256)S(1)}, u32[]{:S(2)}) copy-start(f32[256]{0:T(256)S(1)} %fusion.105) | copy-start | bytes 3076
  27.1 32.7 %copy-start.35 = (f32[256,64]{1,0:T(8,128)}, f32[256,64]{1,0:T(8,128)S(1)}, u32[]{:S(2)}) copy-start(f32[256,64]{1,0:T(8,128)S(1)} %get-tuple-element.331) | copy-start | bytes 196612
  101.2 260.9 %copy-start.65 = (f32[64]{0:T(128)}, f32[64]{0:T(128)S(1)}, u32[]{:S(2)}) copy-start(f32[64]{0:T(128)S(1)} %get-tuple-element.312) | copy-start | bytes 772
  146.0 42.2 %copy-start.55 = (s32[256,8]{0,1:T(8,128)S(1)}, s32[256,8]{0,1:T(8,128)}, u32[]{:S(2)}) copy-start(s32[256,8]{0,1:T(8,128)} %param.22) | copy-start | bytes 24580
  306.4 54.9 %copy-start.11 = (f32[64,2048]{1,0:T(8,128)S(1)}, f32[64,2048]{1,0:T(8,128)}, u32[]{:S(2)}) copy-start(f32[64,2048]{1,0:T(8,128)} %copy-done.10) | copy-start | bytes 1572868
  379.7 306.2 %reduce-scatter.3.cloned.1.call-start = ((), (), s32[]{:S(2)}) async-start(), calls=%async_computation.2 | async-start | bytes 5898240 | tf_op jit(solution)/shard_map/reduce_scatter | solution.py:677
  423.0 24.9 %copy-start.14 = (f32[256,8,64]{2,1,0:T(8,128)S(1)}, f32[256,8,64]{2,1,0:T(8,128)}, u32[]{:S(2)}) copy-start(f32[256,8,64]{2,1,0:T(8,128)} %copy-done.13) | copy-start | bytes 1572868
  426.7 24.4 %copy-start.64 = (f32[256]{0:T(256)S(1)}, f32[256]{0:T(256)}, u32[]{:S(2)}) copy-start(f32[256]{0:T(256)} %get-tuple-element.333) | copy-start | bytes 3076
  426.7 24.6 %copy-start.23 = (bf16[256,2048]{1,0:T(8,128)(2,1)S(1)}, bf16[256,2048]{1,0:T(8,128)(2,1)}, u32[]{:S(2)}) copy-start(bf16[256,2048]{1,0:T(8,128)(2,1)} %param.20) | copy-start | bytes 3145732
  426.7 24.6 %copy-start.48 = (f32[2048]{0:T(1024)S(1)}, f32[2048]{0:T(1024)}, u32[]{:S(2)}) copy-start(f32[2048]{0:T(1024)} %param.23) | copy-start | bytes 24580
  426.8 24.6 %copy-start.68 = (f32[256]{0:T(256)S(1)}, f32[256]{0:T(256)}, u32[]{:S(2)}) copy-start(f32[256]{0:T(256)} %copy-done.67) | copy-start | bytes 3076
  479.9 55.5 %copy-start.16 = (f32[256,2048]{1,0:T(8,128)S(1)}, f32[256,2048]{1,0:T(8,128)}, u32[]{:S(2)}) copy-start(f32[256,2048]{1,0:T(8,128)} %convert_element_type.129) | copy-start | bytes 6291460
  479.9 55.5 %copy-start.62 = (f32[64]{0:T(128)S(1)}, f32[64]{0:T(128)}, u32[]{:S(2)}) copy-start(f32[64]{0:T(128)} %get-tuple-element.339) | copy-start | bytes 772
  479.9 55.7 %copy-start.66 = (f32[64]{0:T(128)S(1)}, f32[64]{0:T(128)}, u32[]{:S(2)}) copy-start(f32[64]{0:T(128)} %copy-done.65) | copy-start | bytes 772
  479.9 55.7 %copy-start.12 = (f32[64,2048]{1,0:T(8,128)S(1)}, f32[64,2048]{1,0:T(8,128)}, u32[]{:S(2)}) copy-start(f32[64,2048]{1,0:T(8,128)} %copy-done.10) | copy-start | bytes 1572868
  479.9 55.7 %copy-start.21 = (f32[64,2048]{1,0:T(8,128)S(1)}, f32[64,2048]{1,0:T(8,128)}, u32[]{:S(2)}) copy-start(f32[64,2048]{1,0:T(8,128)} %copy-done.20) | copy-start | bytes 1572868
  479.9 55.7 %copy-start.43 = (f32[2048]{0:T(1024)S(1)}, f32[2048]{0:T(1024)}, u32[]{:S(2)}) copy-start(f32[2048]{0:T(1024)} %param.30) | copy-start | bytes 24580
  479.9 55.7 %copy-start.57 = (f32[64]{0:T(128)S(1)}, f32[64]{0:T(128)}, u32[]{:S(2)}) copy-start(f32[64]{0:T(128)} %copy-done.56) | copy-start | bytes 772
  535.4 37.4 %copy-start.41 = (bf16[64,32]{1,0:T(8,128)(2,1)S(1)}, bf16[64,32]{1,0:T(8,128)(2,1)}, u32[]{:S(2)}) copy-start(bf16[64,32]{1,0:T(8,128)(2,1)} %copy-done.40) | copy-start | bytes 12292
  535.4 76.7 %copy-start.49 = (f32[2048]{0:T(1024)S(1)}, f32[2048]{0:T(1024)}, u32[]{:S(2)}) copy-start(f32[2048]{0:T(1024)} %get-tuple-element.258) | copy-start | bytes 24580
  (58 other events, 500.5 us)
Sparse Core Ops, SparseCore 0:
  379.9 92.8 reduce-scatter.4
  476.8 118.9 reduce-scatter.2

commit v2 on v1

--- a/solution.py
+++ b/solution.py
@@ -139,69 +139,200 @@
         zz=zfar(z,k)
         cp(zup,zz,up,0,0).wait_send()
 
-def rs32_kernel(in_ref,out_ref,acc,cbuf,bbuf,abuf,zup,zdn,stage,lsem,csend,crecv,bsend,brecv,asend,arecv,zsend,zrecv):
-    rows=out_ref.shape[0]
-    z,x,y,c,ax,ay,bx,by=neighbours()
-    dx,dy=1-x,1-y
+
+def far_z(z, k):
+    half = z // 2
+    near = z + half * (3 - 2 * z)
+    place = 3 - k + (k // 2) * (2 * (k % 2) - 1) * near
+    return place + half * (3 - 2 * place)
+
+
+def reduce_all_kernel(
+    part_ref,
+    out_ref,
+    acc, cbuf, bbuf, abuf, zbuf,
+    lsem, csend, crecv, bsend, brecv, asend, arecv, zsend, zrecv,
+):
+    f32 = jnp.float32
+    rows = out_ref.shape[0]
+    z, x, y, c, ax, ay, bx, by = neighbours()
+    dx, dy = 1 - x, 1 - y
+    A, B, C = dev(z, ax, ay, c), dev(z, bx, by, c), dev(z, x, y, 1 - c)
+    up, down = dev(z + 1, x, y, c), dev(z - 1, x, y, c)
+
+    def q(zz, xx, yy):
+        return zz * 4 + xx * 2 + yy
+
+    def at(p):
+        return part_ref.at[pl.ds(pl.multiple_of(p * rows, rows), rows)]
+
+    def ccopy(zz, xx, yy):
+        i = q(zz, xx, yy)
+        return pltpu.make_async_remote_copy(
+            src_ref=at(pid(zz, xx, yy, 1 - c)), dst_ref=cbuf.at[i], send_sem=csend.at[i],
+            recv_sem=crecv.at[i], device_id=C, device_id_type=MESH)
+
+    def lcopy(zz, xx, yy):
+        i = q(zz, xx, yy)
+        return pltpu.make_async_copy(at(pid(zz, xx, yy, c)), acc.at[i], lsem.at[i])
+
+    def bcopy(zz, far):
+        i = zz + 4 * far
+        place = q(zz, dx, dy) if far else q(zz, bx, by)
+        return pltpu.make_async_remote_copy(
+            src_ref=acc.at[place], dst_ref=bbuf.at[i], send_sem=bsend.at[i],
+            recv_sem=brecv.at[i], device_id=B, device_id_type=MESH)
+
+    def acopy(zz):
+        return pltpu.make_async_remote_copy(
+            src_ref=acc.at[q(zz, ax, ay)], dst_ref=abuf.at[zz], send_sem=asend.at[zz],
+            recv_sem=arecv.at[zz], device_id=A, device_id_type=MESH)
+
+    def zcopy(zz, to, slot):
+        return pltpu.make_async_remote_copy(
+            src_ref=acc.at[q(zz, x, y)], dst_ref=zbuf.at[slot], send_sem=zsend.at[zz],
+            recv_sem=zrecv.at[slot], device_id=to, device_id_type=MESH)
+
+    def stage_c(k):
+        zz = far_z(z, k)
+        for xx, yy in ((dx, dy), (bx, by), (ax, ay), (x, y)):
+            lcopy(zz, xx, yy).start()
+        for xx, yy in ((dx, dy), (ax, ay), (bx, by), (x, y)):
+            ccopy(zz, xx, yy).start()
+
+    def plus_c(zz, xx, yy):
+        lcopy(zz, xx, yy).wait()
+        ccopy(zz, xx, yy).wait_recv()
+        i = q(zz, xx, yy)
+        return acc[i].astype(f32) + cbuf[i].astype(f32)
+
+    def stage_b(k):
+        zz = far_z(z, k)
+        acc[q(zz, dx, dy)] = plus_c(zz, dx, dy).astype(acc.dtype)
+        bcopy(zz, 1).start()
+        acc[q(zz, bx, by)] = plus_c(zz, bx, by).astype(acc.dtype)
+        bcopy(zz, 0).start()
+
+    def stage_a(k):
+        zz = far_z(z, k)
+        value = plus_c(zz, ax, ay)
+        bcopy(zz, 1).wait_recv()
+        acc[q(zz, ax, ay)] = (value + bbuf[zz + 4].astype(f32)).astype(acc.dtype)
+        acopy(zz).start()
+
+    def stage_z(k):
+        zz = far_z(z, k)
+        place = q(zz, x, y)
+        value = plus_c(zz, x, y)
+        bcopy(zz, 0).wait_recv()
+        acopy(zz).wait_recv()
+        value = value + bbuf[zz].astype(f32) + abuf[zz].astype(f32)
+
+        @pl.when(zz != z)
+        def _():
+            acc[place] = value.astype(acc.dtype)
+
+            @pl.when((zz > z) & (z > 0))
+            def _():
+                zcopy(zz, up, zz).wait_recv()
+                acc[place] = (acc[place].astype(f32) + zbuf[zz].astype(f32)).astype(acc.dtype)
+
+            @pl.when((zz < z) & (z < 3))
+            def _():
+                zcopy(zz, down, zz).wait_recv()
+                acc[place] = (acc[place].astype(f32) + zbuf[zz].astype(f32)).astype(acc.dtype)
+
+            @pl.when(zz > z)
+            def _():
+                zcopy(zz, up, zz).start()
+
+            @pl.when((zz < z) & (zz != z - 1))
+            def _():
+                zcopy(zz, down, zz).start()
+
+            @pl.when(zz == z - 1)
+            def _():
+                zcopy(zz, down, 4).start()
+
+        @pl.when(zz == z)
+        def _():
+            out_ref[...] = value
+
+            @pl.when(z > 0)
+            def _():
+                zcopy(z, up, z).wait_recv()
+                out_ref[...] += zbuf[z].astype(f32)
+
+            @pl.when(z < 3)
+            def _():
+                zcopy(z, down, 4).wait_recv()
+                out_ref[...] += zbuf[4].astype(f32)
+
     barrier_all()
-    f32=jnp.float32
-    A,B,C=dev(z,ax,ay,c),dev(z,bx,by,c),dev(z,x,y,1-c)
-    def q(zz,xx,yy): return zz*4+xx*2+yy
-    def at(p): return in_ref.at[pl.ds(pl.multiple_of(p*rows,rows),rows)]
-    def ccopy(zz,xx,yy,cc):
-        return pltpu.make_async_remote_copy(src_ref=at(pid(zz,xx,yy,cc)),dst_ref=cbuf.at[q(zz,xx,yy)],send_sem=csend.at[q(zz,xx,yy)],recv_sem=crecv.at[q(zz,xx,yy)],device_id=C,device_id_type=MESH)
-    def lcopy(zz,xx,yy):
-        return pltpu.make_async_copy(at(pid(zz,xx,yy,c)),acc.at[q(zz,xx,yy)],lsem.at[q(zz,xx,yy)])
-    sides=[(dx,dy),(bx,by),(ax,ay),(x,y)]
-    for (xx,yy) in sides:
-        for k in range(4):
-            zz=zfar(z,k)
-            lcopy(zz,xx,yy).start()
-    for (xx,yy) in [(dx,dy),(ax,ay),(bx,by),(x,y)]:
-        for k in range(4):
-            zz=zfar(z,k)
-            ccopy(zz,xx,yy,1-c).start()
-    def have_c(zz,xx,yy):
-        lcopy(zz,xx,yy).wait(); ccopy(zz,xx,yy,1-c).wait_recv()
-        i=q(zz,xx,yy)
-        return acc[i].astype(f32)+cbuf[i].astype(f32)
-    def bcopy(zz,far):
-        xx,yy=(dx,dy) if far else (bx,by)
-        i=zz+4*far
-        return pltpu.make_async_remote_copy(src_ref=acc.at[q(zz,xx,yy)],dst_ref=bbuf.at[i],send_sem=bsend.at[i],recv_sem=brecv.at[i],device_id=B,device_id_type=MESH)
-    for far in (1,0):
-        xx,yy=(dx,dy) if far else (bx,by)
-        for k in range(4):
-            zz=zfar(z,k)
-            acc[q(zz,xx,yy)]=have_c(zz,xx,yy).astype(acc.dtype)
-            bcopy(zz,far).start()
-    def acopy(zz):
-        return pltpu.make_async_remote_copy(src_ref=acc.at[q(zz,ax,ay)],dst_ref=abuf.at[zz],send_sem=asend.at[zz],recv_sem=arecv.at[zz],device_id=A,device_id_type=MESH)
-    for k in range(4):
-        zz=zfar(z,k)
-        v=have_c(zz,ax,ay)
-        bcopy(zz,1).wait_recv()
-        acc[q(zz,ax,ay)]=(v+bbuf[zz+4].astype(f32)).astype(acc.dtype)
-        acopy(zz).start()
-    def load(zz):
-        v=have_c(zz,x,y)
-        bcopy(zz,0).wait_recv(); acopy(zz).wait_recv()
-        return v+bbuf[zz].astype(f32)+abuf[zz].astype(f32)
-    def store(v,first):
-        out_ref[...]=v if first else out_ref[...]+v
-    zreduce(z,x,y,c,load,zup,zdn,stage,zsend,zrecv,store)
-    for zz in range(4):
-        for (xx,yy) in sides: ccopy(zz,xx,yy,1-c).wait_send()
-        bcopy(zz,1).wait_send(); bcopy(zz,0).wait_send(); acopy(zz).wait_send()
-
-def rs32(part,cid=1):
-    n,w=part.shape; rows=n//32
-    S=pltpu.SemaphoreType.DMA
-    def V(k): return pltpu.VMEM((k,rows,w),part.dtype)
-    return pl.pallas_call(rs32_kernel,out_shape=jax.ShapeDtypeStruct((rows,w),jnp.float32),
-        in_specs=[pl.BlockSpec(memory_space=pl.ANY)],out_specs=pl.BlockSpec(memory_space=pltpu.VMEM),
-        scratch_shapes=[V(16),V(16),V(8),V(4),V(4),V(4),V(4),S((16,)),S((16,)),S((16,)),S((8,)),S((8,)),S((4,)),S((4,)),S((4,)),S((2,4))],
-        compiler_params=pltpu.CompilerParams(collective_id=cid,has_side_effects=True,vmem_limit_bytes=48*2**20))(part)
+
+    def first(k, carry):
+        stage_c(k)
+        return carry
+
+    lax.fori_loop(0, 4, first, 0)
+    stage_b(0)
+
+    def step(t, carry):
+        @pl.when(t < 3)
+        def _():
+            stage_b(t + 1)
+
+        @pl.when(t < 4)
+        def _():
+            stage_a(t)
+
+        @pl.when(t > 0)
+        def _():
+            stage_z(t - 1)
+
+        return carry
+
+    lax.fori_loop(0, 5, step, 0)
+    def last(zz, carry):
+        for xx, yy in ((dx, dy), (bx, by), (ax, ay), (x, y)):
+            ccopy(zz, xx, yy).wait_send()
+        bcopy(zz, 1).wait_send()
+        bcopy(zz, 0).wait_send()
+        acopy(zz).wait_send()
+
+        @pl.when(zz != z)
+        def _():
+            zcopy(zz, up, zz).wait_send()
+
+        return carry
+
+    lax.fori_loop(0, 4, last, 0)
+
+
+def reduce_all(part, cid):
+    n, w = part.shape
+    rows = n // 32
+    dma = pltpu.SemaphoreType.DMA
+
+    def pieces(k):
+        return pltpu.VMEM((k, rows, w), part.dtype)
+
+    return pl.pallas_call(
+        reduce_all_kernel,
+        in_specs=[pl.BlockSpec(memory_space=pl.ANY)],
+        out_specs=pl.BlockSpec(memory_space=pltpu.VMEM),
+        out_shape=jax.ShapeDtypeStruct((rows, w), jnp.float32),
+        scratch_shapes=[
+            pieces(16), pieces(16), pieces(8), pieces(4), pieces(5),
+            dma((16,)), dma((16,)), dma((16,)), dma((8,)), dma((8,)), dma((4,)), dma((4,)),
+            dma((4,)), dma((5,)),
+        ],
+        compiler_params=pltpu.CompilerParams(
+            collective_id=cid, has_side_effects=True, vmem_limit_bytes=48 * 2**20
+        ),
+        name="reduce_all",
+    )(part)
+
 
 def barrier_plane():
     z,x,y,c=coords()
@@ -346,6 +477,58 @@
         compiler_params=pltpu.CompilerParams(collective_id=cid,has_side_effects=True))(piece)
 
 
+def finish_kernel(a_ref,b_ref,v_ref,ao_ref,bo_ref,vo_ref,vbuf,part,tbuf,lsem,send,recv,vsend,vrecv,tsend,trecv):
+    rows=a_ref.shape[0]; vr=vo_ref.shape[0]
+    z,x,y,c=coords()
+    ctx=lax.axis_index("ctx"); tp=lax.axis_index("tp")
+    b=pltpu.get_barrier_semaphore()
+    Y,C,D=dev(z,x,1-y,c),dev(z,x,y,1-c),dev(z,x,1-y,1-c)
+    peers=[((ctx+i)%8,tp) for i in range(1,8)]+[Y,C,D]
+    for d in peers: pl.semaphore_signal(b,inc=1,device_id=d,device_id_type=MESH)
+    pl.semaphore_wait(b,10)
+    def vcopy(i):
+        to=(ctx+i)%8
+        return pltpu.make_async_remote_copy(src_ref=v_ref.at[pl.ds(pl.multiple_of(to*vr,vr),vr)],dst_ref=vbuf.at[i],send_sem=vsend.at[i],recv_sem=vrecv.at[i],device_id=(to,tp),device_id_type=MESH)
+    for i in range(1,8): vcopy(i).start()
+    def at(o,yy,cc): return o.at[pl.ds(pl.multiple_of((yy*2+cc)*rows,rows),rows)]
+    pairs=[(a_ref,ao_ref),(b_ref,bo_ref)]
+    def cp(n,src,yy,cc,d,k):
+        return pltpu.make_async_remote_copy(src_ref=src,dst_ref=at(pairs[n][1],yy,cc),send_sem=send.at[n,k],recv_sem=recv.at[n,yy*2+cc],device_id=d,device_id_type=MESH)
+    locs=[]
+    for n,(s,o) in enumerate(pairs):
+        l=pltpu.make_async_copy(s,at(o,y,c),lsem.at[n]); l.start(); locs.append(l)
+        cp(n,s,y,c,Y,0).start(); cp(n,s,y,c,C,1).start()
+    total=v_ref[pl.ds(pl.multiple_of(ctx*vr,vr),vr)]
+    for i in range(1,8):
+        vcopy(i).wait_recv()
+        total=total+vbuf[i]
+    part[...]=total
+    def tcopy(k,d):
+        return pltpu.make_async_remote_copy(src_ref=part,dst_ref=tbuf.at[k],send_sem=tsend.at[k],recv_sem=trecv.at[k],device_id=d,device_id_type=MESH)
+    ts=[tcopy(k,d) for k,d in enumerate((Y,C,D))]
+    for t in ts: t.start()
+    for n,(s,o) in enumerate(pairs):
+        cp(n,s,1-y,c,Y,0).wait_recv()
+        cp(n,at(o,1-y,c),1-y,c,C,2).start()
+    for t in ts: t.wait_recv()
+    vo_ref[...]=(part[...]+tbuf[0])+(tbuf[1]+tbuf[2])
+    for n,(s,o) in enumerate(pairs):
+        cp(n,s,y,1-c,C,1).wait_recv(); cp(n,s,1-y,1-c,C,2).wait_recv()
+        locs[n].wait()
+        cp(n,s,y,c,Y,0).wait_send(); cp(n,s,y,c,C,1).wait_send(); cp(n,at(o,1-y,c),1-y,c,C,2).wait_send()
+    for t in ts: t.wait_send()
+    for i in range(1,8): vcopy(i).wait_send()
+
+def finish(a,b,v,cid):
+    rows,w=a.shape; vr=v.shape[0]//8
+    S=pltpu.SemaphoreType.DMA
+    any_=pl.BlockSpec(memory_space=pl.ANY); vm=pl.BlockSpec(memory_space=pltpu.VMEM)
+    return pl.pallas_call(finish_kernel,out_shape=[jax.ShapeDtypeStruct((rows*4,w),a.dtype),jax.ShapeDtypeStruct((rows*4,w),a.dtype),jax.ShapeDtypeStruct((vr,128),jnp.float32)],
+        in_specs=[any_,any_,vm],out_specs=[any_,any_,vm],
+        scratch_shapes=[pltpu.VMEM((8,vr,128),jnp.float32),pltpu.VMEM((vr,128),jnp.float32),pltpu.VMEM((3,vr,128),jnp.float32),S((2,)),S((2,3)),S((2,4)),S((8,)),S((8,)),S((3,)),S((3,))],
+        compiler_params=pltpu.CompilerParams(collective_id=cid,has_side_effects=True))(a,b,v)
+
+
 EPSILON = 1e-06
 ROPE_BASE = 1000000.0
 MASKED_SCORE = -1000000000.0
@@ -357,6 +540,116 @@
     return lax.dot_general(a, b, (dims, ((), ())), preferred_element_type=F32)
 
 
+def nt(a, b):
+    return lax.dot_general(a, b, (((1,), (1,)), ((), ())), preferred_element_type=jnp.float32)
+
+
+def nn(a, b):
+    return lax.dot_general(a, b, (((1,), (0,)), ((), ())), preferred_element_type=jnp.float32)
+
+
+def tn(a, b):
+    return lax.dot_general(a, b, (((0,), (0,)), ((), ())), preferred_element_type=jnp.float32)
+
+
+def expert_kernel(x_ref, cot_ref, wg_ref, wu_ref, wd_ref, s_ref, t_ref, part_ref, gl_ref, ul_ref, hs_ref):
+    bf = jnp.bfloat16
+    width = cot_ref.shape[1]
+    x = x_ref[:, :width]
+    spread = nn(x_ref[:, width:], s_ref[...])
+    gate = nt(x, wg_ref[...])
+    up = nt(x, wu_ref[...])
+    back = nt(cot_ref[...], wd_ref[...])
+    sig = 1.0 / (1.0 + jnp.exp(-gate))
+    silu = gate * sig
+    hidden = silu * up
+    hs = (hidden * spread).astype(bf)
+    hs_ref[...] = hs.T
+    part_ref[:, :width] = nn(hs, wd_ref[...]).astype(bf)
+    prod = hidden * back
+    high = prod.astype(bf)
+    low = (prod - high.astype(jnp.float32)).astype(bf)
+    part_ref[:, 2 * width :] = (nn(high, t_ref[...]) + nn(low, t_ref[...])).astype(bf)
+    grad = back * spread
+    gl = (grad * up * sig * (1.0 + gate * (1.0 - sig))).astype(bf)
+    ul = (grad * silu).astype(bf)
+    gl_ref[...] = gl.T
+    ul_ref[...] = ul.T
+    part_ref[:, width : 2 * width] = (nn(gl, wg_ref[...]) + nn(ul, wu_ref[...])).astype(bf)
+
+
+def expert_blocks(x_all, cot_all, gate_mat, up_mat, down_mat, spread_mat, pick_mat, block=256):
+    n, width = cot_all.shape
+    wide = x_all.shape[1]
+    hid = gate_mat.shape[0]
+    bf = jnp.bfloat16
+
+    def rows(w):
+        return pl.BlockSpec((block, w), lambda i: (i, 0))
+
+    def whole(v):
+        return pl.BlockSpec(v.shape, lambda i: (0, 0), pipeline_mode=pl.Buffered(1))
+
+    return pl.pallas_call(
+        expert_kernel,
+        grid=(n // block,),
+        in_specs=[rows(wide), rows(width)]
+        + [whole(v) for v in (gate_mat, up_mat, down_mat, spread_mat, pick_mat)],
+        out_specs=[rows(width + wide)] + [pl.BlockSpec((hid, block), lambda i: (0, i))] * 3,
+        out_shape=[jax.ShapeDtypeStruct((n, width + wide), bf)]
+        + [jax.ShapeDtypeStruct((hid, n), bf)] * 3,
+        compiler_params=pltpu.CompilerParams(
+            dimension_semantics=("arbitrary",), vmem_limit_bytes=56 * 2**20
+        ),
+        cost_estimate=pl.CostEstimate(
+            flops=12 * n * width * hid, bytes_accessed=10 * n * width, transcendentals=n * hid
+        ),
+        name="experts",
+    )(x_all, cot_all, gate_mat, up_mat, down_mat, spread_mat, pick_mat)
+
+
+def expert_grad_kernel(x_ref, cot_ref, gl_ref, ul_ref, hs_ref, gg_ref, gu_ref, gd_ref):
+    first = pl.program_id(1) == 0
+
+    def put(ref, low, full):
+        value = nn(low[...], full[...])
+
+        @pl.when(first)
+        def _():
+            ref[...] = value
+
+        @pl.when(jnp.logical_not(first))
+        def _():
+            ref[...] += value
+
+    put(gg_ref, gl_ref, x_ref)
+    put(gu_ref, ul_ref, x_ref)
+    put(gd_ref, hs_ref, cot_ref)
+
+
+def expert_grads(x_all, cot_all, gl, ul, hs, block=256):
+    n, width = cot_all.shape
+    hid = gl.shape[0]
+    span = min(n, 2048)
+    cols = pl.BlockSpec((span, block), lambda i, j: (j, i))
+    rows = pl.BlockSpec((hid, span), lambda i, j: (0, j))
+    out = pl.BlockSpec((hid, block), lambda i, j: (0, i))
+    return pl.pallas_call(
+        expert_grad_kernel,
+        grid=(width // block, n // span),
+        in_specs=[cols, cols, rows, rows, rows],
+        out_specs=[out] * 3,
+        out_shape=[jax.ShapeDtypeStruct((hid, width), jnp.float32)] * 3,
+        compiler_params=pltpu.CompilerParams(
+            dimension_semantics=("arbitrary", "arbitrary"), vmem_limit_bytes=56 * 2**20
+        ),
+        cost_estimate=pl.CostEstimate(
+            flops=6 * n * width * hid, bytes_accessed=10 * n * width, transcendentals=0
+        ),
+        name="expert_grads",
+    )(x_all, cot_all, gl, ul, hs)
+
+
 class Links:
     def __init__(self, own):
         self.own = own
@@ -368,7 +661,7 @@
 
     def rs_all(self, part, cid):
         if self.own:
-            return rs32(part, cid)
+            return reduce_all(part, cid)
         return lax.psum_scatter(part, ("ctx", "tp"), scatter_dimension=0, tiled=True).astype(F32)
 
     def ag_ctx(self, piece, cid):
@@ -390,6 +683,14 @@
         if self.own:
             return agtp(piece, cid)
         return lax.all_gather(piece, "tp", axis=0, tiled=True)
+
+
+    def finish(self, a, b, vectors, cid):
+        if self.own:
+            return finish(a, b, vectors, cid)
+        total = lax.psum_scatter(vectors, "ctx", scatter_dimension=0, tiled=True)
+        gathered = (lax.all_gather(v, "tp", axis=0, tiled=True) for v in (a, b))
+        return (*gathered, lax.psum(total, "tp"))
 
 
 def rms_norm(values, gain_vec):
@@ -529,8 +830,7 @@
         return lax.dynamic_slice_in_dim(v, tp_me * rows, rows, axis=0)
 
     cot_own = own_rows(cotangent)
-    cot_all = links.ag_all(cot_own, 0)
-    routes_all = lax.all_gather(routes, "ctx", axis=0, tiled=True)
+    cot_all = lax.all_gather(cot_own, ("ctx", "tp"), axis=0, tiled=True)
 
     token_positions = positions_of(block_order, devices, block_len)
     query_pos = lax.dynamic_index_in_dim(token_positions, me, 0, keepdims=False)
@@ -570,80 +870,41 @@
     residual = own_rows(inputs) + links.rs_tp(attn_part, 2)
     second_normed, second_back = jax.vjp(rms_norm, residual, norm2_gain)
     second_in = second_normed.astype(BF)
-    second_all = links.ag_all(second_in, 3)
-
-    gates_all = gates_of(jnp.dot(second_all, w_router, preferred_element_type=F32), routes_all)
-    gates_mine = lax.dynamic_slice_in_dim(gates_all, me * own_experts, own_experts, axis=1)
-    gates_own = lax.dynamic_slice_in_dim(
-        gates_all, (me * tp_size + tp_me) * rows, rows, axis=0
-    )
-    spread = jnp.repeat(gates_mine, units, axis=1)
-    gate_mat = w_gate.transpose(1, 0, 2).reshape(model_width, hid)
-    up_mat = w_up.transpose(1, 0, 2).reshape(model_width, hid)
+    extra = -(-2 * experts // 128) * 128
+    gates = gates_of(jnp.dot(second_in, w_router, preferred_element_type=F32), own_rows(routes))
+    gates_high = gates.astype(BF)
+    gates_low = (gates - gates_high.astype(F32)).astype(BF)
+    pad = jnp.zeros((rows, extra - 2 * experts), BF)
+    second_all = links.ag_all(
+        jnp.concatenate([second_in, gates_high, gates_low, pad], axis=1), 3
+    )
+    column = jnp.arange(extra, dtype=jnp.int32)[:, None]
+    named = me * own_experts + jnp.arange(hid, dtype=jnp.int32)[None, :] // units
+    pick = (column == named).astype(BF)
+    spread = pick + (column == named + experts).astype(BF)
+    gate_mat = w_gate.transpose(0, 2, 1).reshape(hid, model_width)
+    up_mat = w_up.transpose(0, 2, 1).reshape(hid, model_width)
     down_mat = w_down.reshape(hid, model_width)
-    def expert_block(block):
-        rows_in, cots, weights, own = block
-        gate_pre = jnp.dot(rows_in, gate_mat, preferred_element_type=F32)
-        up_pre = jnp.dot(rows_in, up_mat, preferred_element_type=F32)
-        sig = 1.0 / (1.0 + jnp.exp(-gate_pre))
-        silu = gate_pre * sig
-        hidden = silu * up_pre
-        hidden_low = (hidden * weights).astype(BF)
-        out_part = jnp.dot(hidden_low, down_mat, preferred_element_type=F32).astype(BF)
-        back = dotf(cots, down_mat, ((1,), (1,)))
-        gate_grad = jnp.sum((hidden * back).reshape(-1, own_experts, units), axis=2)
-        grad_hidden = back * weights
-        gate_low = (grad_hidden * up_pre * sig * (1.0 + gate_pre * (1.0 - sig))).astype(BF)
-        up_low = (grad_hidden * silu).astype(BF)
-        entry = dotf(gate_low, gate_mat, ((1,), (1,))) + dotf(up_low, up_mat, ((1,), (1,)))
-        gate_wide = lax.dynamic_update_slice(
-            jnp.zeros((rows_in.shape[0], extra), F32), gate_grad, (0, me * own_experts)
-        )
-        entry = jnp.concatenate([entry.astype(BF), gate_wide.astype(BF)], axis=1)
-        sums = (
-            dotf(rows_in, gate_low, ((0,), (0,))),
-            dotf(rows_in, up_low, ((0,), (0,))),
-            dotf(hidden_low, cots, ((0,), (0,))),
-        )
-        return out_part, entry, sums
-
-    extra = -(-experts // 128) * 128
-    steps = max(1, all_tok // 2048)
-    if steps == 1:
-        out_part, entry, sums = expert_block((second_all, cot_all, spread, gates_mine))
-    else:
-
-        def step(total, block):
-            out_part, entry, sums = expert_block(block)
-            return tuple(a + b for a, b in zip(total, sums)), (out_part, entry)
-
-        def cut(v):
-            return v.reshape(steps, -1, v.shape[1])
-
-        zero = jnp.zeros((model_width, hid), F32)
-        sums, (out_part, entry) = lax.scan(
-            step, (zero, zero, zero.T), (cut(second_all), cut(cot_all), cut(spread), cut(gates_mine))
-        )
-        out_part = out_part.reshape(all_tok, model_width)
-        entry = entry.reshape(all_tok, model_width + extra)
-    out_own = links.rs_all(out_part, 4)
-    layer_out = links.ag_tp((residual + out_own).astype(BF), 5)
-    grad_gate = sums[0].reshape(model_width, own_experts, units).transpose(1, 0, 2)
-    grad_up = sums[1].reshape(model_width, own_experts, units).transpose(1, 0, 2)
-    grad_down = sums[2].reshape(own_experts, units, model_width)
-    entry_own = links.rs_all(entry, 6)
+    part, gate_low, up_low, hidden_low = expert_blocks(
+        second_all, cot_all, gate_mat, up_mat, down_mat, spread, pick.T
+    )
+    sums_own = links.rs_all(part, 6)
+    out_own = sums_own[:, :model_width]
+    entry_own = sums_own[:, model_width:]
     gate_total = entry_own[:, model_width : model_width + experts]
     grad_logits = (
-        gates_own * (gate_total - jnp.sum(gates_own * gate_total, axis=1, keepdims=True))
+        gates * (gate_total - jnp.sum(gates * gate_total, axis=1, keepdims=True))
     ).astype(BF)
-    logits_all = lax.all_gather(grad_logits, ("ctx", "tp"), axis=0, tiled=True)
-    width_part = model_width // devices
-    second_cols = lax.dynamic_slice_in_dim(second_all, me * width_part, width_part, axis=1)
-    grad_router = dotf(second_cols, logits_all, ((0,), (0,)))
     grad_second = entry_own[:, :model_width] + dotf(grad_logits, w_router, ((1,), (1,)))
     grad_resid_norm, grad_norm2 = second_back(grad_second)
     grad_residual = cot_own.astype(F32) + grad_resid_norm
-    grad_attn_low = links.ag_tp(grad_residual.astype(BF), 7)
+    pad = jnp.zeros((rows, -experts % 128), BF)
+    back_all = links.ag_tp(
+        jnp.concatenate([grad_residual.astype(BF), grad_logits, pad], axis=1), 7
+    )
+    grad_attn_low = back_all[:, :model_width]
+    second_own = lax.dynamic_slice(second_all, (me * tok_count, 0), (tok_count, model_width))
+    router_part = dotf(second_own, back_all[:, model_width:], ((0,), (0,)))
     grad_out = dotf(attended, grad_attn_low, ((0,), (0,)))
     grad_mixed = dotf(grad_attn_low, w_out, ((1,), (1,))).astype(BF)
     grad_mixed = grad_mixed.reshape(
@@ -669,39 +930,50 @@
     first_part = first_part + dotf(key_low, key_weight, ((1,), (1,)))
     first_part = first_part + dotf(value_low, value_weight, ((1,), (1,)))
     grad_first = links.rs_tp(first_part.astype(BF), 9)
+    grad_first, gate_low = lax.optimization_barrier((grad_first, gate_low))
+    grads = expert_grads(second_all, cot_all, gate_low, up_low, hidden_low)
+    grad_gate, grad_up = (
+        v.reshape(own_experts, units, model_width).transpose(0, 2, 1) for v in grads[:2]
+    )
+    grad_down = grads[2].reshape(own_experts, units, model_width)
     _, first_back = jax.vjp(rms_norm, own_rows(inputs), norm1_gain)
     grad_input_norm, grad_norm1 = first_back(grad_first)
-    grad_input = links.ag_tp((grad_residual + grad_input_norm).astype(BF), 10)
-
     def over_ctx(v, dim):
         return lax.psum_scatter(v.astype(BF), "ctx", scatter_dimension=dim, tiled=True).astype(F32)
 
-    low_all = jnp.concatenate([query_low, key_low, value_low], axis=1)
-    weight_grads = over_ctx(dotf(first_in, low_all, ((0,), (0,))), 0)
-    wide = query_low.shape[1]
-    grad_query = weight_grads[:, :wide]
-    grad_key = weight_grads[:, wide : wide + kv_width]
-    grad_value = weight_grads[:, wide + kv_width :]
+    grad_query = over_ctx(dotf(first_in, query_low, ((0,), (0,))), 0)
+    kv_part = dotf(first_in, jnp.concatenate([key_low, value_low], axis=1), ((0,), (0,)))
+    small = links.rs_ctx(jnp.concatenate([kv_part, router_part], axis=1).astype(BF), 11)
+    grad_key = small[:, :kv_width]
+    grad_value = small[:, kv_width : 2 * kv_width]
+    grad_router = small[:, 2 * kv_width : 2 * kv_width + experts]
     grad_out = over_ctx(grad_out, 1)
-    vectors = lax.psum(
-        jnp.concatenate([grad_norm1, grad_norm2, grad_qgain, grad_kgain]), ("ctx", "tp")
-    )
-
-    def piece_of(start, size):
-        part = size // devices
-        return lax.dynamic_slice_in_dim(vectors, start + me * part, part, axis=0)
+    vectors = [
+        v.reshape(devices, -1) for v in (grad_norm1, grad_norm2, grad_qgain, grad_kgain)
+    ]
+    sizes = [v.shape[1] for v in vectors]
+    pad = jnp.zeros((devices, -sum(sizes) % 1024), F32)
+    packed = jnp.concatenate([*vectors, pad], axis=1).reshape(-1, 128)
+    grad_input, layer_out, total = links.finish(
+        (grad_residual + grad_input_norm).astype(BF), (residual + out_own).astype(BF), packed, 10
+    )
+    total = total.reshape(-1)
+
+    def piece_of(n):
+        start = sum(sizes[:n])
+        return total[start : start + sizes[n]]
 
     return (
         layer_out,
         grad_input,
-        piece_of(0, model_width),
+        piece_of(0),
         grad_query,
         grad_key,
         grad_value,
-        piece_of(2 * model_width, head_size),
-        piece_of(2 * model_width + head_size, head_size),
+        piece_of(2),
+        piece_of(3),
         grad_out,
-        piece_of(model_width, model_width),
+        piece_of(1),
         grad_router,
         grad_gate,
         grad_up,

time: 707 us -> 520 us (0.74)
  matrix products: 168 us -> 51.3 us
  blocking collectives: 107 us -> 0 us
  Pallas kernels: 300 us -> 357 us
  other arithmetic: 57.1 us -> 45.7 us
  local copies, waits for them, and re-layouts: 51.7 us -> 42.4 us
    pallas_call x2 -> x4, Pallas kernels: 109 us -> 185 us  [the longest x1 78.7 us: reduce_all(): pl.pallas_call(reduce_all_kernel, in_specs=[pl.BlockSpec(memory_space=pl....]
    dot_general x14 -> x9, matrix products: 87.3 us -> 17.1 us  [dotf(): return lax.dot_general(a, b, (dims, ((), ())), preferred_element_type=F32)]
    all_gather x2 -> x0, blocking collectives: 69.5 us -> none  [the longest x1 38.9 us: shards(): logits_all = lax.all_gather(grad_logits, ('ctx', 'tp'), axis=0, tiled=True)]
    pallas_call x1 -> x2, Pallas kernels: 21.1 us -> 67.9 us  [rsctx(): pl.pallas_call(rsctx_kernel, out_shape=jax.ShapeDtypeStruct((rows, w), jn...]
    dot_general x4 -> x1, matrix products: 40.1 us -> 0.3 us  [shards(): jnp.dot(second_in, w_router, preferred_element_type=F32)]
    pallas_call x2 -> x1, Pallas kernels: 83.6 us -> 45.3 us  [ag32(): pl.pallas_call(ag32_kernel, out_shape=jax.ShapeDtypeStruct((rows * 32, w)...]
    psum x1 -> x0, blocking collectives: 37.1 us -> none  [shards(): lax.psum(jnp.concatenate([grad_norm1, grad_norm2, grad_qgain, grad_kgain]...]
    pallas_call x3 -> x1, Pallas kernels: 45.4 us -> 10.6 us  [agtp(): pl.pallas_call(agtp_kernel, out_shape=jax.ShapeDtypeStruct((rows * 4, w),...]
  transfers between devices with their start and end apart: 2 -> 3, of which waited for: 0 -> 0; matrix products, arithmetic and copies ran while one was open for 15% -> 23% of each run, Pallas kernels for 17% -> 42%
where the time goes in v2:
time: 520 us; the launch traced here: 513 us
  Pallas kernels  357 us (69%)
  matrix products  51.3 us (10%)
  other arithmetic  45.7 us (9%)
  local copies, waits for them, and re-layouts  42.4 us (8%)
  between operations  15.1 us (3%)
    pallas_call x1, Pallas kernels, reduce_all(): pl.pallas_call(reduce_all_kernel, in_specs=[pl.BlockSpec(memory_space=pl....  78.7 us
    pallas_call x2, Pallas kernels, rsctx(): pl.pallas_call(rsctx_kernel, out_shape=jax.ShapeDtypeStruct((rows, w), jn...  67.9 us
    pallas_call x1, Pallas kernels, expert_blocks(): pl.pallas_call(expert_kernel, grid=(n // block,), in_specs=[rows(wide), r...  51.3 us
    pallas_call x1, Pallas kernels, ag32(): pl.pallas_call(ag32_kernel, out_shape=jax.ShapeDtypeStruct((rows * 32, w)...  45.3 us
    pallas_call x1, Pallas kernels, finish(): pl.pallas_call(finish_kernel, out_shape=[jax.ShapeDtypeStruct((rows * 4,...  28.1 us
    pallas_call x1, Pallas kernels, agctx(): pl.pallas_call(agctx_kernel, out_shape=jax.ShapeDtypeStruct((rows * 8, w)...  27.4 us
    pallas_call x1, Pallas kernels, expert_grads(): pl.pallas_call(expert_grad_kernel, grid=(width // block, n // span), in_s...  26.7 us
    pallas_call x2, Pallas kernels, rstp(): pl.pallas_call(rstp_kernel, out_shape=jax.ShapeDtypeStruct((rows, w), jnp...  21.4 us
  transfers between devices with their start and end apart: 3, of which 0 were waited for; matrix products, arithmetic and copies ran while one was open for 23% of the time, Pallas kernels for 42%

profile of v2, /device:TPU:0, one launch (start us, length us, event | category | flops | bytes accessed | tf_op | source)
XLA Modules:
  0.0 512.6 jit_solution(6703072348117165913)
XLA Ops:
  10.9 2.8 convert_element_type.131
  14.0 3.5 convolution_bitcast_fusion.2
  32.7 27.4 %shard_map.263 = bf16[2048,256]{1,0:T(8,128)(2,1)} custom-call(bf16[256,256]{1,0:T(8,128)(2,1)} %pad_maximum_fusion.3.x_ref), custom_call_target="tpu_custom_call" | custom-call | tf_op jit(solution)/shard_map/pallas_call | solution.py:396
  63.7 8.9 %while.26 = (s32[]{:T(128)}, bf16[2,128,1,8,128]{1,4,3,2,0:T(8,128)(2,1)S(1)}, f32[2,128,1,8]{1,3,2,0:T(8,128)}, bf16[2,1024,1,128]{3,1,2,0:T(8,128)(2,1)S(1)}, ...) while((s32[]{:T(128)}, ...), condition=%wide.region_6.7_spmd, body=%wide.region_3.6_spmd.sunk | while | flops 549583872 | bytes 14467173 | solution.py:865
  74.8 3.5 convolution_convert_fusion.3.in_ref
  78.4 12.8 %shard_map.264 = f32[64,2048]{1,0:T(8,128)S(1)} custom-call(bf16[256,2048]{1,0:T(8,128)(2,1)S(1)} %convolution_convert_fusion.3.in_ref), custom_call_target="tpu_custom_call" | custom-call | tf_op jit(solution)/shard_map/pallas_call | solution.py:450
  97.2 45.3 %shard_map.265.x_ref = bf16[2048,2176]{1,0:T(8,128)(2,1)} custom-call(bf16[64,2176]{1,0:T(8,128)(2,1)} %concatenate.58.x_ref), custom_call_target="tpu_custom_call" | custom-call | tf_op jit(solution)/shard_map/pallas_call | solution.py:95
  144.1 51.3 %experts.1 = (bf16[2048,4224]{1,0:T(8,128)(2,1)}, bf16[768,2048]{1,0:T(8,128)(2,1)}, bf16[768,2048]{1,0:T(8,128)(2,1)}, bf16[768,2048]{1,0:T(8,128)(2,1)}) custom-call(bf16[2048,2176]{1,0:T(8,128)(2,1)} %shard_map.265.x_ref, bf16[2048,2048]{1,0:T(8,128)(2,1)} %all-gather.2.cloned.1.call-done.cot_ref, bf16[768,2048]{1,0:T(8,128)(2,1)} %bitcast.375, ...), custom_call_target="tpu_custom_call" | custom-call | flops 38654705664 | bytes 41943040 | tf_op jit(solution)/shard_map/experts/pallas_call | solution.py:593
  195.4 78.7 %reduce_all.1 = f32[64,4224]{1,0:T(8,128)S(1)} custom-call(bf16[2048,4224]{1,0:T(8,128)(2,1)} %get-tuple-element.129.part_ref), custom_call_target="tpu_custom_call" | custom-call | tf_op jit(solution)/shard_map/reduce_all/pallas_call | solution.py:320
  279.2 10.6 %shard_map.266 = bf16[256,2176]{1,0:T(8,128)(2,1)} custom-call(bf16[64,2176]{1,0:T(8,128)(2,1)} %concatenate.59.x_ref), custom_call_target="tpu_custom_call" | custom-call | tf_op jit(solution)/shard_map/pallas_call | solution.py:474
  289.9 4.5 convolution_convert_fusion
  294.5 3.8 fusion.61
  298.4 30.7 %while.27 = (s32[]{:T(128)}, f32[2,128,1,8,128]{4,3,1,0,2:T(8,128)}, bf16[2,1024,1,128]{1,3,2,0:T(8,128)(2,1)}, bf16[2,1024,1,128]{1,3,2,0:T(8,128)(2,1)}, bf16[...) while((s32[]{:T(128)}, ...), condition=%wide.region_15.16_spmd, body=%wide.region_13.15_spmd.sunk | while | flops 1359084544 | bytes 71611280 | solution.py:913
  309.6 4.2 fusion.182
  324.8 4.2 fusion.182
  329.1 3.0 multiply_add_fusion.1
  338.1 3.5 convolution_convert_fusion.1
  347.4 2.7 copy.172
  350.1 3.6 pad_maximum_fusion.1
  353.9 27.2 %shard_map.267 = f32[256,256]{1,0:T(8,128)S(1)} custom-call(bf16[2048,256]{1,0:T(8,128)(2,1)S(1)} %bitcast.348), custom_call_target="tpu_custom_call" | custom-call | tf_op jit(solution)/shard_map/pallas_call | solution.py:423
  384.4 8.6 %shard_map.268 = f32[64,2048]{1,0:T(8,128)S(1)} custom-call(bf16[256,2048]{1,0:T(8,128)(2,1)S(1)} %fusion.60.in_ref), custom_call_target="tpu_custom_call" | custom-call | tf_op jit(solution)/shard_map/pallas_call | solution.py:450
  395.6 40.7 %shard_map.270 = f32[256,384]{1,0:T(8,128)S(1)} custom-call(bf16[2048,384]{1,0:T(8,128)(2,1)S(1)} %pad_maximum_fusion.in_ref), custom_call_target="tpu_custom_call" | custom-call | tf_op jit(solution)/shard_map/pallas_call | solution.py:423
  441.3 28.1 %shard_map.269 = (bf16[256,2048]{1,0:T(8,128)(2,1)}, bf16[256,2048]{1,0:T(8,128)(2,1)}, f32[8,128]{1,0:T(8,128)}) custom-call(bf16[64,2048]{1,0:T(8,128)(2,1)} %fusion.68.a_ref, bf16[64,2048]{1,0:T(8,128)(2,1)} %get-tuple-element.374.b_ref, f32[64,128]{1,0:T(8,128)} %reshape.626.v_ref), custom_call_target="tpu_custom_call" | custom-call | tf_op jit(solution)/shard_map/pallas_call | solution.py:526
  472.9 26.7 %expert_grads.1 = (f32[768,2048]{1,0:T(8,128)}, f32[768,2048]{1,0:T(8,128)}, f32[768,2048]{1,0:T(8,128)}) custom-call(bf16[2048,2176]{1,0:T(8,128)(2,1)} %shard_map.265.x_ref, bf16[2048,2048]{1,0:T(8,128)(2,1)} %all-gather.2.cloned.1.call-done.cot_ref, bf16[768,2048]{1,0:T(8,128)(2,1)} %get-tuple-element.139.gl_ref, ...), custom_call_target="tpu_custom_call" | custom-call | flops 19327352832 | bytes 41943040 | tf_op jit(solution)/shard_map/expert_grads/pallas_call | solution.py:637
  (306 shorter events, 100.1 us)
Async XLA Ops:
  7.2 136.9 %all-gather.2.cloned.1.call-start = ((), (), s32[]{:S(2)}) async-start(), calls=%async_computation.2 | async-start | bytes 8650752 | tf_op jit(solution)/shard_map/all_gather | solution.py:833
  9.1 490.5 %reduce-scatter.5.cloned.1.call-start = ((), (), s32[]{:S(2)}) async-start(), calls=%async_computation.4 | async-start | bytes 4718592 | tf_op jit(solution)/shard_map/reduce_scatter | solution.py:942
  27.2 36.2 %copy-start.21 = (f32[256,128]{1,0:T(8,128)}, f32[256,128]{1,0:T(8,128)S(1)}, u32[]{:S(2)}) copy-start(f32[256,128]{1,0:T(8,128)S(1)} %copy.151) | copy-start | bytes 393220
  93.2 182.7 %copy-start.10 = (f32[64,2048]{1,0:T(8,128)}, f32[64,2048]{1,0:T(8,128)S(1)}, u32[]{:S(2)}) copy-start(f32[64,2048]{1,0:T(8,128)S(1)} %get-tuple-element.360) | copy-start | bytes 1572868
  195.4 78.8 %copy-start.32 = (f32[64,32]{1,0:T(8,128)S(1)}, f32[64,32]{1,0:T(8,128)}, u32[]{:S(2)}) copy-start(f32[64,32]{1,0:T(8,128)} %get-tuple-element.358) | copy-start | bytes 24580
  195.4 79.0 %copy-start.37 = (f32[2048]{0:T(1024)S(1)}, f32[2048]{0:T(1024)}, u32[]{:S(2)}) copy-start(f32[2048]{0:T(1024)} %param.30) | copy-start | bytes 24580
  195.4 79.9 %copy-start.59 = (f32[64]{0:T(128)S(1)}, f32[64]{0:T(128)}, u32[]{:S(2)}) copy-start(f32[64]{0:T(128)} %get-tuple-element.367) | copy-start | bytes 772
  195.4 79.9 %copy-start.62 = (f32[64]{0:T(128)S(1)}, f32[64]{0:T(128)}, u32[]{:S(2)}) copy-start(f32[64]{0:T(128)} %copy-done.61) | copy-start | bytes 772
  294.4 207.4 %reduce-scatter.3.cloned.1.call-start = ((), (), s32[]{:S(2)}) async-start(), calls=%async_computation.3 | async-start | bytes 4718592 | tf_op jit(solution)/shard_map/reduce_scatter | solution.py:942
  347.4 33.8 %copy-start.43 = (f32[1,2,128]{2,0,1:T(1,128)S(1)}, f32[1,2,128]{2,0,1:T(1,128)}, u32[]{:S(2)}) copy-start(f32[1,2,128]{2,0,1:T(1,128)} %copy-done.42) | copy-start | bytes 3076
  347.4 33.8 %copy-start.52 = (f32[64]{0:T(128)S(1)}, f32[64]{0:T(128)}, u32[]{:S(2)}) copy-start(f32[64]{0:T(128)} %copy-done.51) | copy-start | bytes 772
  347.4 34.4 %copy-start.22 = (f32[256,128]{1,0:T(8,128)S(1)}, f32[256,128]{1,0:T(8,128)}, u32[]{:S(2)}) copy-start(f32[256,128]{1,0:T(8,128)} %copy-done.21) | copy-start | bytes 393220
  347.4 34.4 %copy-start.45 = (f32[256]{0:T(256)S(1)}, f32[256]{0:T(256)}, u32[]{:S(2)}) copy-start(f32[256]{0:T(256)} %copy-done.44) | copy-start | bytes 3076
  347.4 34.4 %copy-start.56 = (f32[128]{0:T(128)S(1)}, f32[128]{0:T(128)}, u32[]{:S(2)}) copy-start(f32[128]{0:T(128)} %param.28) | copy-start | bytes 1540
  350.1 31.9 %copy-start.58 = (f32[256]{0:T(256)S(1)}, f32[256]{0:T(256)}, u32[]{:S(2)}) copy-start(f32[256]{0:T(256)} %copy-done.57) | copy-start | bytes 3076
  350.1 32.1 %copy-start.66 = (bf16[2048,1024]{1,0:T(8,128)(2,1)S(1)}, bf16[2048,1024]{1,0:T(8,128)(2,1)}, u32[]{:S(2)}) copy-start(bf16[2048,1024]{1,0:T(8,128)(2,1)} %param.24) | copy-start | bytes 12582916
  394.7 42.2 %copy-start.55 = (f32[64]{0:T(128)S(1)}, f32[64]{0:T(128)}, u32[]{:S(2)}) copy-start(f32[64]{0:T(128)} %get-tuple-element.394) | copy-start | bytes 772
  394.7 43.7 %copy-start.41 = (f32[2048]{0:T(1024)S(1)}, f32[2048]{0:T(1024)}, u32[]{:S(2)}) copy-start(f32[2048]{0:T(1024)} %get-tuple-element.314) | copy-start | bytes 24580
  395.4 43.8 %copy-start.60 = (f32[64]{0:T(128)S(1)}, f32[64]{0:T(128)}, u32[]{:S(2)}) copy-start(f32[64]{0:T(128)} %get-tuple-element.367) | copy-start | bytes 772
  395.4 43.8 %copy-start.11 = (f32[64,2048]{1,0:T(8,128)S(1)}, f32[64,2048]{1,0:T(8,128)}, u32[]{:S(2)}) copy-start(f32[64,2048]{1,0:T(8,128)} %copy-done.10) | copy-start | bytes 1572868
  395.4 43.8 %copy-start.18 = (f32[64,2048]{1,0:T(8,128)S(1)}, f32[64,2048]{1,0:T(8,128)}, u32[]{:S(2)}) copy-start(f32[64,2048]{1,0:T(8,128)} %copy-done.17) | copy-start | bytes 1572868
  395.4 43.8 %copy-start.38 = (f32[2048]{0:T(1024)S(1)}, f32[2048]{0:T(1024)}, u32[]{:S(2)}) copy-start(f32[2048]{0:T(1024)} %param.30) | copy-start | bytes 24580
  395.4 43.8 %copy-start.54 = (f32[64]{0:T(128)S(1)}, f32[64]{0:T(128)}, u32[]{:S(2)}) copy-start(f32[64]{0:T(128)} %copy-done.53) | copy-start | bytes 772
  472.9 31.0 %copy-start.26 = (bf16[256,2048]{1,0:T(8,128)(2,1)S(1)}, bf16[256,2048]{1,0:T(8,128)(2,1)}, u32[]{:S(2)}) copy-start(bf16[256,2048]{1,0:T(8,128)(2,1)} %get-tuple-element.596) | copy-start | bytes 3145732
  (55 other events, 258.9 us)
Sparse Core Ops, SparseCore 0:
  11.5 91.8 all-gather.1
  294.5 92.9 reduce-scatter.4
  391.6 101.0 reduce-scatter.2

commit v3 on v2

--- a/solution.py
+++ b/solution.py
@@ -97,49 +97,6 @@
         scratch_shapes=[pltpu.SemaphoreType.DMA,pltpu.SemaphoreType.DMA((5,32)),pltpu.SemaphoreType.DMA((32,))],
         compiler_params=pltpu.CompilerParams(collective_id=cid,has_side_effects=True))(piece)
 
-def zmask(z):
-    return (3-z)//3, (z%3)%2, (z%3)//2, z//3
-def zfar(z,k):
-    m0,m1,m2,m3=zmask(z)
-    t=((3,2,1,0),(3,0,2,1),(0,3,1,2),(0,1,2,3))
-    return m0*t[0][k]+m1*t[1][k]+m2*t[2][k]+m3*t[3][k]
-
-def zreduce(z,x,y,c,load,zup,zdn,stage,zsend,zrecv,out_store):
-    def cp(buf,zz,d,k,r):
-        return pltpu.make_async_remote_copy(src_ref=stage.at[zz],dst_ref=buf.at[zz],send_sem=zsend.at[zz],recv_sem=zrecv.at[r,zz],device_id=d,device_id_type=MESH)
-    up,down=dev(z+1,x,y,c),dev(z-1,x,y,c)
-    for k in range(3):
-        zz=zfar(z,k)
-        @pl.when(zz>z)
-        def _():
-            stage[zz]=load(zz).astype(stage.dtype)
-            @pl.when(z>0)
-            def _():
-                cp(zup,zz,up,0,0).wait_recv()
-                stage[zz]=(stage[zz].astype(jnp.float32)+zup[zz].astype(jnp.float32)).astype(stage.dtype)
-            cp(zup,zz,up,0,0).start()
-        @pl.when(zz<z)
-        def _():
-            stage[zz]=load(zz).astype(stage.dtype)
-            @pl.when(z<3)
-            def _():
-                cp(zdn,zz,down,1,1).wait_recv()
-                stage[zz]=(stage[zz].astype(jnp.float32)+zdn[zz].astype(jnp.float32)).astype(stage.dtype)
-            cp(zdn,zz,down,1,1).start()
-    out_store(load(z),True)
-    @pl.when(z>0)
-    def _():
-        cp(zup,z,up,0,0).wait_recv()
-        out_store(zup[z].astype(jnp.float32),False)
-    @pl.when(z<3)
-    def _():
-        cp(zdn,z,down,1,1).wait_recv()
-        out_store(zdn[z].astype(jnp.float32),False)
-    for k in range(3):
-        zz=zfar(z,k)
-        cp(zup,zz,up,0,0).wait_send()
-
-
 def far_z(z, k):
     half = z // 2
     near = z + half * (3 - 2 * z)
@@ -334,199 +291,730 @@
     )(part)
 
 
-def barrier_plane():
-    z,x,y,c=coords()
-    b=pltpu.get_barrier_semaphore()
-    def sig(d): pl.semaphore_signal(b,inc=1,device_id=d,device_id_type=MESH)
-    sig(dev(z,1-x,y,c))
-    @pl.when(z<3)
-    def _(): sig(dev(z+1,x,y,c))
-    @pl.when(z>0)
-    def _(): sig(dev(z-1,x,y,c))
-    pl.semaphore_wait(b,3-(3-z)//3-z//3)
-
-def barrier_tp():
-    z,x,y,c=coords()
-    b=pltpu.get_barrier_semaphore()
-    for d in (dev(z,x,1-y,c),dev(z,x,y,1-c)):
-        pl.semaphore_signal(b,inc=1,device_id=d,device_id_type=MESH)
-    pl.semaphore_wait(b,2)
-
-def agctx_kernel(x_ref,out_ref,lsem,send,recv):
-    rows=x_ref.shape[0]
-    z,x,y,c=coords()
-    barrier_plane()
-    def at(p): return out_ref.at[pl.ds(pl.multiple_of(p*rows,rows),rows)]
-    def cp(p,d,k,own=False):
-        return pltpu.make_async_remote_copy(src_ref=x_ref if own else at(p),dst_ref=at(p),send_sem=send.at[k,p],recv_sem=recv.at[p],device_id=d,device_id_type=MESH)
-    up,down,X=dev(z+1,x,y,c),dev(z-1,x,y,c),dev(z,1-x,y,c)
-    me=z*2+x
-    loc=pltpu.make_async_copy(x_ref,at(me),lsem); loc.start()
-    @pl.when(z<3)
-    def _(): cp(me,up,0,True).start()
-    @pl.when(z>0)
-    def _(): cp(me,down,1,True).start()
-    cp(me,X,2,True).start()
-    for d in (1,2,3):
-        @pl.when(z-d>=0)
-        def _():
-            p=(z-d)*2+x; cp(p,X,2).wait_recv()
-            @pl.when(z<3)
-            def _(): cp(p,up,0).start()
-            cp(p,X,2).start()
-        @pl.when(z+d<=3)
-        def _():
-            p=(z+d)*2+x; cp(p,X,2).wait_recv()
-            @pl.when(z>0)
-            def _(): cp(p,down,1).start()
-            cp(p,X,2).start()
-    loc.wait()
-    for zz in range(4):
-        cp(zz*2+1-x,X,2).wait_recv()
-        p=zz*2+x
-        @pl.when((z<3)&(zz<=z))
-        def _(): cp(p,up,0).wait_send()
-        @pl.when((z>0)&(zz>=z))
-        def _(): cp(p,down,1).wait_send()
-        cp(p,X,2).wait_send()
-
-def agctx(piece,cid=2):
-    rows,w=piece.shape
-    S=pltpu.SemaphoreType.DMA
-    return pl.pallas_call(agctx_kernel,out_shape=jax.ShapeDtypeStruct((rows*8,w),piece.dtype),
-        in_specs=[pl.BlockSpec(memory_space=pl.ANY)],out_specs=pl.BlockSpec(memory_space=pl.ANY),
-        scratch_shapes=[S,S((3,8)),S((8,))],
-        compiler_params=pltpu.CompilerParams(collective_id=cid,has_side_effects=True))(piece)
-
-def rsctx_kernel(in_ref,out_ref,xbuf,zup,zdn,stage,xsend,xrecv,zsend,zrecv):
-    rows=out_ref.shape[0]
-    z,x,y,c=coords()
-    barrier_plane()
-    f32=jnp.float32
-    X=dev(z,1-x,y,c)
-    def at(p): return in_ref.at[pl.ds(pl.multiple_of(p*rows,rows),rows)]
-    def xcopy(zz):
-        return pltpu.make_async_remote_copy(src_ref=at(zz*2+1-x),dst_ref=xbuf.at[zz],send_sem=xsend.at[zz],recv_sem=xrecv.at[zz],device_id=X,device_id_type=MESH)
-    for k in range(4): xcopy(zfar(z,k)).start()
-    def load(zz):
-        xcopy(zz).wait_recv()
-        return at(zz*2+x)[...].astype(f32)+xbuf[zz].astype(f32)
-    def store(v,first):
-        out_ref[...]=v if first else out_ref[...]+v
-    zreduce(z,x,y,c,load,zup,zdn,stage,zsend,zrecv,store)
-    for zz in range(4): xcopy(zz).wait_send()
-
-def rsctx(part,cid=3):
-    n,w=part.shape; rows=n//8
-    S=pltpu.SemaphoreType.DMA
-    def V(k): return pltpu.VMEM((k,rows,w),part.dtype)
-    return pl.pallas_call(rsctx_kernel,out_shape=jax.ShapeDtypeStruct((rows,w),jnp.float32),
-        in_specs=[pl.BlockSpec(memory_space=pltpu.VMEM)],out_specs=pl.BlockSpec(memory_space=pltpu.VMEM),
-        scratch_shapes=[V(4),V(4),V(4),V(4),S((4,)),S((4,)),S((4,)),S((2,4))],
-        compiler_params=pltpu.CompilerParams(collective_id=cid,has_side_effects=True,vmem_limit_bytes=32*2**20))(part)
-
-def rstp_kernel(in_ref,out_ref,cbuf,ybuf,stage,csend,crecv,ysend,yrecv):
-    rows=out_ref.shape[0]
-    z,x,y,c=coords()
-    barrier_tp()
-    f32=jnp.float32
-    def at(yy,cc): return in_ref.at[pl.ds(pl.multiple_of((yy*2+cc)*rows,rows),rows)]
+def barrier_wide():
+    z, x, y, c = coords()
+    ctx, tp = lax.axis_index("ctx"), lax.axis_index("tp")
+    bar = pltpu.get_barrier_semaphore()
+    for i in range(1, 8):
+        pl.semaphore_signal(bar, inc=1, device_id=((ctx + i) % 8, tp), device_id_type=MESH)
+    for to in (dev(z, x, 1 - y, c), dev(z, x, y, 1 - c), dev(z, x, 1 - y, 1 - c)):
+        pl.semaphore_signal(bar, inc=1, device_id=to, device_id_type=MESH)
+    pl.semaphore_wait(bar, 10)
+
+
+class Columns:
+    def __init__(self, src, buf, send, recv, tsend, trecv):
+        self.src, self.buf, self.send, self.recv = src, buf, send, recv
+        self.tsend, self.trecv = tsend, trecv
+        self.ctx, self.tp = lax.axis_index("ctx"), lax.axis_index("tp")
+        z, x, y, c = coords()
+        self.Y, self.C = dev(z, x, 1 - y, c), dev(z, x, y, 1 - c)
+        self.mine, self.by_y, self.by_c, self.by_d = y * 2 + c, (1 - y) * 2 + c, y * 2 + 1 - c, (1 - y) * 2 + 1 - c
+
+    def push(self, i):
+        to = (self.ctx + i) % 8
+        return pltpu.make_async_remote_copy(
+            src_ref=self.src.at[to], dst_ref=self.buf.at[self.ctx, self.tp],
+            send_sem=self.send.at[i], recv_sem=self.recv.at[i], device_id=(to, self.tp),
+            device_id_type=MESH)
+
+    def over(self, part, to, k):
+        return pltpu.make_async_remote_copy(
+            src_ref=self.buf.at[:, part], dst_ref=self.buf.at[:, part], send_sem=self.tsend.at[k],
+            recv_sem=self.trecv.at[part], device_id=to, device_id_type=MESH)
+
+    def start(self):
+        for i in range(1, 8):
+            self.push(i).start()
+        self.buf[self.ctx, self.tp] = self.src[self.ctx]
+
+    def exchange(self):
+        for i in range(1, 8):
+            self.push(i).wait_recv()
+        self.over(self.mine, self.Y, 0).start()
+        self.over(self.mine, self.C, 1).start()
+
+    def forward(self):
+        self.over(self.by_y, self.Y, 0).wait_recv()
+        self.over(self.by_y, self.C, 2).start()
+
+    def finish(self):
+        self.over(self.by_c, self.C, 1).wait_recv()
+        self.over(self.by_d, self.C, 2).wait_recv()
+        for i in range(1, 8):
+            self.push(i).wait_send()
+        self.over(self.mine, self.Y, 0).wait_send()
+        self.over(self.mine, self.C, 1).wait_send()
+        self.over(self.by_y, self.C, 2).wait_send()
+
+
+class Spread:
+    def __init__(self, place, send, recv, first=None):
+        self.place, self.send, self.recv, self.first = place, send, recv, first
+        z, x, y, c = coords()
+        self.z, self.x = z, x
+        self.X = dev(z, 1 - x, y, c)
+        self.up, self.down = dev(z + 1, x, y, c), dev(z - 1, x, y, c)
+        self.me = z * 2 + x
+
+    def copy(self, p, to, k, own=False):
+        src = self.first if own and self.first is not None else self.place(p)
+        return pltpu.make_async_remote_copy(
+            src_ref=src, dst_ref=self.place(p), send_sem=self.send.at[k, p],
+            recv_sem=self.recv.at[p], device_id=to, device_id_type=MESH)
+
+    def start_x(self):
+        self.copy(self.me, self.X, 2, True).start()
+
+    def start_z(self):
+        @pl.when(self.z < 3)
+        def _():
+            self.copy(self.me, self.up, 0, True).start()
+
+        @pl.when(self.z > 0)
+        def _():
+            self.copy(self.me, self.down, 1, True).start()
+
+    def pass_on(self, d):
+        z, x = self.z, self.x
+
+        @pl.when(z - d >= 0)
+        def _():
+            p = (z - d) * 2 + x
+            self.copy(p, self.X, 2).wait_recv()
+
+            @pl.when(z < 3)
+            def _():
+                self.copy(p, self.up, 0).start()
+
+            self.copy(p, self.X, 2).start()
+
+        @pl.when(z + d <= 3)
+        def _():
+            p = (z + d) * 2 + x
+            self.copy(p, self.X, 2).wait_recv()
+
+            @pl.when(z > 0)
+            def _():
+                self.copy(p, self.down, 1).start()
+
+            self.copy(p, self.X, 2).start()
+
+    def arrive(self):
+        for zz in range(4):
+            self.copy(zz * 2 + 1 - self.x, self.X, 2).wait_recv()
+
+    def finish(self):
+        z, x = self.z, self.x
+        for zz in range(4):
+            p = zz * 2 + x
+
+            @pl.when((z < 3) & (zz <= z))
+            def _():
+                self.copy(p, self.up, 0).wait_send()
+
+            @pl.when((z > 0) & (zz >= z))
+            def _():
+                self.copy(p, self.down, 1).wait_send()
+
+            self.copy(p, self.X, 2).wait_send()
+
+
+def row_norm(v):
+    return lax.rsqrt(jnp.mean(v * v, axis=1, keepdims=True) + 1e-06)
+
+
+def turn(v, cos, sin):
+    return v * cos + pltpu.roll(v, v.shape[1] // 2, 1) * sin
+
+
+def turn_back(v, cos, sin):
+    return v * cos - pltpu.roll(v, v.shape[1] // 2, 1) * sin
+
+
+def front_kernel(
+    x_ref, g1_ref, wq_ref, wk_ref, wv_ref, qg_ref, kg_ref, cos_ref, sin_ref, qpos_ref, kpos_ref,
+    wo_ref, g2_ref, wr_ref, routes_ref,
+    first_ref, qraw_ref, kraw_ref, qrot_ref, kv_ref, att_ref, log_ref, res_ref, gates_ref, piece_ref, cols_ref,
+    wq, wo, part, cbuf, ybuf, stage, csrc,
+    wsem, ksend, krecv, csend, crecv, ysend, yrecv, psend, precv, tsend, trecv,
+):
+    f32, bf = jnp.float32, jnp.bfloat16
+    z, x, y, c = coords()
+    rows = res_ref.shape[0]
+    experts = wr_ref.shape[0] // 4
+    head = qg_ref.shape[1]
+    heads = wq_ref.shape[1] // head
+    half = x_ref.shape[0] // 2
+    wqc = pltpu.make_async_copy(wq_ref, wq, wsem.at[0])
+    woc = pltpu.make_async_copy(wo_ref, wo, wsem.at[1])
+    wqc.start()
+    woc.start()
+    Y, C = dev(z, x, 1 - y, c), dev(z, x, y, 1 - c)
+    barrier_wide()
+
+    value = x_ref[...].astype(f32)
+    first = (value * row_norm(value) * g1_ref[...]).astype(bf)
+    first_ref[...] = first
+    cos, sin = cos_ref[...], sin_ref[...]
+    kraw = nn(first, wk_ref[...])
+    kraw_ref[...] = kraw
+    krot = turn(kraw * row_norm(kraw) * kg_ref[...], cos, sin).astype(bf)
+    vrow = nn(first, wv_ref[...]).astype(bf)
+    me = z * 2 + x
+    for s in range(2):
+        kv_ref[s, me] = krot[s * half : (s + 1) * half]
+        kv_ref[2 + s, me] = vrow[s * half : (s + 1) * half]
+
+    keys_out = Spread(lambda p: kv_ref.at[:, p], ksend, krecv)
+    keys_out.start_z()
+    keys_out.start_x()
+
+    wqc.wait()
+    qraw_ref[...] = nn(first, wq[...])
+    keys_out.pass_on(1)
+
+    def rope_head(h, carry):
+        lanes = pl.ds(pl.multiple_of(h * head, head), head)
+        raw = qraw_ref[:, lanes]
+        rot = turn(raw * row_norm(raw) * qg_ref[...], cos_ref[...], sin_ref[...]).astype(bf)
+        qrot_ref[h] = rot[:half]
+        qrot_ref[heads + h] = rot[half:]
+        return carry
+
+    lax.fori_loop(0, heads // 2, rope_head, 0)
+    keys_out.pass_on(2)
+    lax.fori_loop(heads // 2, heads, rope_head, 0)
+    keys_out.pass_on(3)
+    keys_out.arrive()
+    width = first.shape[1]
+    per = width // 8
+    own = pl.ds(pl.multiple_of((y * 2 + c) * rows, rows), rows)
+    for i in range(8):
+        csrc[i] = first_ref[own, i * per : (i + 1) * per]
+    blocks = Columns(csrc, cols_ref, psend, precv, tsend, trecv)
+    blocks.start()
+
+    scale = 1.0 / math.sqrt(head)
+
+    def attend(i, carry):
+        s = i // heads
+        h = i % heads
+        span = pl.ds(pl.multiple_of(s * half, half), half)
+        keys = kv_ref[s].reshape(8 * half, head)
+        vals = kv_ref[2 + s].reshape(8 * half, head)
+        scores = nt(qrot_ref[i], keys) * scale
+        allowed = qpos_ref[span, :1] >= kpos_ref[pl.ds(s, 1), :]
+        scores = jnp.where(allowed, scores, -1e9)
+        top = jnp.max(scores, axis=1, keepdims=True)
+        weights = jnp.exp(scores - top)
+        total = jnp.sum(weights, axis=1, keepdims=True)
+        probs = (weights / total).astype(bf)
+        att_ref[span, pl.ds(pl.multiple_of(h * head, head), head)] = nn(probs, vals).astype(bf)
+        log_ref[i] = jnp.broadcast_to(top + jnp.log(total), (half, head))
+        return carry
+
+    lax.fori_loop(0, heads, attend, 0)
+    blocks.exchange()
+    lax.fori_loop(heads, 2 * heads, attend, 0)
+    blocks.forward()
+    woc.wait()
+
+    def at(yy, cc):
+        return part.at[pl.ds(pl.multiple_of((yy * 2 + cc) * rows, rows), rows)]
+
+    def project(yy):
+        span = pl.ds(pl.multiple_of(yy * 2 * rows, 2 * rows), 2 * rows)
+        part[span] = nn(att_ref[span], wo[...]).astype(bf)
+
     def ccopy(yy):
-        return pltpu.make_async_remote_copy(src_ref=at(yy,1-c),dst_ref=cbuf.at[yy],send_sem=csend.at[yy],recv_sem=crecv.at[yy],device_id=dev(z,x,y,1-c),device_id_type=MESH)
-    ccopy(1-y).start(); ccopy(y).start()
-    ccopy(1-y).wait_recv()
-    stage[...]=(at(1-y,c)[...].astype(f32)+cbuf[1-y].astype(f32)).astype(stage.dtype)
-    yc=pltpu.make_async_remote_copy(src_ref=stage,dst_ref=ybuf,send_sem=ysend,recv_sem=yrecv,device_id=dev(z,x,1-y,c),device_id_type=MESH)
+        return pltpu.make_async_remote_copy(
+            src_ref=at(yy, 1 - c), dst_ref=cbuf.at[yy], send_sem=csend.at[yy],
+            recv_sem=crecv.at[yy], device_id=C, device_id_type=MESH)
+
+    project(1 - y)
+    ccopy(1 - y).start()
+    project(y)
+    ccopy(y).start()
+    ccopy(1 - y).wait_recv()
+    stage[...] = (at(1 - y, c)[...].astype(f32) + cbuf[1 - y].astype(f32)).astype(bf)
+    yc = pltpu.make_async_remote_copy(
+        src_ref=stage, dst_ref=ybuf, send_sem=ysend, recv_sem=yrecv, device_id=Y, device_id_type=MESH)
     yc.start()
     ccopy(y).wait_recv()
-    out_ref[...]=at(y,c)[...].astype(f32)+cbuf[y].astype(f32)
+    res = x_ref[own].astype(f32) + (at(y, c)[...].astype(f32) + cbuf[y].astype(f32))
+    lane = lax.broadcasted_iota(jnp.int32, (rows, 4 * experts), 1)
+    named = jnp.zeros((rows, 4 * experts), jnp.bool_)
+    routes = routes_ref[...]
+    for k in range(routes.shape[1]):
+        named = named | (lane % experts == routes[:, k : k + 1])
     yc.wait_recv()
-    out_ref[...]+=ybuf[...].astype(f32)
-    yc.wait_send(); ccopy(0).wait_send(); ccopy(1).wait_send()
-
-def rstp(part,cid=4):
-    n,w=part.shape; rows=n//4
-    S=pltpu.SemaphoreType.DMA
-    return pl.pallas_call(rstp_kernel,out_shape=jax.ShapeDtypeStruct((rows,w),jnp.float32),
-        in_specs=[pl.BlockSpec(memory_space=pltpu.VMEM)],out_specs=pl.BlockSpec(memory_space=pltpu.VMEM),
-        scratch_shapes=[pltpu.VMEM((2,rows,w),part.dtype),pltpu.VMEM((rows,w),part.dtype),pltpu.VMEM((rows,w),part.dtype),S((2,)),S((2,)),S,S],
-        compiler_params=pltpu.CompilerParams(collective_id=cid,has_side_effects=True,vmem_limit_bytes=32*2**20))(part)
-
-def agtp_kernel(x_ref,out_ref,lsem,send,recv):
-    rows=x_ref.shape[0]
-    z,x,y,c=coords()
-    barrier_tp()
-    def at(yy,cc): return out_ref.at[pl.ds(pl.multiple_of((yy*2+cc)*rows,rows),rows)]
-    def cp(src,yy,cc,d,k):
-        return pltpu.make_async_remote_copy(src_ref=src,dst_ref=at(yy,cc),send_sem=send.at[k],recv_sem=recv.at[yy*2+cc],device_id=d,device_id_type=MESH)
-    Y,C=dev(z,x,1-y,c),dev(z,x,y,1-c)
-    loc=pltpu.make_async_copy(x_ref,at(y,c),lsem); loc.start()
-    cp(x_ref,y,c,Y,0).start(); cp(x_ref,y,c,C,1).start()
-    cp(x_ref,1-y,c,Y,0).wait_recv()
-    cp(at(1-y,c),1-y,c,C,2).start()
-    cp(x_ref,y,1-c,C,1).wait_recv(); cp(x_ref,1-y,1-c,C,2).wait_recv()
-    loc.wait()
-    cp(x_ref,y,c,Y,0).wait_send(); cp(x_ref,y,c,C,1).wait_send(); cp(at(1-y,c),1-y,c,C,2).wait_send()
-
-def agtp(piece,cid=5):
-    rows,w=piece.shape
-    S=pltpu.SemaphoreType.DMA
-    return pl.pallas_call(agtp_kernel,out_shape=jax.ShapeDtypeStruct((rows*4,w),piece.dtype),
-        in_specs=[pl.BlockSpec(memory_space=pl.ANY)],out_specs=pl.BlockSpec(memory_space=pl.ANY),
-        scratch_shapes=[S,S((3,)),S((4,))],
-        compiler_params=pltpu.CompilerParams(collective_id=cid,has_side_effects=True))(piece)
-
-
-def finish_kernel(a_ref,b_ref,v_ref,ao_ref,bo_ref,vo_ref,vbuf,part,tbuf,lsem,send,recv,vsend,vrecv,tsend,trecv):
-    rows=a_ref.shape[0]; vr=vo_ref.shape[0]
-    z,x,y,c=coords()
-    ctx=lax.axis_index("ctx"); tp=lax.axis_index("tp")
-    b=pltpu.get_barrier_semaphore()
-    Y,C,D=dev(z,x,1-y,c),dev(z,x,y,1-c),dev(z,x,1-y,1-c)
-    peers=[((ctx+i)%8,tp) for i in range(1,8)]+[Y,C,D]
-    for d in peers: pl.semaphore_signal(b,inc=1,device_id=d,device_id_type=MESH)
-    pl.semaphore_wait(b,10)
+    res = res + ybuf[...].astype(f32)
+    res_ref[...] = res
+    second = (res * row_norm(res) * g2_ref[...]).astype(bf)
+    piece_ref[:, :width] = second
+    logits = nt(second, wr_ref[...])
+    masked = jnp.where(named & (lane < 2 * experts), logits, -1e30)
+    top = jnp.max(masked, axis=1, keepdims=True)
+    weights = jnp.where(named & (lane < 2 * experts), jnp.exp(masked - top), 0.0)
+    total = jnp.sum(jnp.where(lane < experts, weights, 0.0), axis=1, keepdims=True)
+    gates = weights / total
+    high = gates.astype(bf)
+    low = (gates - high.astype(f32)).astype(bf)
+    gates_ref[...] = jnp.where(lane < experts, gates, 0.0)
+    piece_ref[:, width:] = jnp.where(lane < experts, high, low)
+
+    yc.wait_send()
+    ccopy(0).wait_send()
+    ccopy(1).wait_send()
+    blocks.finish()
+    keys_out.finish()
+
+
+def front(x, g1, wq, wk, wv, qg, kg, cos, sin, qpos, kpos, wo, g2, wr, routes, cid):
+    tok, width = x.shape
+    head = qg.shape[1]
+    cols = wq.shape[1]
+    heads = cols // head
+    rows, half = tok // 4, tok // 2
+    f32, bf = jnp.float32, jnp.bfloat16
+    dma = pltpu.SemaphoreType.DMA
+    vm, anywhere = pl.BlockSpec(memory_space=pltpu.VMEM), pl.BlockSpec(memory_space=pl.ANY)
+
+    def out(shape, kind):
+        return jax.ShapeDtypeStruct(shape, kind)
+
+    return pl.pallas_call(
+        front_kernel,
+        in_specs=[vm, vm, anywhere] + [vm] * 8 + [anywhere] + [vm] * 3,
+        out_specs=[vm] * 11,
+        out_shape=[
+            out((tok, width), bf), out((tok, cols), f32), out((tok, head), f32),
+            out((2 * heads, half, head), bf), out((4, 8, half, head), bf), out((tok, cols), bf),
+            out((2 * heads, half, head), f32), out((rows, width), f32), out((rows, 128), f32),
+            out((rows, width + 128), bf), out((8, 4, rows, width // 8), bf),
+        ],
+        scratch_shapes=[
+            pltpu.VMEM((width, cols), bf), pltpu.VMEM((cols, width), bf), pltpu.VMEM((tok, width), bf),
+            pltpu.VMEM((2, rows, width), bf), pltpu.VMEM((rows, width), bf), pltpu.VMEM((rows, width), bf),
+            pltpu.VMEM((8, rows, width // 8), bf),
+            dma((2,)), dma((3, 8)), dma((8,)), dma((2,)), dma((2,)), dma, dma,
+            dma((8,)), dma((8,)), dma((3,)), dma((4,)),
+        ],
+        compiler_params=pltpu.CompilerParams(
+            collective_id=cid, has_side_effects=True, vmem_limit_bytes=52 * 2**20
+        ),
+        name="front",
+    )(x, g1, wq, wk, wv, qg, kg, cos, sin, qpos, kpos, wo, g2, wr, routes)
+
+
+def middle_kernel(
+    sums_ref, res_ref, gates_ref, cot_ref, g2_ref, wr_ref, wo_ref, qrot_ref, kv_ref, log_ref,
+    qraw_ref, qg_ref, cos_ref, sin_ref, qpos_ref, kpos_ref,
+    layer_ref, gres_ref, gn2_ref, cols_ref, qlow_ref, dkv_ref, qgain_ref,
+    wo, back, mixed, dk, dv, csrc, wsem, send, recv, psend, precv, tsend, trecv,
+):
+    f32, bf = jnp.float32, jnp.bfloat16
+    z, x, y, c = coords()
+    rows, width = res_ref.shape
+    experts = wr_ref.shape[0] // 4
+    head = qg_ref.shape[1]
+    heads = qraw_ref.shape[1] // head
+    half = qraw_ref.shape[0] // 2
+    woc = pltpu.make_async_copy(wo_ref, wo, wsem)
+    woc.start()
+    barrier_wide()
+    Y, C = dev(z, x, 1 - y, c), dev(z, x, y, 1 - c)
+
+    def at(yy, cc):
+        return back.at[pl.ds(pl.multiple_of((yy * 2 + cc) * rows, rows), rows)]
+
+    res = res_ref[...]
+    layer_ref[...] = (res + sums_ref[:, :width]).astype(bf)
+    gates = gates_ref[...]
+    pair = sums_ref[:, 2 * width :]
+    glog = (gates * (pair - jnp.sum(gates * pair, axis=1, keepdims=True))).astype(bf)
+    gsec = sums_ref[:, width : 2 * width] + nn(glog, wr_ref[...])
+    rs = row_norm(res)
+    unit = res * rs
+    gn2_ref[...] = jnp.sum(gsec * unit, axis=0, keepdims=True)
+    cg = gsec * g2_ref[...]
+    gres = cot_ref[...].astype(f32) + rs * (cg - unit * jnp.mean(cg * unit, axis=1, keepdims=True))
+    gres_ref[...] = gres
+    mine = pl.ds(pl.multiple_of((y * 2 + c) * rows, rows), rows)
+    glow = gres.astype(bf)
+    back[mine] = glow
+
+    def cp(yy, cc, to, k):
+        return pltpu.make_async_remote_copy(
+            src_ref=at(yy, cc), dst_ref=at(yy, cc), send_sem=send.at[k],
+            recv_sem=recv.at[yy * 2 + cc], device_id=to, device_id_type=MESH)
+
+    cp(y, c, Y, 0).start()
+    cp(y, c, C, 1).start()
+    per = width // 8
+    for i in range(8):
+        csrc[i, :, :per] = glow[:, i * per : (i + 1) * per]
+        csrc[i, :, per:] = glog
+    blocks = Columns(csrc, cols_ref, psend, precv, tsend, trecv)
+    blocks.start()
+    dk[...] = jnp.zeros_like(dk)
+    dv[...] = jnp.zeros_like(dv)
+    qgain_ref[...] = jnp.zeros_like(qgain_ref)
+    woc.wait()
+
+    def mix(yy):
+        span = pl.ds(pl.multiple_of(yy * 2 * rows, 2 * rows), 2 * rows)
+        mixed[span] = nt(back[span], wo[...]).astype(bf)
+
+    cp(y, 1 - c, C, 1).wait_recv()
+    mix(y)
+    cp(1 - y, c, Y, 0).wait_recv()
+    cp(1 - y, c, C, 2).start()
+    cp(1 - y, 1 - c, C, 2).wait_recv()
+    mix(1 - y)
+    scale = 1.0 / math.sqrt(head)
+
+    def attend(i, carry):
+        s = i // heads
+        h = i % heads
+        span = pl.ds(pl.multiple_of(s * half, half), half)
+        lanes = pl.ds(pl.multiple_of(h * head, head), head)
+        keys = kv_ref[s].reshape(8 * half, head)
+        vals = kv_ref[2 + s].reshape(8 * half, head)
+        query = qrot_ref[i]
+        grad = mixed[span, lanes]
+        scores = nt(query, keys) * scale
+        allowed = qpos_ref[span, :1] >= kpos_ref[pl.ds(s, 1), :]
+        probs = jnp.where(allowed, jnp.exp(scores - log_ref[i][:, :1]), 0.0)
+        gprobs = nt(grad, vals)
+        inner = jnp.sum(probs * gprobs, axis=1, keepdims=True)
+        dots = (probs * (gprobs - inner) * scale).astype(bf)
+        dk[s] += tn(dots, query)
+        dv[s] += tn(probs.astype(bf), grad)
+        drot = nn(dots, keys)
+        raw = qraw_ref[span, lanes]
+        dn = turn_back(drot, cos_ref[span], sin_ref[span])
+        rs = row_norm(raw)
+        unit = raw * rs
+        qgain_ref[...] += jnp.sum((dn * unit).reshape(half // 8, 8, head), axis=0)
+        cg = dn * qg_ref[...]
+        qlow_ref[span, lanes] = (rs * (cg - unit * jnp.mean(cg * unit, axis=1, keepdims=True))).astype(bf)
+        return carry
+
+    lax.fori_loop(0, heads, attend, 0)
+    blocks.exchange()
+    lax.fori_loop(heads, 3 * heads // 2, attend, 0)
+    blocks.forward()
+    lax.fori_loop(3 * heads // 2, 2 * heads, attend, 0)
+    for s in range(2):
+        dkv_ref[s] = dk[s].astype(bf).reshape(8, half, head)
+        dkv_ref[2 + s] = dv[s].astype(bf).reshape(8, half, head)
+    cp(y, c, Y, 0).wait_send()
+    cp(y, c, C, 1).wait_send()
+    cp(1 - y, c, C, 2).wait_send()
+    blocks.finish()
+
+
+def middle(sums, res, gates, cot, g2, wr, wo, qrot, kv, logs, qraw, qg, cos, sin, qpos, kpos, cid):
+    rows, width = res.shape
+    tok, cols = qraw.shape
+    head = qg.shape[1]
+    half = tok // 2
+    f32, bf = jnp.float32, jnp.bfloat16
+    dma = pltpu.SemaphoreType.DMA
+    vm, anywhere = pl.BlockSpec(memory_space=pltpu.VMEM), pl.BlockSpec(memory_space=pl.ANY)
+
+    def out(shape, kind):
+        return jax.ShapeDtypeStruct(shape, kind)
+
+    return pl.pallas_call(
+        middle_kernel,
+        in_specs=[vm] * 6 + [anywhere] + [vm] * 9,
+        out_specs=[vm] * 7,
+        out_shape=[
+            out((rows, width), bf), out((rows, width), f32), out((1, width), f32),
+            out((8, 4, rows, width // 8 + 128), bf), out((tok, cols), bf), out((4, 8, half, head), bf),
+            out((8, head), f32),
+        ],
+        scratch_shapes=[
+            pltpu.VMEM((cols, width), bf), pltpu.VMEM((tok, width), bf), pltpu.VMEM((tok, cols), bf),
+            pltpu.VMEM((2, 8 * half, head), f32), pltpu.VMEM((2, 8 * half, head), f32),
+            pltpu.VMEM((8, rows, width // 8 + 128), bf),
+            dma, dma((3,)), dma((4,)), dma((8,)), dma((8,)), dma((3,)), dma((4,)),
+        ],
+        compiler_params=pltpu.CompilerParams(
+            collective_id=cid, has_side_effects=True, vmem_limit_bytes=52 * 2**20
+        ),
+        name="middle",
+    )(sums, res, gates, cot, g2, wr, wo, qrot, kv, logs, qraw, qg, cos, sin, qpos, kpos)
+
+
+def tail_kernel(
+    dkv_ref, qlow_ref, kraw_ref, kg_ref, cos_ref, sin_ref, wq_ref, wk_ref, wv_ref, x_ref, g1_ref,
+    gres_ref, layer_ref, vec_ref,
+    gin_ref, lout_ref, kvall_ref, qall_ref, vo_ref,
+    wq, xbuf, zbuf, zst, part, cbuf, ybuf, stage, vbuf, vpart, tbuf, gin, kvlow,
+    wsem, xsend, xrecv, zsend, zrecv, csend, crecv, ysend, yrecv, send, recv, vsend, vrecv, tsend, trecv,
+    lsem, qsend, qrecv, ksend, krecv,
+):
+    f32, bf = jnp.float32, jnp.bfloat16
+    z, x, y, c = coords()
+    ctx, tp = lax.axis_index("ctx"), lax.axis_index("tp")
+    rows, width = gres_ref.shape
+    half, head = dkv_ref.shape[2:]
+    wqc = pltpu.make_async_copy(wq_ref, wq, wsem.at[0])
+    wqc.start()
+    X, Y, C, D = dev(z, 1 - x, y, c), dev(z, x, 1 - y, c), dev(z, x, y, 1 - c), dev(z, x, 1 - y, 1 - c)
+    up, down = dev(z + 1, x, y, c), dev(z - 1, x, y, c)
+    barrier_wide()
+
+    def xcopy(zz):
+        return pltpu.make_async_remote_copy(
+            src_ref=dkv_ref.at[:, zz * 2 + 1 - x], dst_ref=xbuf.at[zz], send_sem=xsend.at[zz],
+            recv_sem=xrecv.at[zz], device_id=X, device_id_type=MESH)
+
+    def zcopy(zz, to, slot):
+        return pltpu.make_async_remote_copy(
+            src_ref=zst.at[zz], dst_ref=zbuf.at[slot], send_sem=zsend.at[zz],
+            recv_sem=zrecv.at[slot], device_id=to, device_id_type=MESH)
+
+    tok = qlow_ref.shape[0]
+    queries = Spread(
+        lambda p: qall_ref.at[pl.ds(pl.multiple_of(p * tok, tok), tok)], qsend, qrecv, qlow_ref)
+    keys = Spread(
+        lambda p: kvall_ref.at[pl.ds(pl.multiple_of(p * tok, tok), tok)], ksend, krecv, kvlow)
+    mine = [
+        pltpu.make_async_copy(s.first, s.place(s.me), lsem.at[n]) for n, s in enumerate((queries, keys))
+    ]
+    for k in range(4):
+        xcopy(far_z(z, k)).start()
+    queries.start_x()
+    mine[0].start()
+
+    def sum_z(k):
+        zz = far_z(z, k)
+        xcopy(zz).wait_recv()
+        total = dkv_ref[:, zz * 2 + x].astype(f32) + xbuf[zz].astype(f32)
+        zst[zz] = total.astype(bf)
+
+        @pl.when((zz > z) & (z > 0))
+        def _():
+            zcopy(zz, up, zz).wait_recv()
+            zst[zz] = (zst[zz].astype(f32) + zbuf[zz].astype(f32)).astype(bf)
+
+        @pl.when((zz < z) & (z < 3))
+        def _():
+            zcopy(zz, down, zz).wait_recv()
+            zst[zz] = (zst[zz].astype(f32) + zbuf[zz].astype(f32)).astype(bf)
+
+        @pl.when(zz > z)
+        def _():
+            zcopy(zz, up, zz).start()
+
+        @pl.when((zz < z) & (zz != z - 1))
+        def _():
+            zcopy(zz, down, zz).start()
+
+        @pl.when(zz == z - 1)
+        def _():
+            zcopy(zz, down, 4).start()
+
+    def at(yy, cc):
+        return part.at[pl.ds(pl.multiple_of((yy * 2 + cc) * rows, rows), rows)]
+
+    def two(yy):
+        return pl.ds(pl.multiple_of(yy * 2 * rows, 2 * rows), 2 * rows)
+
+    sum_z(0)
+    wqc.wait()
+    first_a = nt(qlow_ref[two(1 - y)], wq[...])
+    sum_z(1)
+    first_b = nt(qlow_ref[two(y)], wq[...])
+    sum_z(2)
+    queries.start_z()
+    xcopy(z).wait_recv()
+    dkv = dkv_ref[:, ctx].astype(f32) + xbuf[z].astype(f32)
+
+    @pl.when(z > 0)
+    def _():
+        zcopy(z, up, z).wait_recv()
+
+    @pl.when(z == 0)
+    def _():
+        zbuf[0] = jnp.zeros_like(zbuf[0])
+
+    @pl.when(z < 3)
+    def _():
+        zcopy(z, down, 4).wait_recv()
+
+    @pl.when(z == 3)
+    def _():
+        zbuf[4] = jnp.zeros_like(zbuf[4])
+
+    dkv = dkv + zbuf[z].astype(f32) + zbuf[4].astype(f32)
+    dkey = jnp.concatenate([dkv[0], dkv[1]], axis=0)
+    vlow = jnp.concatenate([dkv[2], dkv[3]], axis=0).astype(bf)
+    raw = kraw_ref[...]
+    dn = turn_back(dkey, cos_ref[...], sin_ref[...])
+    rs = row_norm(raw)
+    unit = raw * rs
+    kgain = jnp.sum(dn * unit, axis=0, keepdims=True)
+    cg = dn * kg_ref[...]
+    klow = (rs * (cg - unit * jnp.mean(cg * unit, axis=1, keepdims=True))).astype(bf)
+    kvlow[:, :head] = klow
+    kvlow[:, head:] = vlow
+    keys.start_z()
+    keys.start_x()
+    mine[1].start()
+
+    def ccopy(yy):
+        return pltpu.make_async_remote_copy(
+            src_ref=at(yy, 1 - c), dst_ref=cbuf.at[yy], send_sem=csend.at[yy],
+            recv_sem=crecv.at[yy], device_id=C, device_id_type=MESH)
+
+    def project(yy, first):
+        keys, vals = kvlow[two(yy), :head], kvlow[two(yy), head:]
+        part[two(yy)] = (first + nt(keys, wk_ref[...]) + nt(vals, wv_ref[...])).astype(bf)
+        ccopy(yy).start()
+
+    project(1 - y, first_a)
+    project(y, first_b)
+    ccopy(1 - y).wait_recv()
+    stage[...] = (at(1 - y, c)[...].astype(f32) + cbuf[1 - y].astype(f32)).astype(bf)
+    yc = pltpu.make_async_remote_copy(
+        src_ref=stage, dst_ref=ybuf, send_sem=ysend, recv_sem=yrecv, device_id=Y, device_id_type=MESH)
+    yc.start()
+    queries.pass_on(1)
+    ccopy(y).wait_recv()
+    gfirst = at(y, c)[...].astype(f32) + cbuf[y].astype(f32)
+    own = pl.ds(pl.multiple_of((y * 2 + c) * rows, rows), rows)
+    value = x_ref[own].astype(f32)
+    rs = row_norm(value)
+    unit = value * rs
+    yc.wait_recv()
+    gfirst = gfirst + ybuf[...].astype(f32)
+    gn1 = jnp.sum(gfirst * unit, axis=0, keepdims=True)
+    cg = gfirst * g1_ref[...]
+    gin[...] = (gres_ref[...] + rs * (cg - unit * jnp.mean(cg * unit, axis=1, keepdims=True))).astype(bf)
+
+    keys.pass_on(1)
+    pairs = [(gin, gin_ref), (layer_ref, lout_ref)]
+
+    def place(ref, yy, cc):
+        return ref.at[pl.ds(pl.multiple_of((yy * 2 + cc) * rows, rows), rows)]
+
+    def cp(n, src, yy, cc, to, k):
+        return pltpu.make_async_remote_copy(
+            src_ref=src, dst_ref=place(pairs[n][1], yy, cc), send_sem=send.at[n, k],
+            recv_sem=recv.at[n, yy * 2 + cc], device_id=to, device_id_type=MESH)
+
+    for n, (src, dst) in enumerate(pairs):
+        cp(n, src, y, c, Y, 0).start()
+        cp(n, src, y, c, C, 1).start()
+        dst[own] = src[...]
+    per = width // 8
+    for i in range(8):
+        for j in range(per // 128):
+            lo = i * per + j * 128
+            vpart[i, j : j + 1] = gn1[:, lo : lo + 128]
+        vpart[i, per // 128 : 8] = vec_ref[i, per // 128 : 8]
+        vpart[i, 7:8] = jnp.broadcast_to(kgain, (1, head))
+
     def vcopy(i):
-        to=(ctx+i)%8
-        return pltpu.make_async_remote_copy(src_ref=v_ref.at[pl.ds(pl.multiple_of(to*vr,vr),vr)],dst_ref=vbuf.at[i],send_sem=vsend.at[i],recv_sem=vrecv.at[i],device_id=(to,tp),device_id_type=MESH)
-    for i in range(1,8): vcopy(i).start()
-    def at(o,yy,cc): return o.at[pl.ds(pl.multiple_of((yy*2+cc)*rows,rows),rows)]
-    pairs=[(a_ref,ao_ref),(b_ref,bo_ref)]
-    def cp(n,src,yy,cc,d,k):
-        return pltpu.make_async_remote_copy(src_ref=src,dst_ref=at(pairs[n][1],yy,cc),send_sem=send.at[n,k],recv_sem=recv.at[n,yy*2+cc],device_id=d,device_id_type=MESH)
-    locs=[]
-    for n,(s,o) in enumerate(pairs):
-        l=pltpu.make_async_copy(s,at(o,y,c),lsem.at[n]); l.start(); locs.append(l)
-        cp(n,s,y,c,Y,0).start(); cp(n,s,y,c,C,1).start()
-    total=v_ref[pl.ds(pl.multiple_of(ctx*vr,vr),vr)]
-    for i in range(1,8):
+        to = (ctx + i) % 8
+        return pltpu.make_async_remote_copy(
+            src_ref=vpart.at[to], dst_ref=vbuf.at[i], send_sem=vsend.at[i], recv_sem=vrecv.at[i],
+            device_id=(to, tp), device_id_type=MESH)
+
+    for i in range(1, 8):
+        vcopy(i).start()
+    queries.pass_on(2)
+    keys.pass_on(2)
+    total = vpart[ctx]
+    for i in range(1, 8):
         vcopy(i).wait_recv()
-        total=total+vbuf[i]
-    part[...]=total
-    def tcopy(k,d):
-        return pltpu.make_async_remote_copy(src_ref=part,dst_ref=tbuf.at[k],send_sem=tsend.at[k],recv_sem=trecv.at[k],device_id=d,device_id_type=MESH)
-    ts=[tcopy(k,d) for k,d in enumerate((Y,C,D))]
-    for t in ts: t.start()
-    for n,(s,o) in enumerate(pairs):
-        cp(n,s,1-y,c,Y,0).wait_recv()
-        cp(n,at(o,1-y,c),1-y,c,C,2).start()
-    for t in ts: t.wait_recv()
-    vo_ref[...]=(part[...]+tbuf[0])+(tbuf[1]+tbuf[2])
-    for n,(s,o) in enumerate(pairs):
-        cp(n,s,y,1-c,C,1).wait_recv(); cp(n,s,1-y,1-c,C,2).wait_recv()
-        locs[n].wait()
-        cp(n,s,y,c,Y,0).wait_send(); cp(n,s,y,c,C,1).wait_send(); cp(n,at(o,1-y,c),1-y,c,C,2).wait_send()
-    for t in ts: t.wait_send()
-    for i in range(1,8): vcopy(i).wait_send()
-
-def finish(a,b,v,cid):
-    rows,w=a.shape; vr=v.shape[0]//8
-    S=pltpu.SemaphoreType.DMA
-    any_=pl.BlockSpec(memory_space=pl.ANY); vm=pl.BlockSpec(memory_space=pltpu.VMEM)
-    return pl.pallas_call(finish_kernel,out_shape=[jax.ShapeDtypeStruct((rows*4,w),a.dtype),jax.ShapeDtypeStruct((rows*4,w),a.dtype),jax.ShapeDtypeStruct((vr,128),jnp.float32)],
-        in_specs=[any_,any_,vm],out_specs=[any_,any_,vm],
-        scratch_shapes=[pltpu.VMEM((8,vr,128),jnp.float32),pltpu.VMEM((vr,128),jnp.float32),pltpu.VMEM((3,vr,128),jnp.float32),S((2,)),S((2,3)),S((2,4)),S((8,)),S((8,)),S((3,)),S((3,))],
-        compiler_params=pltpu.CompilerParams(collective_id=cid,has_side_effects=True))(a,b,v)
+        total = total + vbuf[i]
+    tbuf[3] = total
+
+    def tcopy(k, to):
+        return pltpu.make_async_remote_copy(
+            src_ref=tbuf.at[3], dst_ref=tbuf.at[k], send_sem=tsend.at[k], recv_sem=trecv.at[k],
+            device_id=to, device_id_type=MESH)
+
+    sums = [tcopy(k, to) for k, to in enumerate((Y, C, D))]
+    for t in sums:
+        t.start()
+    for n, (src, dst) in enumerate(pairs):
+        cp(n, src, 1 - y, c, Y, 0).wait_recv()
+        cp(n, place(dst, 1 - y, c), 1 - y, c, C, 2).start()
+    keys.pass_on(3)
+    queries.pass_on(3)
+    for t in sums:
+        t.wait_recv()
+    vo_ref[...] = (tbuf[3] + tbuf[0]) + (tbuf[1] + tbuf[2])
+    for n, (src, dst) in enumerate(pairs):
+        cp(n, src, y, 1 - c, C, 1).wait_recv()
+        cp(n, src, 1 - y, 1 - c, C, 2).wait_recv()
+        cp(n, src, y, c, Y, 0).wait_send()
+        cp(n, src, y, c, C, 1).wait_send()
+        cp(n, place(dst, 1 - y, c), 1 - y, c, C, 2).wait_send()
+    for t in sums:
+        t.wait_send()
+    for i in range(1, 8):
+        vcopy(i).wait_send()
+    for s in (keys, queries):
+        s.arrive()
+        s.finish()
+    for cp_own in mine:
+        cp_own.wait()
+    yc.wait_send()
+    ccopy(0).wait_send()
+    ccopy(1).wait_send()
+    for zz in range(4):
+        xcopy(zz).wait_send()
+
+        @pl.when(zz != z)
+        def _():
+            zcopy(zz, up, zz).wait_send()
+
+
+def tail(dkv, qlow, kraw, kg, cos, sin, wq, wk, wv, x, g1, gres, layer, vec, cid):
+    tok, width = x.shape
+    rows = gres.shape[0]
+    half, head = dkv.shape[2:]
+    f32, bf = jnp.float32, jnp.bfloat16
+    dma = pltpu.SemaphoreType.DMA
+    vm, anywhere = pl.BlockSpec(memory_space=pltpu.VMEM), pl.BlockSpec(memory_space=pl.ANY)
+
+    def out(shape, kind):
+        return jax.ShapeDtypeStruct(shape, kind)
+
+    def mem(*shape, kind=bf):
+        return pltpu.VMEM(shape, kind)
+
+    return pl.pallas_call(
+        tail_kernel,
+        in_specs=[vm] * 6 + [anywhere] + [vm] * 7,
+        out_specs=[vm] * 2 + [anywhere] * 2 + [vm],
+        out_shape=[
+            out((tok, width), bf), out((tok, width), bf), out((8 * tok, 2 * head), bf),
+            out((8 * tok, qlow.shape[1]), bf), out((8, 128), f32),
+        ],
+        scratch_shapes=[
+            mem(*wq.shape), mem(4, 4, half, head), mem(5, 4, half, head), mem(4, 4, half, head),
+            mem(tok, width), mem(2, rows, width), mem(rows, width), mem(rows, width),
+            mem(8, 8, 128, kind=f32), mem(8, 8, 128, kind=f32), mem(4, 8, 128, kind=f32), mem(rows, width),
+            mem(tok, 2 * head),
+            dma((1,)), dma((4,)), dma((4,)), dma((4,)), dma((5,)), dma((2,)), dma((2,)), dma, dma,
+            dma((2, 3)), dma((2, 4)), dma((8,)), dma((8,)), dma((3,)), dma((3,)),
+            dma((2,)), dma((3, 8)), dma((8,)), dma((3, 8)), dma((8,)),
+        ],
+        compiler_params=pltpu.CompilerParams(
+            collective_id=cid, has_side_effects=True, vmem_limit_bytes=52 * 2**20
+        ),
+        name="tail",
+    )(dkv, qlow, kraw, kg, cos, sin, wq, wk, wv, x, g1, gres, layer, vec)
 
 
 EPSILON = 1e-06
@@ -651,43 +1139,25 @@
 
 
 class Links:
-    def __init__(self, own):
-        self.own = own
-
-    def ag_all(self, piece, cid):
-        if self.own:
-            return ag32(piece, cid)
+    def ag_all(self, piece):
         return lax.all_gather(piece, ("ctx", "tp"), axis=0, tiled=True)
 
-    def rs_all(self, part, cid):
-        if self.own:
-            return reduce_all(part, cid)
+    def rs_all(self, part):
         return lax.psum_scatter(part, ("ctx", "tp"), scatter_dimension=0, tiled=True).astype(F32)
 
-    def ag_ctx(self, piece, cid):
-        if self.own:
-            return agctx(piece, cid)
+    def ag_ctx(self, piece):
         return lax.all_gather(piece, "ctx", axis=0, tiled=True)
 
-    def rs_ctx(self, part, cid):
-        if self.own:
-            return rsctx(part, cid)
+    def rs_ctx(self, part):
         return lax.psum_scatter(part, "ctx", scatter_dimension=0, tiled=True).astype(F32)
 
-    def rs_tp(self, part, cid):
-        if self.own:
-            return rstp(part, cid)
+    def rs_tp(self, part):
         return lax.psum_scatter(part, "tp", scatter_dimension=0, tiled=True).astype(F32)
 
-    def ag_tp(self, piece, cid):
-        if self.own:
-            return agtp(piece, cid)
+    def ag_tp(self, piece):
         return lax.all_gather(piece, "tp", axis=0, tiled=True)
 
-
-    def finish(self, a, b, vectors, cid):
-        if self.own:
-            return finish(a, b, vectors, cid)
+    def finish(self, a, b, vectors):
         total = lax.psum_scatter(vectors, "ctx", scatter_dimension=0, tiled=True)
         gathered = (lax.all_gather(v, "tp", axis=0, tiled=True) for v in (a, b))
         return (*gathered, lax.psum(total, "tp"))
@@ -792,7 +1262,7 @@
     return weights / jnp.sum(weights, axis=1, keepdims=True)
 
 
-def shards(
+def plain_shards(
     tokens_in,
     block_order,
     routes,
@@ -817,7 +1287,7 @@
     query_group_width = local_heads // local_kv
     seq_count = block_order.shape[0]
     devices, tp_size = lax.axis_size("ctx"), lax.axis_size("tp")
-    links = Links(devices == 8 and tp_size == 4)
+    links = Links()
     me, tp_me = lax.axis_index("ctx"), lax.axis_index("tp")
     rows = tok_count // tp_size
     block_len = tok_count // (2 * seq_count)
@@ -856,7 +1326,7 @@
     )
     kv_width = local_kv * head_size
     kv_own = jnp.concatenate([key_rot.astype(BF).reshape(tok_count, kv_width), value_rows], axis=1)
-    kv_all = links.ag_ctx(kv_own, 1)
+    kv_all = links.ag_ctx(kv_own)
     kv_seq = kv_all.reshape(devices, seq_count, 2 * block_len, 2, local_kv, head_size)
     kv_seq = kv_seq.transpose(3, 1, 0, 2, 4, 5).reshape(
         2, seq_count, devices * 2 * block_len, local_kv, head_size
@@ -867,7 +1337,7 @@
     )
     attended = attended_mix.reshape(tok_count, local_heads * head_size).astype(BF)
     attn_part = jnp.dot(attended, w_out, preferred_element_type=F32).astype(BF)
-    residual = own_rows(inputs) + links.rs_tp(attn_part, 2)
+    residual = own_rows(inputs) + links.rs_tp(attn_part)
     second_normed, second_back = jax.vjp(rms_norm, residual, norm2_gain)
     second_in = second_normed.astype(BF)
     extra = -(-2 * experts // 128) * 128
@@ -876,7 +1346,7 @@
     gates_low = (gates - gates_high.astype(F32)).astype(BF)
     pad = jnp.zeros((rows, extra - 2 * experts), BF)
     second_all = links.ag_all(
-        jnp.concatenate([second_in, gates_high, gates_low, pad], axis=1), 3
+        jnp.concatenate([second_in, gates_high, gates_low, pad], axis=1)
     )
     column = jnp.arange(extra, dtype=jnp.int32)[:, None]
     named = me * own_experts + jnp.arange(hid, dtype=jnp.int32)[None, :] // units
@@ -888,7 +1358,7 @@
     part, gate_low, up_low, hidden_low = expert_blocks(
         second_all, cot_all, gate_mat, up_mat, down_mat, spread, pick.T
     )
-    sums_own = links.rs_all(part, 6)
+    sums_own = links.rs_all(part)
     out_own = sums_own[:, :model_width]
     entry_own = sums_own[:, model_width:]
     gate_total = entry_own[:, model_width : model_width + experts]
@@ -900,7 +1370,7 @@
     grad_residual = cot_own.astype(F32) + grad_resid_norm
     pad = jnp.zeros((rows, -experts % 128), BF)
     back_all = links.ag_tp(
-        jnp.concatenate([grad_residual.astype(BF), grad_logits, pad], axis=1), 7
+        jnp.concatenate([grad_residual.astype(BF), grad_logits, pad], axis=1)
     )
     grad_attn_low = back_all[:, :model_width]
     second_own = lax.dynamic_slice(second_all, (me * tok_count, 0), (tok_count, model_width))
@@ -917,7 +1387,7 @@
     grad_kv = jnp.stack([grad_key_seq, grad_value_seq]).astype(BF)
     grad_kv = grad_kv.reshape(2, seq_count, devices, 2 * block_len, kv_width)
     grad_kv = grad_kv.transpose(2, 1, 3, 0, 4).reshape(all_tok, 2 * kv_width)
-    grad_kv_own = links.rs_ctx(grad_kv, 8)
+    grad_kv_own = links.rs_ctx(grad_kv)
     grad_query_rot = grad_query_seq.reshape(tok_count, local_heads, head_size)
     grad_key_rot = grad_kv_own[:, :kv_width].reshape(tok_count, local_kv, head_size)
     grad_query_raw, grad_key_raw, grad_qgain, grad_kgain = rope_back(
@@ -929,7 +1399,7 @@
     first_part = dotf(query_low, w_query, ((1,), (1,)))
     first_part = first_part + dotf(key_low, key_weight, ((1,), (1,)))
     first_part = first_part + dotf(value_low, value_weight, ((1,), (1,)))
-    grad_first = links.rs_tp(first_part.astype(BF), 9)
+    grad_first = links.rs_tp(first_part.astype(BF))
     grad_first, gate_low = lax.optimization_barrier((grad_first, gate_low))
     grads = expert_grads(second_all, cot_all, gate_low, up_low, hidden_low)
     grad_gate, grad_up = (
@@ -943,7 +1413,7 @@
 
     grad_query = over_ctx(dotf(first_in, query_low, ((0,), (0,))), 0)
     kv_part = dotf(first_in, jnp.concatenate([key_low, value_low], axis=1), ((0,), (0,)))
-    small = links.rs_ctx(jnp.concatenate([kv_part, router_part], axis=1).astype(BF), 11)
+    small = links.rs_ctx(jnp.concatenate([kv_part, router_part], axis=1).astype(BF))
     grad_key = small[:, :kv_width]
     grad_value = small[:, kv_width : 2 * kv_width]
     grad_router = small[:, 2 * kv_width : 2 * kv_width + experts]
@@ -955,7 +1425,7 @@
     pad = jnp.zeros((devices, -sum(sizes) % 1024), F32)
     packed = jnp.concatenate([*vectors, pad], axis=1).reshape(-1, 128)
     grad_input, layer_out, total = links.finish(
-        (grad_residual + grad_input_norm).astype(BF), (residual + out_own).astype(BF), packed, 10
+        (grad_residual + grad_input_norm).astype(BF), (residual + out_own).astype(BF), packed
     )
     total = total.reshape(-1)
 
@@ -974,6 +1444,131 @@
         piece_of(3),
         grad_out,
         piece_of(1),
+        grad_router,
+        grad_gate,
+        grad_up,
+        grad_down,
+    )
+
+
+def fast_shards(
+    tokens_in,
+    block_order,
+    routes,
+    norm1_gain,
+    w_query,
+    key_weight,
+    value_weight,
+    query_gain,
+    key_gain,
+    w_out,
+    norm2_gain,
+    w_router,
+    w_gate,
+    w_up,
+    w_down,
+    cotangent,
+):
+    tok_count, model_width = tokens_in.shape
+    head_size = query_gain.shape[0]
+    seq_count = block_order.shape[0]
+    devices, tp_size = lax.axis_size("ctx"), lax.axis_size("tp")
+    me, tp_me = lax.axis_index("ctx"), lax.axis_index("tp")
+    rows = tok_count // tp_size
+    block_len = tok_count // (2 * seq_count)
+    experts = w_router.shape[1]
+    own_experts, _, units = w_gate.shape
+    hid = own_experts * units
+
+    def own_rows(v):
+        return lax.dynamic_slice_in_dim(v, tp_me * rows, rows, axis=0)
+
+    def row(v):
+        return v.reshape(1, -1)
+
+    cot_own = own_rows(cotangent)
+    cot_all = lax.all_gather(cot_own, ("ctx", "tp"), axis=0, tiled=True)
+
+    token_positions = positions_of(block_order, devices, block_len)
+    query_pos = lax.dynamic_index_in_dim(token_positions, me, 0, keepdims=False).reshape(-1)
+    key_pos = jnp.transpose(token_positions, (1, 0, 2)).reshape(seq_count, -1).astype(F32)
+    angles = angles_of(query_pos, head_size)
+    cos = jnp.concatenate([jnp.cos(angles)] * 2, axis=1)
+    sin = jnp.concatenate([-jnp.sin(angles), jnp.sin(angles)], axis=1)
+    query_pos = jnp.broadcast_to(query_pos.astype(F32)[:, None], (tok_count, head_size))
+    router_rows = w_router.T
+    router_rows = jnp.concatenate([router_rows, router_rows, jnp.zeros((2 * experts, model_width), BF)])
+    _, query_raw, key_raw, query_rot, kv_all, attended, logs, residual, gates, piece, first_cols = front(
+        tokens_in, row(norm1_gain), w_query, key_weight, value_weight, row(query_gain),
+        row(key_gain), cos, sin, query_pos, key_pos, w_out, row(norm2_gain), router_rows,
+        own_rows(routes), 1,
+    )
+    second_all = ag32(piece, 3)
+    attended_all = lax.all_gather(attended, "ctx", axis=0, tiled=True)
+    all_tok = devices * tok_count
+    first_cols = first_cols.reshape(all_tok, -1)
+
+    extra = 4 * experts
+    column = jnp.arange(extra, dtype=jnp.int32)[:, None]
+    named = me * own_experts + jnp.arange(hid, dtype=jnp.int32)[None, :] // units
+    pick = (column == named).astype(BF)
+    spread = pick + (column == named + experts).astype(BF)
+    gate_mat = w_gate.transpose(0, 2, 1).reshape(hid, model_width)
+    up_mat = w_up.transpose(0, 2, 1).reshape(hid, model_width)
+    down_mat = w_down.reshape(hid, model_width)
+    part, gate_low, up_low, hidden_low = expert_blocks(
+        second_all, cot_all, gate_mat, up_mat, down_mat, spread, pick.T
+    )
+    sums_own = reduce_all(part, 6)
+    layer_piece, grad_residual, grad_norm2, back_cols, query_low, grad_kv, qgain_part = middle(
+        sums_own, residual, gates, cot_own, row(norm2_gain), router_rows, w_out, query_rot, kv_all,
+        logs, query_raw, row(query_gain), cos, sin, query_pos, key_pos, 7,
+    )
+
+    back_cols = back_cols.reshape(all_tok, -1)
+    width_part = model_width // devices
+    grad_out = dotf(attended_all, back_cols[:, :width_part], ((0,), (0,)))
+    second_cols = lax.dynamic_slice_in_dim(second_all, me * width_part, width_part, axis=1)
+    grad_router = dotf(second_cols, back_cols[:, width_part : width_part + experts], ((0,), (0,)))
+    per = model_width // devices // 128
+    vectors = jnp.concatenate(
+        [
+            jnp.zeros((devices, per, 128), F32),
+            grad_norm2.reshape(devices, per, 128),
+            jnp.broadcast_to(jnp.sum(qgain_part, axis=0), (devices, 1, 128)),
+            jnp.zeros((devices, 7 - 2 * per, 128), F32),
+        ],
+        axis=1,
+    )
+    grad_input, layer_out, kv_low_all, query_low_all, total = tail(
+        grad_kv, query_low, key_raw, row(key_gain), cos, sin, w_query, key_weight, value_weight,
+        tokens_in, row(norm1_gain), grad_residual, layer_piece, vectors, 8,
+    )
+    grad_query = dotf(first_cols, query_low_all, ((0,), (0,)))
+    kv_grads = dotf(first_cols, kv_low_all, ((0,), (0,)))
+    grad_key = kv_grads[:, :head_size]
+    grad_value = kv_grads[:, head_size:]
+    grads = expert_grads(second_all, cot_all, gate_low, up_low, hidden_low)
+    grad_gate, grad_up = (
+        v.reshape(own_experts, units, model_width).transpose(0, 2, 1) for v in grads[:2]
+    )
+    grad_down = grads[2].reshape(own_experts, units, model_width)
+    share = head_size // devices
+
+    def gain_of(n):
+        return lax.dynamic_slice_in_dim(total[n], me * share, share, axis=0)
+
+    return (
+        layer_out,
+        grad_input,
+        total[:per].reshape(-1),
+        grad_query,
+        grad_key,
+        grad_value,
+        gain_of(2 * per),
+        gain_of(7),
+        grad_out,
+        total[per : 2 * per].reshape(-1),
         grad_router,
         grad_gate,
         grad_up,
@@ -1016,4 +1611,6 @@
         P("ctx", None, "tp"),
         P("ctx", "tp", None),
     )
+    own = mesh.shape["ctx"] == 8 and mesh.shape["tp"] == 4
+    shards = fast_shards if own else plain_shards
     return jax.shard_map(shards, mesh=mesh, in_specs=in_specs, out_specs=out_specs, check_vma=False)

time: 520 us -> 444 us (0.85); the launches traced: 513 us -> 443 us
  Pallas kernels: 357 us -> 399 us
  matrix products: 51.3 us -> 10.8 us
  other arithmetic: 45.7 us -> 5.67 us
  local copies, waits for them, and re-layouts: 42.4 us -> 13.8 us
    dot_general x19 -> x0, matrix products: 34.1 us -> none  [the longest x2 8.47 us: attend_backward(): jnp.einsum('axfv,axfz->vxz', attention_probs.astype(BF), grad_attended_mi...]
    pallas_call x7 -> x3, Pallas kernels: 155 us -> 184 us  [the longest x1 80 us: tail(): pl.pallas_call(tail_kernel, in_specs=[vm] * 6 + [anywhere] + [vm] * 7, ou...]
    convert_element_type x11 -> x1, other arithmetic: 15.2 us -> 0.85 us  [fast_shards(): pick = (column == named).astype(BF)]
    pallas_call x1, Pallas kernels: 45.3 us -> 58.3 us  [ag32(): pl.pallas_call(ag32_kernel, out_shape=jax.ShapeDtypeStruct((rows * 32, w)...]
    reduce_sum x10 -> x1, other arithmetic: 8.41 us -> 0.02 us  [fast_shards(): jnp.sum(qgain_part, axis=0)]
    another operation x8 -> x0, other arithmetic: 7.54 us -> none
    dot_general x9 -> x4, matrix products: 17.1 us -> 10.8 us  [dotf(): return lax.dot_general(a, b, (dims, ((), ())), preferred_element_type=F32)]
    concatenate x5 -> x3, local copies, waits for them, and re-layouts: 5.7 us -> 0.16 us  [the longest x2 0.08 us: fast_shards(): jnp.concatenate([jnp.zeros((devices, per, 128), F32), grad_norm2.reshape(...]
  transfers between devices with their start and end apart: 3 -> 2, of which waited for: 0 -> 0; matrix products, arithmetic and copies ran while one was open for 23% -> 4% of each run, Pallas kernels for 42% -> 84%
where the time goes in v3:
time: 444 us; the launch traced here: 443 us
  Pallas kernels  399 us (90%)
  between operations  14.3 us (3%)
  local copies, waits for them, and re-layouts  13.8 us (3%)
  matrix products  10.8 us (2%)
  other arithmetic  5.67 us (1%)
    pallas_call x1, Pallas kernels, tail(): pl.pallas_call(tail_kernel, in_specs=[vm] * 6 + [anywhere] + [vm] * 7, ou...  80 us
    pallas_call x1, Pallas kernels, reduce_all(): pl.pallas_call(reduce_all_kernel, in_specs=[pl.BlockSpec(memory_space=pl....  78.5 us
    pallas_call x1, Pallas kernels, front(): pl.pallas_call(front_kernel, in_specs=[vm, vm, anywhere] + [vm] * 8 + [an...  64.7 us
    pallas_call x1, Pallas kernels, ag32(): pl.pallas_call(ag32_kernel, out_shape=jax.ShapeDtypeStruct((rows * 32, w)...  58.3 us
    pallas_call x1, Pallas kernels, expert_blocks(): pl.pallas_call(expert_kernel, grid=(n // block,), in_specs=[rows(wide), r...  51.4 us
    pallas_call x1, Pallas kernels, middle(): pl.pallas_call(middle_kernel, in_specs=[vm] * 6 + [anywhere] + [vm] * 9,...  38.8 us
    pallas_call x1, Pallas kernels, expert_grads(): pl.pallas_call(expert_grad_kernel, grid=(width // block, n // span), in_s...  26.8 us
    dot_general x4, matrix products, dotf(): return lax.dot_general(a, b, (dims, ((), ())), preferred_element_type=F32)  10.8 us
  transfers between devices with their start and end apart: 2, of which 0 were waited for; matrix products, arithmetic and copies ran while one was open for 4% of the time, Pallas kernels for 84%

profile of v3, /device:TPU:0, one launch (start us, length us, event | category | flops | bytes accessed | tf_op | source)
XLA Modules:
  0.0 443.2 jit_solution(14474829411534727116)
XLA Ops:
  7.2 1.2 copy-done
  8.4 0.7 constant_dynamic-slice_fusion.2.cot_ref
  10.9 0.8 constant_dynamic-slice_fusion.3
  12.6 1.9 maximum_maximum_fusion.wr_ref
  17.3 64.7 %front.1 = (bf16[256,2048]{1,0:T(8,128)(2,1)}, f32[256,1024]{1,0:T(8,128)}, f32[256,128]{1,0:T(8,128)S(1)}, bf16[16,128,128]{2,1,0:T(8,128)(2,1)S(1)}, bf16[4,8,...) custom-call(bf16[256,2048]{1,0:T(8,128)(2,1)} %x_ref.3, ...), custom_call_target="tpu_custom_call" | custom-call | tf_op jit(solution)/shard_map/front/pallas_call | solution.py:587
  82.0 0.8 copy-done.5
  82.8 0.7 copy-done.7
  83.6 58.3 %shard_map.263.x_ref = bf16[2048,2176]{1,0:T(8,128)(2,1)} custom-call(bf16[64,2176]{1,0:T(8,128)(2,1)} %copy-done.7), custom_call_target="tpu_custom_call" | custom-call | tf_op jit(solution)/shard_map/pallas_call | solution.py:95
  142.0 0.8 fusion.7.t_ref
  142.8 0.8 fusion.8.s_ref
  143.6 51.4 %experts.1 = (bf16[2048,4224]{1,0:T(8,128)(2,1)}, bf16[768,2048]{1,0:T(8,128)(2,1)}, bf16[768,2048]{1,0:T(8,128)(2,1)}, bf16[768,2048]{1,0:T(8,128)(2,1)}) custom-call(bf16[2048,2176]{1,0:T(8,128)(2,1)} %shard_map.263.x_ref, bf16[2048,2048]{1,0:T(8,128)(2,1)} %all-gather.3.cloned.1.call-done.cot_ref, bf16[768,2048]{1,0:T(8,128)(2,1)} %bitcast.69, ...), custom_call_target="tpu_custom_call" | custom-call | flops 38654705664 | bytes 41943040 | tf_op jit(solution)/shard_map/experts/pallas_call | solution.py:1081
  195.0 78.5 %reduce_all.1.sums_ref = f32[64,4224]{1,0:T(8,128)S(1)} custom-call(bf16[2048,4224]{1,0:T(8,128)(2,1)} %get-tuple-element.44.part_ref), custom_call_target="tpu_custom_call" | custom-call | tf_op jit(solution)/shard_map/reduce_all/pallas_call | solution.py:277
  273.6 1.0 copy-done.2
  274.6 38.8 %middle.1 = (bf16[64,2048]{1,0:T(8,128)(2,1)S(1)}, f32[64,2048]{1,0:T(8,128)S(1)}, f32[1,2048]{1,0:T(1,128)S(1)}, bf16[8,4,64,384]{3,2,1,0:T(8,128)(2,1)}, bf16[...) custom-call(f32[64,4224]{1,0:T(8,128)} %copy-done.2, ...), custom_call_target="tpu_custom_call" | custom-call | tf_op jit(solution)/shard_map/middle/pallas_call | solution.py:731
  313.4 0.8 copy-done.6
  314.3 80.0 %tail.1 = (bf16[256,2048]{1,0:T(8,128)(2,1)}, bf16[256,2048]{1,0:T(8,128)(2,1)}, bf16[2048,256]{1,0:T(8,128)(2,1)}, bf16[2048,1024]{1,0:T(8,128)(2,1)}, f32[8,128]{1,0:T(8,128)S(1)}) custom-call(bf16[4,8,128,128]{3,2,1,0:T(8,128)(2,1)} %get-tuple-element.51.dkv_ref, bf16[256,1024]{1,0:T(8,128)(2,1)S(1)} %get-tuple-element.52.qlow_ref, ...), custom_call_target="tpu_custom_call" | custom-call | tf_op jit(solution)/shard_map/tail/pallas_call | solution.py:996
  396.1 1.7 fusion.22
  397.8 0.7 fusion.19
  398.5 2.4 fusion.2
  400.9 2.3 fusion.21
  403.2 4.4 %fusion = f32[1024,256]{1,0:T(8,128)} fusion(bf16[2048,1024]{1,0:T(8,128)(2,1)} %all-gather.5.cloned.1.call-done, bf16[2048,384]{1,0:T(8,128)(2,1)S(1)} %bitcast.73), kind=kOutput, calls=%fused_computation | convolution fusion | flops 1073741824 | bytes 6291456 | tf_op jit(solution)/shard_map/dot_general | solution.py:1028
  407.6 26.8 %expert_grads.1 = (f32[768,2048]{1,0:T(8,128)}, f32[768,2048]{1,0:T(8,128)}, f32[768,2048]{1,0:T(8,128)}) custom-call(bf16[2048,2176]{1,0:T(8,128)(2,1)} %shard_map.263.x_ref, bf16[2048,2048]{1,0:T(8,128)(2,1)} %all-gather.3.cloned.1.call-done.cot_ref, bf16[768,2048]{1,0:T(8,128)(2,1)} %get-tuple-element.66.gl_ref, ...), custom_call_target="tpu_custom_call" | custom-call | flops 19327352832 | bytes 41943040 | tf_op jit(solution)/shard_map/expert_grads/pallas_call | solution.py:1125
  434.4 1.0 copy.38
  435.4 1.0 copy.39
  (72 shorter events, 7.5 us)
Async XLA Ops:
  7.2 1.2 copy-start
  7.2 136.4 %all-gather.3.cloned.1.call-start = ((), (), s32[]{:S(2)}) async-start(), calls=%async_computation | async-start | bytes 8650752 | tf_op jit(solution)/shard_map/all_gather | solution.py:1490
  9.2 394.0 %all-gather.5.cloned.1.call-start = ((), (), s32[]{:S(2)}) async-start(), calls=%async_computation.1 | async-start | bytes 4718592 | tf_op jit(solution)/shard_map/all_gather | solution.py:1507
  14.6 0.7 copy-start.8
  15.3 0.7 copy-start.10
  16.0 0.7 copy-start.12
  16.6 0.7 copy-start.14
  82.0 0.8 copy-start.5
  82.8 0.7 copy-start.7
  195.0 79.6 %copy-start.3 = (bf16[64,2048]{1,0:T(8,128)(2,1)S(1)}, bf16[64,2048]{1,0:T(8,128)(2,1)}, u32[]{:S(2)}) copy-start(bf16[64,2048]{1,0:T(8,128)(2,1)} %constant_dynamic-slice_fusion.2.cot_ref) | copy-start | bytes 786436
  195.0 79.5 %copy-start.9 = (f32[2048]{0:T(1024)S(1)}, f32[2048]{0:T(1024)}, u32[]{:S(2)}) copy-start(f32[2048]{0:T(1024)} %param.26) | copy-start | bytes 24580
  195.0 79.5 %copy-start.13 = (f32[128]{0:T(128)S(1)}, f32[128]{0:T(128)}, u32[]{:S(2)}) copy-start(f32[128]{0:T(128)} %param.23) | copy-start | bytes 1540
  273.5 1.0 copy-start.2
  274.5 39.8 %copy-start.4 = (bf16[2048,128]{1,0:T(8,128)(2,1)S(1)}, bf16[2048,128]{1,0:T(8,128)(2,1)}, u32[]{:S(2)}) copy-start(bf16[2048,128]{1,0:T(8,128)(2,1)} %wk_ref.3) | copy-start | bytes 1572868
  274.5 39.8 %copy-start.11 = (f32[2048]{0:T(1024)S(1)}, f32[2048]{0:T(1024)}, u32[]{:S(2)}) copy-start(f32[2048]{0:T(1024)} %param.19) | copy-start | bytes 24580
  274.6 39.7 %copy-start.15 = (f32[128]{0:T(128)S(1)}, f32[128]{0:T(128)}, u32[]{:S(2)}) copy-start(f32[128]{0:T(128)} %param.24) | copy-start | bytes 1540
  313.4 0.8 copy-start.6
  314.3 81.8 %copy-start.16 = (bf16[8,4,64,256]{3,2,1,0:T(8,128)(2,1)S(1)}, bf16[8,4,64,256]{3,2,1,0:T(8,128)(2,1)}, u32[]{:S(2)}) copy-start(bf16[8,4,64,256]{3,2,1,0:T(8,128)(2,1)} %get-tuple-element.61) | copy-start | bytes 3145732
  394.3 6.6 %copy-start.19 = (bf16[2048,1024]{1,0:T(8,128)(2,1)S(1)}, bf16[2048,1024]{1,0:T(8,128)(2,1)}, u32[]{:S(2)}) copy-start(bf16[2048,1024]{1,0:T(8,128)(2,1)} %get-tuple-element.62) | copy-start | bytes 12582916
  398.5 4.7 %copy-start.20 = (bf16[8,4,64,384]{3,2,1,0:T(8,128)(2,1)S(1)}, bf16[8,4,64,384]{3,2,1,0:T(8,128)(2,1)}, u32[]{:S(2)}) copy-start(bf16[8,4,64,384]{3,2,1,0:T(8,128)(2,1)} %get-tuple-element.65) | copy-start | bytes 4718596
  407.6 26.8 %copy-start.18 = (bf16[256,2048]{1,0:T(8,128)(2,1)S(1)}, bf16[256,2048]{1,0:T(8,128)(2,1)}, u32[]{:S(2)}) copy-start(bf16[256,2048]{1,0:T(8,128)(2,1)} %get-tuple-element.101) | copy-start | bytes 3145732
  407.6 27.7 %copy-start.17 = (bf16[256,2048]{1,0:T(8,128)(2,1)S(1)}, bf16[256,2048]{1,0:T(8,128)(2,1)}, u32[]{:S(2)}) copy-start(bf16[256,2048]{1,0:T(8,128)(2,1)} %get-tuple-element.102) | copy-start | bytes 3145732
  407.6 28.7 %copy-start.1 = (bf16[256,2048]{1,0:T(8,128)(2,1)S(1)}, bf16[256,2048]{1,0:T(8,128)(2,1)}, u32[]{:S(2)}) copy-start(bf16[256,2048]{1,0:T(8,128)(2,1)} %param.31) | copy-start | bytes 3145732
Sparse Core Ops, SparseCore 0:
  11.5 92.3 all-gather.2
  106.0 77.3 all-gather.4

commit v4 on v3

--- a/solution.py
+++ b/solution.py
@@ -30,72 +30,102 @@
     def _(): sig(dev(z-1,x,y,c))
     pl.semaphore_wait(b,5-(3-z)//3-z//3)
 
-def ag32_kernel(x_ref,out_ref,lsem,send,recv):
-    rows=x_ref.shape[0]
-    z,x,y,c,ax,ay,bx,by=neighbours()
-    barrier_all()
-    me=pid(z,x,y,c)
-    def at(p): return out_ref.at[pl.ds(pl.multiple_of(p*rows,rows),rows)]
-    def cp(p,d,k,own=False):
-        return pltpu.make_async_remote_copy(src_ref=x_ref if own else at(p),dst_ref=at(p),send_sem=send.at[k,p],recv_sem=recv.at[p],device_id=d,device_id_type=MESH)
-    up,down,A,B,C=dev(z+1,x,y,c),dev(z-1,x,y,c),dev(z,ax,ay,c),dev(z,bx,by,c),dev(z,x,y,1-c)
-    def wait(p):
-        cp(p,C,4).wait_recv()
-    loc=pltpu.make_async_copy(x_ref,at(me),lsem); loc.start()
-    @pl.when(z<3)
-    def _(): cp(me,up,0,True).start()
-    @pl.when(z>0)
-    def _(): cp(me,down,1,True).start()
-    cp(me,A,2,True).start(); cp(me,B,3,True).start(); cp(me,C,4,True).start()
-    def zlow(d):
-        @pl.when(z-d>=0)
-        def _():
-            p=pid(z-d,x,y,c); wait(p)
-            @pl.when(z<3)
-            def _(): cp(p,up,0).start()
-            cp(p,A,2).start(); cp(p,B,3).start(); cp(p,C,4).start()
-    def zhigh(d):
-        @pl.when(z+d<=3)
-        def _():
-            p=pid(z+d,x,y,c); wait(p)
-            @pl.when(z>0)
-            def _(): cp(p,down,1).start()
-            cp(p,A,2).start(); cp(p,B,3).start(); cp(p,C,4).start()
-    def fa(zz):
-        @pl.when((zz>=0)&(zz<=3))
-        def _():
-            p=pid(zz,ax,ay,c); wait(p)
-            cp(p,B,3).start(); cp(p,C,4).start()
-    def fb(zz,xx,yy):
-        @pl.when((zz>=0)&(zz<=3))
-        def _():
-            p=pid(zz,xx,yy,c); wait(p); cp(p,C,4).start()
-    zlow(1); zhigh(1); fa(z); zlow(2); zhigh(2); fa(z-1); fa(z+1); fb(z,bx,by); zlow(3); zhigh(3)
-    fa(z-2); fa(z+2); fb(z-1,bx,by); fb(z+1,bx,by); fa(z-3); fa(z+3)
-    dx,dy=1-x,1-y
-    fb(z,dx,dy); fb(z-2,bx,by); fb(z+2,bx,by); fb(z-1,dx,dy); fb(z+1,dx,dy); fb(z-3,bx,by); fb(z+3,bx,by); fb(z-2,dx,dy); fb(z+2,dx,dy); fb(z-3,dx,dy); fb(z+3,dx,dy)
-    for zz in range(4):
-        for xx in range(2):
-            for yy in range(2):
-                wait(pid(zz,xx,yy,1-c))
-    loc.wait()
-    for zz in range(4):
-        p=pid(zz,x,y,c)
-        @pl.when((z<3)&(zz<=z))
-        def _(): cp(p,up,0).wait_send()
-        @pl.when((z>0)&(zz>=z))
-        def _(): cp(p,down,1).wait_send()
-        cp(p,A,2).wait_send(); cp(p,B,3).wait_send(); cp(p,C,4).wait_send()
-        q=pid(zz,ax,ay,c)
-        cp(q,B,3).wait_send(); cp(q,C,4).wait_send()
-        cp(pid(zz,bx,by,c),C,4).wait_send(); cp(pid(zz,dx,dy,c),C,4).wait_send()
-
-def ag32(piece,cid=0):
-    rows,w=piece.shape
-    return pl.pallas_call(ag32_kernel,out_shape=jax.ShapeDtypeStruct((rows*32,w),piece.dtype),
-        in_specs=[pl.BlockSpec(memory_space=pl.ANY)],out_specs=pl.BlockSpec(memory_space=pl.ANY),
-        scratch_shapes=[pltpu.SemaphoreType.DMA,pltpu.SemaphoreType.DMA((5,32)),pltpu.SemaphoreType.DMA((32,))],
-        compiler_params=pltpu.CompilerParams(collective_id=cid,has_side_effects=True))(piece)
+class Gather:
+    def __init__(self, own_ref, out_ref, lsem, send, recv):
+        self.own, self.out, self.lsem, self.send, self.recv = own_ref, out_ref, lsem, send, recv
+        self.rows = own_ref.shape[0]
+        z, x, y, c, ax, ay, bx, by = neighbours()
+        self.at_me = (z, x, y, c, ax, ay, bx, by)
+        self.up, self.down = dev(z + 1, x, y, c), dev(z - 1, x, y, c)
+        self.A, self.B, self.C = dev(z, ax, ay, c), dev(z, bx, by, c), dev(z, x, y, 1 - c)
+
+    def place(self, p):
+        return self.out.at[pl.ds(pl.multiple_of(p * self.rows, self.rows), self.rows)]
+
+    def copy(self, p, to, k, own=False):
+        return pltpu.make_async_remote_copy(
+            src_ref=self.own if own else self.place(p), dst_ref=self.place(p),
+            send_sem=self.send.at[k, p], recv_sem=self.recv.at[p], device_id=to, device_id_type=MESH)
+
+    def wait(self, p):
+        self.copy(p, self.C, 4).wait_recv()
+
+    def local(self):
+        z, x, y, c = self.at_me[:4]
+        return pltpu.make_async_copy(self.own, self.place(pid(z, x, y, c)), self.lsem)
+
+    def start(self):
+        z, x, y, c = self.at_me[:4]
+        me = pid(z, x, y, c)
+        self.local().start()
+
+        @pl.when(z < 3)
+        def _():
+            self.copy(me, self.up, 0, True).start()
+
+        @pl.when(z > 0)
+        def _():
+            self.copy(me, self.down, 1, True).start()
+
+        for to, k in ((self.A, 2), (self.B, 3), (self.C, 4)):
+            self.copy(me, to, k, True).start()
+
+    def from_line(self, zz):
+        z, x, y, c = self.at_me[:4]
+        p = pid(zz, x, y, c)
+        self.wait(p)
+
+        @pl.when((zz < z) & (z < 3))
+        def _():
+            self.copy(p, self.up, 0).start()
+
+        @pl.when((zz > z) & (z > 0))
+        def _():
+            self.copy(p, self.down, 1).start()
+
+        for to, k in ((self.A, 2), (self.B, 3), (self.C, 4)):
+            self.copy(p, to, k).start()
+
+    def from_a(self, zz):
+        z, x, y, c, ax, ay, bx, by = self.at_me
+
+        p = pid(zz, ax, ay, c)
+        self.wait(p)
+        self.copy(p, self.B, 3).start()
+        self.copy(p, self.C, 4).start()
+
+    def from_b(self, zz, xx, yy):
+        c = self.at_me[3]
+
+        p = pid(zz, xx, yy, c)
+        self.wait(p)
+        self.copy(p, self.C, 4).start()
+
+    def finish(self):
+        z, x, y, c, ax, ay, bx, by = self.at_me
+
+        def one(zz, carry):
+            p = pid(zz, x, y, c)
+
+            @pl.when((z < 3) & (zz <= z))
+            def _():
+                self.copy(p, self.up, 0).wait_send()
+
+            @pl.when((z > 0) & (zz >= z))
+            def _():
+                self.copy(p, self.down, 1).wait_send()
+
+            for to, k in ((self.A, 2), (self.B, 3), (self.C, 4)):
+                self.copy(p, to, k).wait_send()
+            p = pid(zz, ax, ay, c)
+            self.copy(p, self.B, 3).wait_send()
+            self.copy(p, self.C, 4).wait_send()
+            self.copy(pid(zz, bx, by, c), self.C, 4).wait_send()
+            self.copy(pid(zz, 1 - x, 1 - y, c), self.C, 4).wait_send()
+            return carry
+
+        lax.fori_loop(0, 4, one, 0)
+
 
 def far_z(z, k):
     half = z // 2
@@ -104,34 +134,70 @@
     return place + half * (3 - 2 * place)
 
 
-def reduce_all_kernel(
-    part_ref,
-    out_ref,
-    acc, cbuf, bbuf, abuf, zbuf,
-    lsem, csend, crecv, bsend, brecv, asend, arecv, zsend, zrecv,
+def reduce_kernel(
+    hs_ref, gl_ref, ul_ref, pair_ref, wd_ref, wg_ref, wu_ref, att_ref,
+    out_ref, line_ref,
+    acc, cbuf, bbuf, abuf, zbuf, blk, mats, low, pair,
+    csend, crecv, bsend, brecv, asend, arecv, zsend, zrecv, msem, lsem, psem, nsem, nsend, nrecv,
 ):
     f32 = jnp.float32
     rows = out_ref.shape[0]
+    width = wd_ref.shape[1]
     z, x, y, c, ax, ay, bx, by = neighbours()
     dx, dy = 1 - x, 1 - y
     A, B, C = dev(z, ax, ay, c), dev(z, bx, by, c), dev(z, x, y, 1 - c)
     up, down = dev(z + 1, x, y, c), dev(z - 1, x, y, c)
+    tok = 4 * rows
 
     def q(zz, xx, yy):
         return zz * 4 + xx * 2 + yy
 
-    def at(p):
-        return part_ref.at[pl.ds(pl.multiple_of(p * rows, rows), rows)]
-
-    def ccopy(zz, xx, yy):
+    def place_of(u):
+        return far_z(z, u // 2), (u % 2) * (2 * x - 1) + 1 - x
+
+    def loads(u):
+        zz, xx = place_of(u)
+        span = pl.ds(pl.multiple_of((zz * 2 + xx) * tok, tok), tok)
+        slot = u % 2
+        return [
+            pltpu.make_async_copy(r.at[span], low.at[slot, n], lsem.at[slot, n])
+            for n, r in enumerate((hs_ref, gl_ref, ul_ref))
+        ] + [pltpu.make_async_copy(pair_ref.at[span], pair.at[slot], psem.at[slot])]
+
+    def part_rows(slot, yy, cc):
+        return blk.at[slot, pl.ds(pl.multiple_of((yy * 2 + cc) * rows, rows), rows)]
+
+    def ccopy(zz, xx, yy, slot):
         i = q(zz, xx, yy)
         return pltpu.make_async_remote_copy(
-            src_ref=at(pid(zz, xx, yy, 1 - c)), dst_ref=cbuf.at[i], send_sem=csend.at[i],
+            src_ref=part_rows(slot, yy, 1 - c), dst_ref=cbuf.at[i], send_sem=csend.at[slot, yy],
             recv_sem=crecv.at[i], device_id=C, device_id_type=MESH)
 
-    def lcopy(zz, xx, yy):
-        i = q(zz, xx, yy)
-        return pltpu.make_async_copy(at(pid(zz, xx, yy, c)), acc.at[i], lsem.at[i])
+    def products(u):
+        slot = u % 2
+        zz, xx = place_of(u)
+        for cp in loads(u):
+            cp.wait()
+
+        @pl.when(u < 7)
+        def _():
+            for cp in loads(u + 1):
+                cp.start()
+
+        @pl.when(u > 1)
+        def _():
+            for yy in range(2):
+                ccopy(zz, xx, yy, slot).wait_send()
+
+        blk[slot, :, :width] = nn(low[slot, 0], mats[0]).astype(blk.dtype)
+        blk[slot, :, width : 2 * width] = (
+            nn(low[slot, 1], mats[1]) + nn(low[slot, 2], mats[2])
+        ).astype(blk.dtype)
+        blk[slot, :, 2 * width :] = pair[slot]
+        for yy in range(2):
+            ccopy(zz, xx, yy, slot).start()
+        for yy in range(2):
+            acc[q(zz, xx, yy)] = part_rows(slot, yy, c)[...]
 
     def bcopy(zz, far):
         i = zz + 4 * far
@@ -150,25 +216,16 @@
             src_ref=acc.at[q(zz, x, y)], dst_ref=zbuf.at[slot], send_sem=zsend.at[zz],
             recv_sem=zrecv.at[slot], device_id=to, device_id_type=MESH)
 
-    def stage_c(k):
-        zz = far_z(z, k)
-        for xx, yy in ((dx, dy), (bx, by), (ax, ay), (x, y)):
-            lcopy(zz, xx, yy).start()
-        for xx, yy in ((dx, dy), (ax, ay), (bx, by), (x, y)):
-            ccopy(zz, xx, yy).start()
-
     def plus_c(zz, xx, yy):
-        lcopy(zz, xx, yy).wait()
-        ccopy(zz, xx, yy).wait_recv()
+        ccopy(zz, xx, yy, 0).wait_recv()
         i = q(zz, xx, yy)
         return acc[i].astype(f32) + cbuf[i].astype(f32)
 
-    def stage_b(k):
+    def stage_b(k, far):
         zz = far_z(z, k)
-        acc[q(zz, dx, dy)] = plus_c(zz, dx, dy).astype(acc.dtype)
-        bcopy(zz, 1).start()
-        acc[q(zz, bx, by)] = plus_c(zz, bx, by).astype(acc.dtype)
-        bcopy(zz, 0).start()
+        xx, yy = (dx, dy) if far else (bx, by)
+        acc[q(zz, xx, yy)] = plus_c(zz, xx, yy).astype(acc.dtype)
+        bcopy(zz, far).start()
 
     def stage_a(k):
         zz = far_z(z, k)
@@ -225,34 +282,57 @@
                 zcopy(z, down, 4).wait_recv()
                 out_ref[...] += zbuf[4].astype(f32)
 
+    weights = [pltpu.make_async_copy(r, mats.at[n], msem.at[n]) for n, r in enumerate((wd_ref, wg_ref, wu_ref))]
+    for cp in weights:
+        cp.start()
+    for cp in loads(0):
+        cp.start()
+    line = Line(lambda zz: line_ref.at[zz], nsend, nrecv, att_ref)
+    mine = pltpu.make_async_copy(att_ref, line_ref.at[z], nsem)
+    mine.start()
     barrier_all()
-
-    def first(k, carry):
-        stage_c(k)
+    line.start()
+    for cp in weights:
+        cp.wait()
+
+    def step(u, carry):
+        @pl.when(u < 8)
+        def _():
+            products(u)
+
+        for d in (1, 2, 3):
+            @pl.when(u == 2 * d + 1)
+            def _():
+                line.pass_on(d)
+
+        k = (u - 1) // 2
+
+        @pl.when((u > 0) & (u < 9) & (u % 2 == 1))
+        def _():
+            stage_b(k, 1)
+
+        @pl.when((u > 0) & (u < 9) & (u % 2 == 0))
+        def _():
+            stage_b(k, 0)
+
+        @pl.when((u >= 5) & (u < 13) & (u % 2 == 1))
+        def _():
+            stage_a((u - 5) // 2)
+
+        @pl.when((u >= 8) & (u % 2 == 0))
+        def _():
+            stage_z((u - 8) // 2)
+
         return carry
 
-    lax.fori_loop(0, 4, first, 0)
-    stage_b(0)
-
-    def step(t, carry):
-        @pl.when(t < 3)
-        def _():
-            stage_b(t + 1)
-
-        @pl.when(t < 4)
-        def _():
-            stage_a(t)
-
-        @pl.when(t > 0)
-        def _():
-            stage_z(t - 1)
-
-        return carry
-
-    lax.fori_loop(0, 5, step, 0)
+    lax.fori_loop(0, 15, step, 0)
+    mine.wait()
+    line.finish()
+    for slot in range(2):
+        for yy in range(2):
+            ccopy(z, x, yy, slot).wait_send()
+
     def last(zz, carry):
-        for xx, yy in ((dx, dy), (bx, by), (ax, ay), (x, y)):
-            ccopy(zz, xx, yy).wait_send()
         bcopy(zz, 1).wait_send()
         bcopy(zz, 0).wait_send()
         acopy(zz).wait_send()
@@ -266,29 +346,42 @@
     lax.fori_loop(0, 4, last, 0)
 
 
-def reduce_all(part, cid):
-    n, w = part.shape
+def reduce_experts(hs, gl, ul, pair, wd, wg, wu, att, cid):
+    n, hid = hs.shape
+    width = wd.shape[1]
     rows = n // 32
+    w = 2 * width + pair.shape[1]
     dma = pltpu.SemaphoreType.DMA
+    bf = jnp.bfloat16
 
     def pieces(k):
-        return pltpu.VMEM((k, rows, w), part.dtype)
-
+        return pltpu.VMEM((k, rows, w), bf)
+
+    anywhere = pl.BlockSpec(memory_space=pl.ANY)
     return pl.pallas_call(
-        reduce_all_kernel,
-        in_specs=[pl.BlockSpec(memory_space=pl.ANY)],
-        out_specs=pl.BlockSpec(memory_space=pltpu.VMEM),
-        out_shape=jax.ShapeDtypeStruct((rows, w), jnp.float32),
+        reduce_kernel,
+        in_specs=[anywhere] * 8,
+        out_specs=[pl.BlockSpec(memory_space=pltpu.VMEM), anywhere],
+        out_shape=[
+            jax.ShapeDtypeStruct((rows, w), jnp.float32), jax.ShapeDtypeStruct((4, *att.shape), bf),
+        ],
         scratch_shapes=[
             pieces(16), pieces(16), pieces(8), pieces(4), pieces(5),
-            dma((16,)), dma((16,)), dma((16,)), dma((8,)), dma((8,)), dma((4,)), dma((4,)),
-            dma((4,)), dma((5,)),
+            pltpu.VMEM((2, 4 * rows, w), bf),
+            pltpu.VMEM((3, hid, width), bf),
+            pltpu.VMEM((2, 3, 4 * rows, hid), bf),
+            pltpu.VMEM((2, 4 * rows, pair.shape[1]), bf),
+            dma((2, 2)), dma((16,)), dma((8,)), dma((8,)), dma((4,)), dma((4,)),
+            dma((4,)), dma((5,)), dma((3,)), dma((2, 3)), dma((2,)), dma, dma((2, 4)), dma((4,)),
         ],
         compiler_params=pltpu.CompilerParams(
-            collective_id=cid, has_side_effects=True, vmem_limit_bytes=48 * 2**20
+            collective_id=cid, has_side_effects=True, vmem_limit_bytes=56 * 2**20
         ),
-        name="reduce_all",
-    )(part)
+        cost_estimate=pl.CostEstimate(
+            flops=6 * n * width * hid, bytes_accessed=10 * n * width, transcendentals=0
+        ),
+        name="reduce_experts",
+    )(hs, gl, ul, pair, wd, wg, wu, att)
 
 
 def barrier_wide():
@@ -306,17 +399,18 @@
     def __init__(self, src, buf, send, recv, tsend, trecv):
         self.src, self.buf, self.send, self.recv = src, buf, send, recv
         self.tsend, self.trecv = tsend, trecv
-        self.ctx, self.tp = lax.axis_index("ctx"), lax.axis_index("tp")
+        self.tp = lax.axis_index("tp")
         z, x, y, c = coords()
+        self.z, self.x, self.y, self.c = z, x, y, c
         self.Y, self.C = dev(z, x, 1 - y, c), dev(z, x, y, 1 - c)
         self.mine, self.by_y, self.by_c, self.by_d = y * 2 + c, (1 - y) * 2 + c, y * 2 + 1 - c, (1 - y) * 2 + 1 - c
 
     def push(self, i):
-        to = (self.ctx + i) % 8
+        to = (self.z + i) % 4
         return pltpu.make_async_remote_copy(
-            src_ref=self.src.at[to], dst_ref=self.buf.at[self.ctx, self.tp],
-            send_sem=self.send.at[i], recv_sem=self.recv.at[i], device_id=(to, self.tp),
-            device_id_type=MESH)
+            src_ref=self.src.at[to], dst_ref=self.buf.at[self.z, self.tp],
+            send_sem=self.send.at[i], recv_sem=self.recv.at[i],
+            device_id=dev(to, self.x, self.y, self.c), device_id_type=MESH)
 
     def over(self, part, to, k):
         return pltpu.make_async_remote_copy(
@@ -324,12 +418,12 @@
             recv_sem=self.trecv.at[part], device_id=to, device_id_type=MESH)
 
     def start(self):
-        for i in range(1, 8):
+        for i in range(1, 4):
             self.push(i).start()
-        self.buf[self.ctx, self.tp] = self.src[self.ctx]
+        self.buf[self.z, self.tp] = self.src[self.z]
 
     def exchange(self):
-        for i in range(1, 8):
+        for i in range(1, 4):
             self.push(i).wait_recv()
         self.over(self.mine, self.Y, 0).start()
         self.over(self.mine, self.C, 1).start()
@@ -341,11 +435,64 @@
     def finish(self):
         self.over(self.by_c, self.C, 1).wait_recv()
         self.over(self.by_d, self.C, 2).wait_recv()
-        for i in range(1, 8):
+        for i in range(1, 4):
             self.push(i).wait_send()
         self.over(self.mine, self.Y, 0).wait_send()
         self.over(self.mine, self.C, 1).wait_send()
         self.over(self.by_y, self.C, 2).wait_send()
+
+
+class Line:
+    def __init__(self, place, send, recv, first=None):
+        self.place, self.send, self.recv, self.first = place, send, recv, first
+        z, x, y, c = coords()
+        self.z = z
+        self.up, self.down = dev(z + 1, x, y, c), dev(z - 1, x, y, c)
+
+    def copy(self, zz, to, k, own=False):
+        src = self.first if own and self.first is not None else self.place(zz)
+        return pltpu.make_async_remote_copy(
+            src_ref=src, dst_ref=self.place(zz), send_sem=self.send.at[k, zz],
+            recv_sem=self.recv.at[zz], device_id=to, device_id_type=MESH)
+
+    def start(self):
+        @pl.when(self.z < 3)
+        def _():
+            self.copy(self.z, self.up, 0, True).start()
+
+        @pl.when(self.z > 0)
+        def _():
+            self.copy(self.z, self.down, 1, True).start()
+
+    def pass_on(self, d):
+        z = self.z
+
+        @pl.when(z - d >= 0)
+        def _():
+            self.copy(z - d, self.up, 0).wait_recv()
+
+            @pl.when(z < 3)
+            def _():
+                self.copy(z - d, self.up, 0).start()
+
+        @pl.when(z + d <= 3)
+        def _():
+            self.copy(z + d, self.down, 1).wait_recv()
+
+            @pl.when(z > 0)
+            def _():
+                self.copy(z + d, self.down, 1).start()
+
+    def finish(self):
+        z = self.z
+        for zz in range(4):
+            @pl.when((z < 3) & (zz <= z))
+            def _():
+                self.copy(zz, self.up, 0).wait_send()
+
+            @pl.when((z > 0) & (zz >= z))
+            def _():
+                self.copy(zz, self.down, 1).wait_send()
 
 
 class Spread:
@@ -434,33 +581,41 @@
 
 def front_kernel(
     x_ref, g1_ref, wq_ref, wk_ref, wv_ref, qg_ref, kg_ref, cos_ref, sin_ref, qpos_ref, kpos_ref,
-    wo_ref, g2_ref, wr_ref, routes_ref,
+    wo_ref, g2_ref, wr_ref, routes_ref, cot_ref,
     first_ref, qraw_ref, kraw_ref, qrot_ref, kv_ref, att_ref, log_ref, res_ref, gates_ref, piece_ref, cols_ref,
-    wq, wo, part, cbuf, ybuf, stage, csrc,
+    xs, wk, wv, turned, wq, wo, part, cbuf, ybuf, stage, csrc,
     wsem, ksend, krecv, csend, crecv, ysend, yrecv, psend, precv, tsend, trecv,
 ):
     f32, bf = jnp.float32, jnp.bfloat16
     z, x, y, c = coords()
     rows = res_ref.shape[0]
-    experts = wr_ref.shape[0] // 4
+    experts = wr_ref.shape[0]
     head = qg_ref.shape[1]
     heads = wq_ref.shape[1] // head
     half = x_ref.shape[0] // 2
-    wqc = pltpu.make_async_copy(wq_ref, wq, wsem.at[0])
-    woc = pltpu.make_async_copy(wo_ref, wo, wsem.at[1])
-    wqc.start()
-    woc.start()
+    xc, wkc, wvc, wqc, woc = (
+        pltpu.make_async_copy(src, dst, wsem.at[n])
+        for n, (src, dst) in enumerate(((x_ref, xs), (wk_ref, wk), (wv_ref, wv), (wq_ref, wq), (wo_ref, wo)))
+    )
+    for cp in (xc, wkc, wvc, wqc, woc):
+        cp.start()
+    own = pl.ds(pl.multiple_of((y * 2 + c) * rows, rows), rows)
     Y, C = dev(z, x, 1 - y, c), dev(z, x, y, 1 - c)
     barrier_wide()
-
-    value = x_ref[...].astype(f32)
+    cotc = pltpu.make_async_copy(cot_ref.at[own], piece_ref.at[:, x_ref.shape[1] : 2 * x_ref.shape[1]], wsem.at[5])
+    cotc.start()
+    turned[...] = routes_ref[...].T
+    xc.wait()
+    value = xs[...].astype(f32)
     first = (value * row_norm(value) * g1_ref[...]).astype(bf)
     first_ref[...] = first
     cos, sin = cos_ref[...], sin_ref[...]
-    kraw = nn(first, wk_ref[...])
+    wkc.wait()
+    wvc.wait()
+    kraw = nn(first, wk[...])
     kraw_ref[...] = kraw
     krot = turn(kraw * row_norm(kraw) * kg_ref[...], cos, sin).astype(bf)
-    vrow = nn(first, wv_ref[...]).astype(bf)
+    vrow = nn(first, wv[...]).astype(bf)
     me = z * 2 + x
     for s in range(2):
         kv_ref[s, me] = krot[s * half : (s + 1) * half]
@@ -488,35 +643,43 @@
     keys_out.pass_on(3)
     keys_out.arrive()
     width = first.shape[1]
-    per = width // 8
-    own = pl.ds(pl.multiple_of((y * 2 + c) * rows, rows), rows)
-    for i in range(8):
+    per = width // 4
+    for i in range(4):
         csrc[i] = first_ref[own, i * per : (i + 1) * per]
     blocks = Columns(csrc, cols_ref, psend, precv, tsend, trecv)
     blocks.start()
 
     scale = 1.0 / math.sqrt(head)
 
+    group = 4
+
     def attend(i, carry):
-        s = i // heads
-        h = i % heads
+        s = i // (heads // group)
+        h = i % (heads // group) * group
         span = pl.ds(pl.multiple_of(s * half, half), half)
         keys = kv_ref[s].reshape(8 * half, head)
         vals = kv_ref[2 + s].reshape(8 * half, head)
-        scores = nt(qrot_ref[i], keys) * scale
+        query = qrot_ref[pl.ds(i * group, group)].reshape(group * half, head)
+        scores = (nt(query, keys) * scale).reshape(group, half, 8 * half)
         allowed = qpos_ref[span, :1] >= kpos_ref[pl.ds(s, 1), :]
-        scores = jnp.where(allowed, scores, -1e9)
+        scores = jnp.where(allowed[None], scores, -1e9).reshape(group * half, 8 * half)
         top = jnp.max(scores, axis=1, keepdims=True)
         weights = jnp.exp(scores - top)
         total = jnp.sum(weights, axis=1, keepdims=True)
-        probs = (weights / total).astype(bf)
-        att_ref[span, pl.ds(pl.multiple_of(h * head, head), head)] = nn(probs, vals).astype(bf)
-        log_ref[i] = jnp.broadcast_to(top + jnp.log(total), (half, head))
+        probs = (weights * (1.0 / total)).astype(bf)
+        mixed = nn(probs, vals).astype(bf)
+        logs = jnp.broadcast_to(top + jnp.log(total), (group * half, head))
+        log_ref[pl.ds(i * group, group)] = logs.reshape(group, half, head)
+        for g in range(group):
+            lanes = pl.ds(pl.multiple_of((h + g) * head, head), head)
+            att_ref[span, lanes] = mixed[g * half : (g + 1) * half]
+        @pl.when(i == steps // 2 - 1)
+        def _():
+            blocks.exchange()
         return carry
 
-    lax.fori_loop(0, heads, attend, 0)
-    blocks.exchange()
-    lax.fori_loop(heads, 2 * heads, attend, 0)
+    steps = 2 * heads // group
+    lax.fori_loop(0, steps, attend, 0)
     blocks.forward()
     woc.wait()
 
@@ -542,10 +705,10 @@
         src_ref=stage, dst_ref=ybuf, send_sem=ysend, recv_sem=yrecv, device_id=Y, device_id_type=MESH)
     yc.start()
     ccopy(y).wait_recv()
-    res = x_ref[own].astype(f32) + (at(y, c)[...].astype(f32) + cbuf[y].astype(f32))
+    res = xs[own].astype(f32) + (at(y, c)[...].astype(f32) + cbuf[y].astype(f32))
     lane = lax.broadcasted_iota(jnp.int32, (rows, 4 * experts), 1)
     named = jnp.zeros((rows, 4 * experts), jnp.bool_)
-    routes = routes_ref[...]
+    routes = turned[own]
     for k in range(routes.shape[1]):
         named = named | (lane % experts == routes[:, k : k + 1])
     yc.wait_recv()
@@ -554,6 +717,7 @@
     second = (res * row_norm(res) * g2_ref[...]).astype(bf)
     piece_ref[:, :width] = second
     logits = nt(second, wr_ref[...])
+    logits = jnp.concatenate([logits, logits, jnp.zeros((rows, 2 * experts), f32)], axis=1)
     masked = jnp.where(named & (lane < 2 * experts), logits, -1e30)
     top = jnp.max(masked, axis=1, keepdims=True)
     weights = jnp.where(named & (lane < 2 * experts), jnp.exp(masked - top), 0.0)
@@ -562,16 +726,17 @@
     high = gates.astype(bf)
     low = (gates - high.astype(f32)).astype(bf)
     gates_ref[...] = jnp.where(lane < experts, gates, 0.0)
-    piece_ref[:, width:] = jnp.where(lane < experts, high, low)
+    piece_ref[:, 2 * width :] = jnp.where(lane < experts, high, low)
 
     yc.wait_send()
     ccopy(0).wait_send()
     ccopy(1).wait_send()
     blocks.finish()
     keys_out.finish()
-
-
-def front(x, g1, wq, wk, wv, qg, kg, cos, sin, qpos, kpos, wo, g2, wr, routes, cid):
+    cotc.wait()
+
+
+def front(x, g1, wq, wk, wv, qg, kg, cos, sin, qpos, kpos, wo, g2, wr, routes, cot, cid):
     tok, width = x.shape
     head = qg.shape[1]
     cols = wq.shape[1]
@@ -586,26 +751,28 @@
 
     return pl.pallas_call(
         front_kernel,
-        in_specs=[vm, vm, anywhere] + [vm] * 8 + [anywhere] + [vm] * 3,
+        in_specs=[anywhere, vm] + [anywhere] * 3 + [vm] * 6 + [anywhere] + [vm] * 3 + [anywhere],
         out_specs=[vm] * 11,
         out_shape=[
             out((tok, width), bf), out((tok, cols), f32), out((tok, head), f32),
             out((2 * heads, half, head), bf), out((4, 8, half, head), bf), out((tok, cols), bf),
             out((2 * heads, half, head), f32), out((rows, width), f32), out((rows, 128), f32),
-            out((rows, width + 128), bf), out((8, 4, rows, width // 8), bf),
+            out((rows, 2 * width + 128), bf), out((4, 4, rows, width // 4), bf),
         ],
         scratch_shapes=[
+            pltpu.VMEM((tok, width), bf), pltpu.VMEM((width, head), bf), pltpu.VMEM((width, head), bf),
+            pltpu.VMEM(routes.shape[::-1], jnp.int32),
             pltpu.VMEM((width, cols), bf), pltpu.VMEM((cols, width), bf), pltpu.VMEM((tok, width), bf),
             pltpu.VMEM((2, rows, width), bf), pltpu.VMEM((rows, width), bf), pltpu.VMEM((rows, width), bf),
-            pltpu.VMEM((8, rows, width // 8), bf),
-            dma((2,)), dma((3, 8)), dma((8,)), dma((2,)), dma((2,)), dma, dma,
-            dma((8,)), dma((8,)), dma((3,)), dma((4,)),
+            pltpu.VMEM((4, rows, width // 4), bf),
+            dma((6,)), dma((3, 8)), dma((8,)), dma((2,)), dma((2,)), dma, dma,
+            dma((4,)), dma((4,)), dma((3,)), dma((4,)),
         ],
         compiler_params=pltpu.CompilerParams(
             collective_id=cid, has_side_effects=True, vmem_limit_bytes=52 * 2**20
         ),
         name="front",
-    )(x, g1, wq, wk, wv, qg, kg, cos, sin, qpos, kpos, wo, g2, wr, routes)
+    )(x, g1, wq, wk, wv, qg, kg, cos, sin, qpos, kpos, wo, g2, wr, routes, cot)
 
 
 def middle_kernel(
@@ -617,7 +784,7 @@
     f32, bf = jnp.float32, jnp.bfloat16
     z, x, y, c = coords()
     rows, width = res_ref.shape
-    experts = wr_ref.shape[0] // 4
+    experts = wr_ref.shape[0]
     head = qg_ref.shape[1]
     heads = qraw_ref.shape[1] // head
     half = qraw_ref.shape[0] // 2
@@ -634,7 +801,7 @@
     gates = gates_ref[...]
     pair = sums_ref[:, 2 * width :]
     glog = (gates * (pair - jnp.sum(gates * pair, axis=1, keepdims=True))).astype(bf)
-    gsec = sums_ref[:, width : 2 * width] + nn(glog, wr_ref[...])
+    gsec = sums_ref[:, width : 2 * width] + nn(glog[:, :experts], wr_ref[...])
     rs = row_norm(res)
     unit = res * rs
     gn2_ref[...] = jnp.sum(gsec * unit, axis=0, keepdims=True)
@@ -652,8 +819,8 @@
 
     cp(y, c, Y, 0).start()
     cp(y, c, C, 1).start()
-    per = width // 8
-    for i in range(8):
+    per = width // 4
+    for i in range(4):
         csrc[i, :, :per] = glow[:, i * per : (i + 1) * per]
         csrc[i, :, per:] = glog
     blocks = Columns(csrc, cols_ref, psend, precv, tsend, trecv)
@@ -665,7 +832,9 @@
 
     def mix(yy):
         span = pl.ds(pl.multiple_of(yy * 2 * rows, 2 * rows), 2 * rows)
-        mixed[span] = nt(back[span], wo[...]).astype(bf)
+        both = nt(back[span], wo[...]).astype(bf)
+        for h in range(heads):
+            mixed[yy * heads + h] = both[:, h * head : (h + 1) * head]
 
     cp(y, 1 - c, C, 1).wait_recv()
     mix(y)
@@ -675,38 +844,44 @@
     mix(1 - y)
     scale = 1.0 / math.sqrt(head)
 
+    group = 4
+
     def attend(i, carry):
-        s = i // heads
-        h = i % heads
+        s = i // (heads // group)
+        h = i % (heads // group) * group
         span = pl.ds(pl.multiple_of(s * half, half), half)
-        lanes = pl.ds(pl.multiple_of(h * head, head), head)
+        mine = pl.ds(i * group, group)
         keys = kv_ref[s].reshape(8 * half, head)
         vals = kv_ref[2 + s].reshape(8 * half, head)
-        query = qrot_ref[i]
-        grad = mixed[span, lanes]
-        scores = nt(query, keys) * scale
+        query = qrot_ref[mine].reshape(group * half, head)
+        grad = mixed[mine].reshape(group * half, head)
+        scores = (nt(query, keys) * scale).reshape(group, half, 8 * half)
         allowed = qpos_ref[span, :1] >= kpos_ref[pl.ds(s, 1), :]
-        probs = jnp.where(allowed, jnp.exp(scores - log_ref[i][:, :1]), 0.0)
+        logs = log_ref[mine][:, :, :1]
+        probs = jnp.where(allowed[None], jnp.exp(scores - logs), 0.0).reshape(group * half, 8 * half)
         gprobs = nt(grad, vals)
         inner = jnp.sum(probs * gprobs, axis=1, keepdims=True)
         dots = (probs * (gprobs - inner) * scale).astype(bf)
         dk[s] += tn(dots, query)
         dv[s] += tn(probs.astype(bf), grad)
         drot = nn(dots, keys)
-        raw = qraw_ref[span, lanes]
-        dn = turn_back(drot, cos_ref[span], sin_ref[span])
-        rs = row_norm(raw)
-        unit = raw * rs
-        qgain_ref[...] += jnp.sum((dn * unit).reshape(half // 8, 8, head), axis=0)
-        cg = dn * qg_ref[...]
-        qlow_ref[span, lanes] = (rs * (cg - unit * jnp.mean(cg * unit, axis=1, keepdims=True))).astype(bf)
+        for g in range(group):
+            lanes = pl.ds(pl.multiple_of((h + g) * head, head), head)
+            raw = qraw_ref[span, lanes]
+            dn = turn_back(drot[g * half : (g + 1) * half], cos_ref[span], sin_ref[span])
+            rs = row_norm(raw)
+            unit = raw * rs
+            qgain_ref[...] += jnp.sum((dn * unit).reshape(half // 8, 8, head), axis=0)
+            cg = dn * qg_ref[...]
+            low = rs * (cg - unit * jnp.mean(cg * unit, axis=1, keepdims=True))
+            qlow_ref[span, lanes] = low.astype(bf)
         return carry
 
-    lax.fori_loop(0, heads, attend, 0)
+    steps = 2 * heads // group
+    lax.fori_loop(0, steps // 2, attend, 0)
     blocks.exchange()
-    lax.fori_loop(heads, 3 * heads // 2, attend, 0)
+    lax.fori_loop(steps // 2, steps, attend, 0)
     blocks.forward()
-    lax.fori_loop(3 * heads // 2, 2 * heads, attend, 0)
     for s in range(2):
         dkv_ref[s] = dk[s].astype(bf).reshape(8, half, head)
         dkv_ref[2 + s] = dv[s].astype(bf).reshape(8, half, head)
@@ -734,14 +909,14 @@
         out_specs=[vm] * 7,
         out_shape=[
             out((rows, width), bf), out((rows, width), f32), out((1, width), f32),
-            out((8, 4, rows, width // 8 + 128), bf), out((tok, cols), bf), out((4, 8, half, head), bf),
+            out((4, 4, rows, width // 4 + 128), bf), out((tok, cols), bf), out((4, 8, half, head), bf),
             out((8, head), f32),
         ],
         scratch_shapes=[
-            pltpu.VMEM((cols, width), bf), pltpu.VMEM((tok, width), bf), pltpu.VMEM((tok, cols), bf),
+            pltpu.VMEM((cols, width), bf), pltpu.VMEM((tok, width), bf), pltpu.VMEM((2 * cols // head, half, head), bf),
             pltpu.VMEM((2, 8 * half, head), f32), pltpu.VMEM((2, 8 * half, head), f32),
-            pltpu.VMEM((8, rows, width // 8 + 128), bf),
-            dma, dma((3,)), dma((4,)), dma((8,)), dma((8,)), dma((3,)), dma((4,)),
+            pltpu.VMEM((4, rows, width // 4 + 128), bf),
+            dma, dma((3,)), dma((4,)), dma((4,)), dma((4,)), dma((3,)), dma((4,)),
         ],
         compiler_params=pltpu.CompilerParams(
             collective_id=cid, has_side_effects=True, vmem_limit_bytes=52 * 2**20
@@ -752,11 +927,11 @@
 
 def tail_kernel(
     dkv_ref, qlow_ref, kraw_ref, kg_ref, cos_ref, sin_ref, wq_ref, wk_ref, wv_ref, x_ref, g1_ref,
-    gres_ref, layer_ref, vec_ref,
-    gin_ref, lout_ref, kvall_ref, qall_ref, vo_ref,
-    wq, xbuf, zbuf, zst, part, cbuf, ybuf, stage, vbuf, vpart, tbuf, gin, kvlow,
+    gres_ref, layer_ref, vec_ref, first_ref, out_part, router_part,
+    gin_ref, lout_ref, gq_ref, gkv_ref, gout_ref, grouter_ref, vo_ref,
+    wq, xbuf, zbuf, zst, part, cbuf, ybuf, stage, vbuf, vpart, tbuf, gin, qbuf, kvbuf, turned, osrc, obuf, rsrc, rbuf, qsrc, qgot, ksrc, kgot,
     wsem, xsend, xrecv, zsend, zrecv, csend, crecv, ysend, yrecv, send, recv, vsend, vrecv, tsend, trecv,
-    lsem, qsend, qrecv, ksend, krecv,
+    qsend, qrecv, ksend, krecv, esend, erecv,
 ):
     f32, bf = jnp.float32, jnp.bfloat16
     z, x, y, c = coords()
@@ -779,18 +954,42 @@
             src_ref=zst.at[zz], dst_ref=zbuf.at[slot], send_sem=zsend.at[zz],
             recv_sem=zrecv.at[slot], device_id=to, device_id_type=MESH)
 
-    tok = qlow_ref.shape[0]
-    queries = Spread(
-        lambda p: qall_ref.at[pl.ds(pl.multiple_of(p * tok, tok), tok)], qsend, qrecv, qlow_ref)
-    keys = Spread(
-        lambda p: kvall_ref.at[pl.ds(pl.multiple_of(p * tok, tok), tok)], ksend, krecv, kvlow)
-    mine = [
-        pltpu.make_async_copy(s.first, s.place(s.me), lsem.at[n]) for n, s in enumerate((queries, keys))
+    span = qlow_ref.shape[1] // 2
+    queries = [
+        Line(lambda zz, n=n: qbuf.at[n, zz], qsend.at[n], qrecv.at[n]) for n in range(2)
     ]
+    keys = Line(lambda zz: kvbuf.at[zz], ksend, krecv)
+    for n in range(2):
+        qbuf[n, z] = qlow_ref[:, n * span : (n + 1) * span]
     for k in range(4):
         xcopy(far_z(z, k)).start()
-    queries.start_x()
-    mine[0].start()
+    queries[0].start()
+
+    per = gq_ref.shape[0]
+    own_cols = pl.ds(pl.multiple_of(x * per, per), per)
+    far_cols = pl.ds(pl.multiple_of((1 - x) * per, per), per)
+
+    def swap(n, src, dst):
+        return pltpu.make_async_remote_copy(
+            src_ref=src, dst_ref=dst, send_sem=esend.at[n], recv_sem=erecv.at[n], device_id=X,
+            device_id_type=MESH)
+
+    swaps = [
+        swap(0, osrc, obuf), swap(1, rsrc, rbuf), swap(2, qsrc.at[0], qgot.at[0]),
+        swap(3, qsrc.at[1], qgot.at[1]), swap(4, ksrc, kgot),
+    ]
+    osrc[...] = out_part[:, far_cols].astype(bf)
+    rsrc[...] = router_part[far_cols].astype(bf)
+    swaps[0].start()
+    swaps[1].start()
+    turned[...] = first_ref[...].T
+
+    def query_part(n):
+        right = qbuf[n].reshape(turned.shape[1], span)
+        cols = slice(n * span, (n + 1) * span)
+        qsrc[n] = nn(turned[far_cols], right).astype(bf)
+        swaps[2 + n].start()
+        gq_ref[:, cols] = nn(turned[own_cols], right)
 
     def sum_z(k):
         zz = far_z(z, k)
@@ -831,8 +1030,9 @@
     first_a = nt(qlow_ref[two(1 - y)], wq[...])
     sum_z(1)
     first_b = nt(qlow_ref[two(y)], wq[...])
+    queries[0].pass_on(1)
     sum_z(2)
-    queries.start_z()
+    queries[1].start()
     xcopy(z).wait_recv()
     dkv = dkv_ref[:, ctx].astype(f32) + xbuf[z].astype(f32)
 
@@ -862,11 +1062,10 @@
     kgain = jnp.sum(dn * unit, axis=0, keepdims=True)
     cg = dn * kg_ref[...]
     klow = (rs * (cg - unit * jnp.mean(cg * unit, axis=1, keepdims=True))).astype(bf)
-    kvlow[:, :head] = klow
-    kvlow[:, head:] = vlow
-    keys.start_z()
-    keys.start_x()
-    mine[1].start()
+    kvbuf[z, :, :head] = klow
+    kvbuf[z, :, head:] = vlow
+    keys.start()
+    queries[0].pass_on(2)
 
     def ccopy(yy):
         return pltpu.make_async_remote_copy(
@@ -874,7 +1073,7 @@
             recv_sem=crecv.at[yy], device_id=C, device_id_type=MESH)
 
     def project(yy, first):
-        keys, vals = kvlow[two(yy), :head], kvlow[two(yy), head:]
+        keys, vals = kvbuf[z, two(yy), :head], kvbuf[z, two(yy), head:]
         part[two(yy)] = (first + nt(keys, wk_ref[...]) + nt(vals, wv_ref[...])).astype(bf)
         ccopy(yy).start()
 
@@ -885,7 +1084,7 @@
     yc = pltpu.make_async_remote_copy(
         src_ref=stage, dst_ref=ybuf, send_sem=ysend, recv_sem=yrecv, device_id=Y, device_id_type=MESH)
     yc.start()
-    queries.pass_on(1)
+    queries[1].pass_on(1)
     ccopy(y).wait_recv()
     gfirst = at(y, c)[...].astype(f32) + cbuf[y].astype(f32)
     own = pl.ds(pl.multiple_of((y * 2 + c) * rows, rows), rows)
@@ -898,6 +1097,8 @@
     cg = gfirst * g1_ref[...]
     gin[...] = (gres_ref[...] + rs * (cg - unit * jnp.mean(cg * unit, axis=1, keepdims=True))).astype(bf)
 
+    queries[0].pass_on(3)
+    query_part(0)
     keys.pass_on(1)
     pairs = [(gin, gin_ref), (layer_ref, lout_ref)]
 
@@ -913,12 +1114,12 @@
         cp(n, src, y, c, Y, 0).start()
         cp(n, src, y, c, C, 1).start()
         dst[own] = src[...]
-    per = width // 8
+    part_width = width // 8
     for i in range(8):
-        for j in range(per // 128):
-            lo = i * per + j * 128
+        for j in range(part_width // 128):
+            lo = i * part_width + j * 128
             vpart[i, j : j + 1] = gn1[:, lo : lo + 128]
-        vpart[i, per // 128 : 8] = vec_ref[i, per // 128 : 8]
+        vpart[i, part_width // 128 : 8] = vec_ref[i, part_width // 128 : 8]
         vpart[i, 7:8] = jnp.broadcast_to(kgain, (1, head))
 
     def vcopy(i):
@@ -929,7 +1130,7 @@
 
     for i in range(1, 8):
         vcopy(i).start()
-    queries.pass_on(2)
+    queries[1].pass_on(2)
     keys.pass_on(2)
     total = vpart[ctx]
     for i in range(1, 8):
@@ -948,8 +1149,17 @@
     for n, (src, dst) in enumerate(pairs):
         cp(n, src, 1 - y, c, Y, 0).wait_recv()
         cp(n, place(dst, 1 - y, c), 1 - y, c, C, 2).start()
+    swaps[0].wait_recv()
+    gout_ref[...] = out_part[:, own_cols] + obuf[...].astype(f32)
+    swaps[1].wait_recv()
+    grouter_ref[...] = router_part[own_cols] + rbuf[...].astype(f32)
+    queries[1].pass_on(3)
+    query_part(1)
     keys.pass_on(3)
-    queries.pass_on(3)
+    right = kvbuf[...].reshape(turned.shape[1], 2 * head)
+    ksrc[...] = nn(turned[far_cols], right).astype(bf)
+    swaps[4].start()
+    gkv_ref[...] = nn(turned[own_cols], right)
     for t in sums:
         t.wait_recv()
     vo_ref[...] = (tbuf[3] + tbuf[0]) + (tbuf[1] + tbuf[2])
@@ -963,11 +1173,15 @@
         t.wait_send()
     for i in range(1, 8):
         vcopy(i).wait_send()
-    for s in (keys, queries):
-        s.arrive()
-        s.finish()
-    for cp_own in mine:
-        cp_own.wait()
+    for line in (*queries, keys):
+        line.finish()
+    for n in range(2):
+        swaps[2 + n].wait_recv()
+        gq_ref[:, n * span : (n + 1) * span] += qgot[n].astype(f32)
+    swaps[4].wait_recv()
+    gkv_ref[...] += kgot[...].astype(f32)
+    for s in swaps:
+        s.wait_send()
     yc.wait_send()
     ccopy(0).wait_send()
     ccopy(1).wait_send()
@@ -979,10 +1193,11 @@
             zcopy(zz, up, zz).wait_send()
 
 
-def tail(dkv, qlow, kraw, kg, cos, sin, wq, wk, wv, x, g1, gres, layer, vec, cid):
+def tail(dkv, qlow, kraw, kg, cos, sin, wq, wk, wv, x, g1, gres, layer, vec, first, out_part, router_part, cid):
     tok, width = x.shape
     rows = gres.shape[0]
     half, head = dkv.shape[2:]
+    per = first.shape[1] // 2
     f32, bf = jnp.float32, jnp.bfloat16
     dma = pltpu.SemaphoreType.DMA
     vm, anywhere = pl.BlockSpec(memory_space=pltpu.VMEM), pl.BlockSpec(memory_space=pl.ANY)
@@ -995,26 +1210,170 @@
 
     return pl.pallas_call(
         tail_kernel,
-        in_specs=[vm] * 6 + [anywhere] + [vm] * 7,
-        out_specs=[vm] * 2 + [anywhere] * 2 + [vm],
+        in_specs=[vm] * 6 + [anywhere] + [vm] * 10,
+        out_specs=[vm] * 7,
         out_shape=[
-            out((tok, width), bf), out((tok, width), bf), out((8 * tok, 2 * head), bf),
-            out((8 * tok, qlow.shape[1]), bf), out((8, 128), f32),
+            out((tok, width), bf), out((tok, width), bf), out((per, qlow.shape[1]), f32),
+            out((per, 2 * head), f32), out((out_part.shape[0], per), f32),
+            out((per, router_part.shape[1]), f32), out((8, 128), f32),
         ],
         scratch_shapes=[
             mem(*wq.shape), mem(4, 4, half, head), mem(5, 4, half, head), mem(4, 4, half, head),
             mem(tok, width), mem(2, rows, width), mem(rows, width), mem(rows, width),
             mem(8, 8, 128, kind=f32), mem(8, 8, 128, kind=f32), mem(4, 8, 128, kind=f32), mem(rows, width),
-            mem(tok, 2 * head),
+            mem(2, 4, tok, qlow.shape[1] // 2), mem(4, tok, 2 * head), mem(2 * per, first.shape[0]),
+            mem(out_part.shape[0], per), mem(out_part.shape[0], per),
+            mem(per, router_part.shape[1]), mem(per, router_part.shape[1]),
+            mem(2, per, qlow.shape[1] // 2), mem(2, per, qlow.shape[1] // 2),
+            mem(per, 2 * head), mem(per, 2 * head),
             dma((1,)), dma((4,)), dma((4,)), dma((4,)), dma((5,)), dma((2,)), dma((2,)), dma, dma,
             dma((2, 3)), dma((2, 4)), dma((8,)), dma((8,)), dma((3,)), dma((3,)),
-            dma((2,)), dma((3, 8)), dma((8,)), dma((3, 8)), dma((8,)),
+            dma((2, 2, 4)), dma((2, 4)), dma((2, 4)), dma((4,)), dma((5,)), dma((5,)),
         ],
         compiler_params=pltpu.CompilerParams(
             collective_id=cid, has_side_effects=True, vmem_limit_bytes=52 * 2**20
         ),
         name="tail",
-    )(dkv, qlow, kraw, kg, cos, sin, wq, wk, wv, x, g1, gres, layer, vec)
+    )(dkv, qlow, kraw, kg, cos, sin, wq, wk, wv, x, g1, gres, layer, vec, first, out_part, router_part)
+
+
+def experts_kernel(
+    piece_ref, wg_ref, wu_ref, wd_ref, s_ref, t_ref,
+    all_ref, pair_ref, hs_ref, gl_ref, ul_ref, hst_ref, glt_ref, ult_ref,
+    land, mats, pairs, lows, turns,
+    gsem, gsend, grecv, msem, asem, psem, lsem, tsem,
+):
+    bf, f32 = jnp.bfloat16, jnp.float32
+    width = wg_ref.shape[1]
+    extra = t_ref.shape[1]
+    tok = 4 * piece_ref.shape[0]
+    weights = [pltpu.make_async_copy(r, mats.at[n], msem.at[n]) for n, r in enumerate((wg_ref, wu_ref, wd_ref))]
+    for cp in weights:
+        cp.start()
+    barrier_all()
+    gather = Gather(piece_ref, land, gsem, gsend, grecv)
+    gather.start()
+    z, x, y, c, ax, ay, bx, by = gather.at_me
+
+    def place_of(u):
+        return far_z(z, 3 - u // 2), x + (u % 2) * (1 - 2 * x)
+
+    def block_rows(u):
+        zz, xx = place_of(u)
+        return pl.ds(pl.multiple_of((zz * 2 + xx) * tok, tok), tok)
+
+    def results(u):
+        slot = u % 2
+        span = block_rows(u)
+        copies = [pltpu.make_async_copy(pairs.at[slot], pair_ref.at[span], psem.at[slot])]
+        for n, (ref, turned) in enumerate(((hs_ref, hst_ref), (gl_ref, glt_ref), (ul_ref, ult_ref))):
+            copies.append(pltpu.make_async_copy(lows.at[slot, n], ref.at[span], lsem.at[slot, n]))
+            copies.append(pltpu.make_async_copy(turns.at[slot, n], turned.at[:, span], tsem.at[slot, n]))
+        return copies
+
+    def whole(u):
+        span = block_rows(u)
+        return pltpu.make_async_copy(land.at[span], all_ref.at[span], asem.at[u])
+
+    gather.local().wait()
+
+    def step(u, carry):
+        zz, xx = place_of(u)
+        slot = u % 2
+
+        @pl.when(u % 2 == 0)
+        def _():
+            gather.from_a(zz)
+
+            @pl.when(u < 6)
+            def _():
+                gather.from_line(far_z(z, 2 - u // 2))
+
+            gather.from_b(zz, bx, by)
+
+        @pl.when(u % 2 == 1)
+        def _():
+            gather.from_b(zz, 1 - x, 1 - y)
+
+        for yy in range(2):
+            gather.wait(pid(zz, xx, yy, 1 - c))
+
+        whole(u).start()
+
+        @pl.when(u == 0)
+        def _():
+            for cp in weights:
+                cp.wait()
+
+        @pl.when(u > 1)
+        def _():
+            for cp in results(u - 2):
+                cp.wait()
+
+        rows = block_rows(u)
+        value = land[rows, :width]
+        spread = nn(land[rows, 2 * width :], s_ref[...])
+        gate = nt(value, mats[0])
+        up = nt(value, mats[1])
+        back = nt(land[rows, width : 2 * width], mats[2])
+        sig = 1.0 / (1.0 + jnp.exp(-gate))
+        silu = gate * sig
+        hidden = silu * up
+        hs = (hidden * spread).astype(bf)
+        prod = hidden * back
+        high = prod.astype(bf)
+        low = (prod - high.astype(f32)).astype(bf)
+        pairs[slot] = (nn(high, t_ref[...]) + nn(low, t_ref[...])).astype(bf)
+        grad = back * spread
+        gl = (grad * up * sig * (1.0 + gate * (1.0 - sig))).astype(bf)
+        ul = (grad * silu).astype(bf)
+        for n, v in enumerate((hs, gl, ul)):
+            lows[slot, n] = v
+            turns[slot, n] = v.T
+        for cp in results(u):
+            cp.start()
+        return carry
+
+    lax.fori_loop(0, 8, step, 0)
+    for u in (6, 7):
+        for cp in results(u):
+            cp.wait()
+    for u in range(8):
+        whole(u).wait()
+    gather.finish()
+
+
+def experts_forward(piece, wg, wu, wd, spread, pick, cid):
+    rows, wide = piece.shape
+    hid, width = wg.shape
+    n = 32 * rows
+    tok = 4 * rows
+    extra = pick.shape[1]
+    bf = jnp.bfloat16
+    dma = pltpu.SemaphoreType.DMA
+    vm, anywhere = pl.BlockSpec(memory_space=pltpu.VMEM), pl.BlockSpec(memory_space=pl.ANY)
+
+    def out(*shape):
+        return jax.ShapeDtypeStruct(shape, bf)
+
+    return pl.pallas_call(
+        experts_kernel,
+        in_specs=[anywhere] * 4 + [vm] * 2,
+        out_specs=[anywhere] * 8,
+        out_shape=[out(n, wide), out(n, extra)] + [out(n, hid)] * 3 + [out(hid, n)] * 3,
+        scratch_shapes=[
+            pltpu.VMEM((n, wide), bf), pltpu.VMEM((3, hid, width), bf), pltpu.VMEM((2, tok, extra), bf),
+            pltpu.VMEM((2, 3, tok, hid), bf), pltpu.VMEM((2, 3, hid, tok), bf),
+            dma, dma((5, 32)), dma((32,)), dma((3,)), dma((8,)), dma((2,)), dma((2, 3)), dma((2, 3)),
+        ],
+        compiler_params=pltpu.CompilerParams(
+            collective_id=cid, has_side_effects=True, vmem_limit_bytes=56 * 2**20
+        ),
+        cost_estimate=pl.CostEstimate(
+            flops=6 * n * width * hid, bytes_accessed=10 * n * width, transcendentals=n * hid
+        ),
+        name="experts_forward",
+    )(piece, wg, wu, wd, spread, pick)
 
 
 EPSILON = 1e-06
@@ -1040,7 +1399,7 @@
     return lax.dot_general(a, b, (((0,), (0,)), ((), ())), preferred_element_type=jnp.float32)
 
 
-def expert_kernel(x_ref, cot_ref, wg_ref, wu_ref, wd_ref, s_ref, t_ref, part_ref, gl_ref, ul_ref, hs_ref):
+def plain_expert_kernel(x_ref, cot_ref, wg_ref, wu_ref, wd_ref, s_ref, t_ref, part_ref, gl_ref, ul_ref, hs_ref):
     bf = jnp.bfloat16
     width = cot_ref.shape[1]
     x = x_ref[:, :width]
@@ -1079,7 +1438,7 @@
         return pl.BlockSpec(v.shape, lambda i: (0, 0), pipeline_mode=pl.Buffered(1))
 
     return pl.pallas_call(
-        expert_kernel,
+        plain_expert_kernel,
         grid=(n // block,),
         in_specs=[rows(wide), rows(width)]
         + [whole(v) for v in (gate_mat, up_mat, down_mat, spread_mat, pick_mat)],
@@ -1092,7 +1451,7 @@
         cost_estimate=pl.CostEstimate(
             flops=12 * n * width * hid, bytes_accessed=10 * n * width, transcendentals=n * hid
         ),
-        name="experts",
+        name="plain_experts",
     )(x_all, cot_all, gate_mat, up_mat, down_mat, spread_mat, pick_mat)
 
 
@@ -1115,17 +1474,18 @@
     put(gd_ref, hs_ref, cot_ref)
 
 
-def expert_grads(x_all, cot_all, gl, ul, hs, block=256):
-    n, width = cot_all.shape
+def expert_grads(x_all, cot_all, gl, ul, hs, width, first=0, block=256):
+    n = x_all.shape[0]
     hid = gl.shape[0]
     span = min(n, 2048)
     cols = pl.BlockSpec((span, block), lambda i, j: (j, i))
+    cots = pl.BlockSpec((span, block), lambda i, j: (j, i + first // block))
     rows = pl.BlockSpec((hid, span), lambda i, j: (0, j))
     out = pl.BlockSpec((hid, block), lambda i, j: (0, i))
     return pl.pallas_call(
         expert_grad_kernel,
         grid=(width // block, n // span),
-        in_specs=[cols, cols, rows, rows, rows],
+        in_specs=[cols, cots, rows, rows, rows],
         out_specs=[out] * 3,
         out_shape=[jax.ShapeDtypeStruct((hid, width), jnp.float32)] * 3,
         compiler_params=pltpu.CompilerParams(
@@ -1401,7 +1761,7 @@
     first_part = first_part + dotf(value_low, value_weight, ((1,), (1,)))
     grad_first = links.rs_tp(first_part.astype(BF))
     grad_first, gate_low = lax.optimization_barrier((grad_first, gate_low))
-    grads = expert_grads(second_all, cot_all, gate_low, up_low, hidden_low)
+    grads = expert_grads(second_all, cot_all, gate_low, up_low, hidden_low, model_width)
     grad_gate, grad_up = (
         v.reshape(own_experts, units, model_width).transpose(0, 2, 1) for v in grads[:2]
     )
@@ -1487,7 +1847,6 @@
         return v.reshape(1, -1)
 
     cot_own = own_rows(cotangent)
-    cot_all = lax.all_gather(cot_own, ("ctx", "tp"), axis=0, tiled=True)
 
     token_positions = positions_of(block_order, devices, block_len)
     query_pos = lax.dynamic_index_in_dim(token_positions, me, 0, keepdims=False).reshape(-1)
@@ -1497,16 +1856,11 @@
     sin = jnp.concatenate([-jnp.sin(angles), jnp.sin(angles)], axis=1)
     query_pos = jnp.broadcast_to(query_pos.astype(F32)[:, None], (tok_count, head_size))
     router_rows = w_router.T
-    router_rows = jnp.concatenate([router_rows, router_rows, jnp.zeros((2 * experts, model_width), BF)])
     _, query_raw, key_raw, query_rot, kv_all, attended, logs, residual, gates, piece, first_cols = front(
         tokens_in, row(norm1_gain), w_query, key_weight, value_weight, row(query_gain),
         row(key_gain), cos, sin, query_pos, key_pos, w_out, row(norm2_gain), router_rows,
-        own_rows(routes), 1,
-    )
-    second_all = ag32(piece, 3)
-    attended_all = lax.all_gather(attended, "ctx", axis=0, tiled=True)
-    all_tok = devices * tok_count
-    first_cols = first_cols.reshape(all_tok, -1)
+        routes.T, cotangent, 1,
+    )
 
     extra = 4 * experts
     column = jnp.arange(extra, dtype=jnp.int32)[:, None]
@@ -1516,20 +1870,28 @@
     gate_mat = w_gate.transpose(0, 2, 1).reshape(hid, model_width)
     up_mat = w_up.transpose(0, 2, 1).reshape(hid, model_width)
     down_mat = w_down.reshape(hid, model_width)
-    part, gate_low, up_low, hidden_low = expert_blocks(
-        second_all, cot_all, gate_mat, up_mat, down_mat, spread, pick.T
-    )
-    sums_own = reduce_all(part, 6)
+    all_rows, pair, hidden, gate_low, up_low, hidden_turned, gate_turned, up_turned = experts_forward(
+        piece, gate_mat, up_mat, down_mat, spread, pick.T, 3
+    )
+    sums_own, attended_line = reduce_experts(
+        hidden, gate_low, up_low, pair, down_mat, gate_mat, up_mat, attended, 6
+    )
     layer_piece, grad_residual, grad_norm2, back_cols, query_low, grad_kv, qgain_part = middle(
         sums_own, residual, gates, cot_own, row(norm2_gain), router_rows, w_out, query_rot, kv_all,
         logs, query_raw, row(query_gain), cos, sin, query_pos, key_pos, 7,
     )
 
-    back_cols = back_cols.reshape(all_tok, -1)
-    width_part = model_width // devices
-    grad_out = dotf(attended_all, back_cols[:, :width_part], ((0,), (0,)))
-    second_cols = lax.dynamic_slice_in_dim(second_all, me * width_part, width_part, axis=1)
-    grad_router = dotf(second_cols, back_cols[:, width_part : width_part + experts], ((0,), (0,)))
+    line_tok = 4 * tok_count
+    back_cols = back_cols.reshape(line_tok, -1)
+    line_cols = model_width // 4
+    out_part = dotf(
+        attended_line.reshape(line_tok, -1), back_cols[:, :line_cols], ((0,), (0,))
+    )
+    second_line = all_rows.reshape(4, 2, tok_count, -1)
+    second_line = lax.dynamic_slice(
+        second_line, (0, me % 2, 0, me // 2 * line_cols), (4, 1, tok_count, line_cols)
+    ).reshape(line_tok, line_cols)
+    router_part = dotf(second_line, back_cols[:, line_cols:], ((0,), (0,)))
     per = model_width // devices // 128
     vectors = jnp.concatenate(
         [
@@ -1540,15 +1902,15 @@
         ],
         axis=1,
     )
-    grad_input, layer_out, kv_low_all, query_low_all, total = tail(
+    grad_input, layer_out, grad_query, kv_grads, grad_out, grad_router, total = tail(
         grad_kv, query_low, key_raw, row(key_gain), cos, sin, w_query, key_weight, value_weight,
-        tokens_in, row(norm1_gain), grad_residual, layer_piece, vectors, 8,
-    )
-    grad_query = dotf(first_cols, query_low_all, ((0,), (0,)))
-    kv_grads = dotf(first_cols, kv_low_all, ((0,), (0,)))
+        tokens_in, row(norm1_gain), grad_residual, layer_piece, vectors,
+        first_cols.reshape(line_tok, -1), out_part, router_part, 8,
+    )
     grad_key = kv_grads[:, :head_size]
     grad_value = kv_grads[:, head_size:]
-    grads = expert_grads(second_all, cot_all, gate_low, up_low, hidden_low)
+    total, gate_turned = lax.optimization_barrier((total, gate_turned))
+    grads = expert_grads(all_rows, all_rows, gate_turned, up_turned, hidden_turned, model_width, model_width)
     grad_gate, grad_up = (
         v.reshape(own_experts, units, model_width).transpose(0, 2, 1) for v in grads[:2]
     )
@@ -1569,7 +1931,7 @@
         gain_of(7),
         grad_out,
         total[per : 2 * per].reshape(-1),
-        grad_router,
+        grad_router[:, :experts],
         grad_gate,
         grad_up,
         grad_down,

time: 444 us -> 382 us (0.86)
  Pallas kernels: 399 us -> 355 us
  between operations: 14.3 us -> 0.88 us
  matrix products: 10.8 us -> 5.25 us
    pallas_call x5 -> x4, Pallas kernels: 333 us -> 296 us  [the longest x1 93.9 us: experts_forward(): pl.pallas_call(experts_kernel, in_specs=[anywhere] * 4 + [vm] * 2, out_sp...]
    pallas_call x1, Pallas kernels: 38.8 us -> 31.6 us  [middle(): pl.pallas_call(middle_kernel, in_specs=[vm] * 6 + [anywhere] + [vm] * 9,...]
    dot_general x4 -> x2, matrix products: 10.8 us -> 5.25 us  [dotf(): return lax.dot_general(a, b, (dims, ((), ())), preferred_element_type=F32)]
  transfers between devices with their start and end apart: 2 -> 0, of which waited for: 0 -> 0; matrix products, arithmetic and copies ran while one was open for 4% -> 0% of each run, Pallas kernels for 84% -> 0%
where the time goes in v4:
time: 382 us; the launch traced here: 381 us
  Pallas kernels  355 us (93%)
  local copies, waits for them, and re-layouts  16.6 us (4%)
  matrix products  5.25 us (1%)
    pallas_call x1, Pallas kernels, experts_forward(): pl.pallas_call(experts_kernel, in_specs=[anywhere] * 4 + [vm] * 2, out_sp...  93.9 us
    pallas_call x1, Pallas kernels, reduce_experts(): pl.pallas_call(reduce_kernel, in_specs=[anywhere] * 8, out_specs=[pl.Bloc...  87.3 us
    pallas_call x1, Pallas kernels, tail(): pl.pallas_call(tail_kernel, in_specs=[vm] * 6 + [anywhere] + [vm] * 10, o...  69.1 us
    pallas_call x1, Pallas kernels, front(): pl.pallas_call(front_kernel, in_specs=[anywhere, vm] + [anywhere] * 3 + [...  46 us
    pallas_call x1, Pallas kernels, middle(): pl.pallas_call(middle_kernel, in_specs=[vm] * 6 + [anywhere] + [vm] * 9,...  31.6 us
    pallas_call x1, Pallas kernels, expert_grads(): pl.pallas_call(expert_grad_kernel, grid=(width // block, n // span), in_s...  26.8 us
    unnamed x46, local copies, waits for them, and re-layouts  11.3 us

profile of v4, /device:TPU:0, one launch (start us, length us, event | category | flops | bytes accessed | tf_op | source)
XLA Modules:
  0.0 381.3 jit_solution(10089034088578112788)
XLA Ops:
  3.2 0.9 copy-done.2
  4.1 0.7 copy-done.5
  4.8 0.7 copy-done.7
  5.5 0.7 copy-done.9
  7.5 46.0 %front.1 = (bf16[256,2048]{1,0:T(8,128)(2,1)}, f32[256,1024]{1,0:T(8,128)}, f32[256,128]{1,0:T(8,128)S(1)}, bf16[16,128,128]{2,1,0:T(8,128)(2,1)S(1)}, bf16[4,8,...) custom-call(bf16[256,2048]{1,0:T(8,128)(2,1)} %x_ref.3, ...), custom_call_target="tpu_custom_call" | custom-call | tf_op jit(solution)/shard_map/front/pallas_call | solution.py:752
  53.5 0.8 copy-done.4
  54.3 0.8 copy-done.14
  55.1 0.8 fusion.7.s_ref
  55.9 0.8 fusion.4.t_ref
  56.7 93.9 %experts_forward.1 = (bf16[2048,4224]{1,0:T(8,128)(2,1)}, bf16[2048,128]{1,0:T(8,128)(2,1)}, bf16[2048,768]{1,0:T(8,128)(2,1)}, bf16[2048,768]{1,0:T(8,128)(2,1)...) custom-call(bf16[64,4224]{1,0:T(8,128)(2,1)} %get-tuple-element.53.p, ...), custom_call_target="tpu_custom_call" | custom-call | flops 19327352832 | bytes 41943040 | tf_op jit(solution)/shard_map/experts_forward/pallas_call | solution.py:1359
  150.7 87.3 %reduce_experts.1 = (f32[64,4224]{1,0:T(8,128)}, bf16[4,256,1024]{2,1,0:T(8,128)(2,1)}) custom-call(bf16[2048,768]{1,0:T(8,128)(2,1)} %get-tuple-element.54.hs_ref, bf16[2048,768]{1,0:T(8,128)(2,1)} %get-tuple-element.55.gl_ref, bf16[2048,768]{1,0:T(8,128)(2,1)} %get-tuple-element.56.ul_ref, bf16[2048,128]{1,0:T(8,128)(2,1)} %get-tuple-element.57.pair_ref, ...), custom_call_target="tpu_custom_call" | custom-call | flops 19327352832 | bytes 41943040 | tf_op jit(solution)/shard_map/reduce_experts/pallas_call | solution.py:361
  238.0 1.0 constant_dynamic-slice_fusion.3.cot_ref
  239.1 31.6 %middle.1 = (bf16[64,2048]{1,0:T(8,128)(2,1)S(1)}, f32[64,2048]{1,0:T(8,128)S(1)}, f32[1,2048]{1,0:T(1,128)S(1)}, bf16[4,4,64,640]{3,2,1,0:T(8,128)(2,1)}, bf16[...) custom-call(f32[64,4224]{1,0:T(8,128)} %get-tuple-element.59.sums_ref, ...), custom_call_target="tpu_custom_call" | custom-call | tf_op jit(solution)/shard_map/middle/pallas_call | solution.py:906
  270.7 0.8 copy-done
  271.7 3.8 %fusion.out_part = f32[1024,512]{1,0:T(8,128)} fusion(bf16[1024,1024]{1,0:T(8,128)(2,1)S(1)} %bitcast.86, bf16[1024,640]{1,0:T(8,128)(2,1)} %bitcast.72), kind=kOutput, calls=%fused_computation | convolution fusion | flops 1073741824 | bytes 5242880 | tf_op jit(solution)/shard_map/dot_general | solution.py:1387
  275.5 1.4 constant_dynamic-slice_fusion.2
  276.9 1.4 fusion.5.router_part
  278.4 69.1 %tail.1 = (bf16[256,2048]{1,0:T(8,128)(2,1)}, bf16[256,2048]{1,0:T(8,128)(2,1)}, f32[256,1024]{1,0:T(8,128)}, f32[256,256]{1,0:T(8,128)S(1)}, f32[1024,256]{1,0:...) custom-call(bf16[4,8,128,128]{3,2,1,0:T(8,128)(2,1)} %get-tuple-element.66.dkv_ref, ...), custom_call_target="tpu_custom_call" | custom-call | tf_op jit(solution)/shard_map/tail/pallas_call | solution.py:1211
  348.0 0.7 fusion.17
  350.6 26.8 %expert_grads.1 = (f32[768,2048]{1,0:T(8,128)}, f32[768,2048]{1,0:T(8,128)}, f32[768,2048]{1,0:T(8,128)}) custom-call(bf16[2048,4224]{1,0:T(8,128)(2,1)} %get-tuple-element.76.x_ref.cot_ref, bf16[2048,4224]{1,0:T(8,128)(2,1)} %get-tuple-element.76.x_ref.cot_ref, bf16[768,2048]{1,0:T(8,128)(2,1)} %get-tuple-element.86.gl_ref, ...), custom_call_target="tpu_custom_call" | custom-call | flops 19327352832 | bytes 41943040 | tf_op jit(solution)/shard_map/expert_grads/pallas_call | solution.py:1485
  377.4 1.0 copy.39
  378.4 1.0 copy.40
  379.4 1.0 copy.41
  380.3 1.0 copy.42
  (60 shorter events, 6.5 us)
Async XLA Ops:
  3.2 0.9 copy-start.2
  4.1 0.7 copy-start.5
  4.8 0.7 copy-start.7
  5.5 0.7 copy-start.9
  6.2 0.7 copy-start.10
  6.8 0.7 copy-start.12
  53.5 0.8 copy-start.4
  54.3 0.8 copy-start.14
  150.7 88.3 %copy-start.3 = (bf16[2048,32]{0,1:T(8,128)(2,1)S(1)}, bf16[2048,32]{0,1:T(8,128)(2,1)}, u32[]{:S(2)}) copy-start(bf16[2048,32]{0,1:T(8,128)(2,1)} %param.27) | copy-start | bytes 393220
  150.7 88.3 %copy-start.6 = (f32[2048]{0:T(1024)S(1)}, f32[2048]{0:T(1024)}, u32[]{:S(2)}) copy-start(f32[2048]{0:T(1024)} %param.26) | copy-start | bytes 24580
  150.7 88.3 %copy-start.13 = (f32[128]{0:T(128)S(1)}, f32[128]{0:T(128)}, u32[]{:S(2)}) copy-start(f32[128]{0:T(128)} %param.23) | copy-start | bytes 1540
  239.0 32.6 %copy-start.19 = (bf16[4,256,1024]{2,1,0:T(8,128)(2,1)S(1)}, bf16[4,256,1024]{2,1,0:T(8,128)(2,1)}, u32[]{:S(2)}) copy-start(bf16[4,256,1024]{2,1,0:T(8,128)(2,1)} %get-tuple-element.74) | copy-start | bytes 6291460
  270.7 0.8 copy-start
  275.5 2.8 copy-start.1
  275.5 2.8 copy-start.8
  275.5 2.8 copy-start.11
  350.6 26.8 %copy-start.18 = (bf16[256,2048]{1,0:T(8,128)(2,1)S(1)}, bf16[256,2048]{1,0:T(8,128)(2,1)}, u32[]{:S(2)}) copy-start(bf16[256,2048]{1,0:T(8,128)(2,1)} %get-tuple-element.135) | copy-start | bytes 3145732
  350.6 27.8 %copy-start.17 = (bf16[256,2048]{1,0:T(8,128)(2,1)S(1)}, bf16[256,2048]{1,0:T(8,128)(2,1)}, u32[]{:S(2)}) copy-start(bf16[256,2048]{1,0:T(8,128)(2,1)} %get-tuple-element.136) | copy-start | bytes 3145732
  377.4 2.0 copy-start.16
  377.4 2.9 copy-start.15

commit v5 on v4

--- a/solution.py
+++ b/solution.py
@@ -1,4 +1,5 @@
 import math
+import functools
 import jax
 import jax.numpy as jnp
 from jax import lax
@@ -31,8 +32,8 @@
     pl.semaphore_wait(b,5-(3-z)//3-z//3)
 
 class Gather:
-    def __init__(self, own_ref, out_ref, lsem, send, recv):
-        self.own, self.out, self.lsem, self.send, self.recv = own_ref, out_ref, lsem, send, recv
+    def __init__(self, own_ref, out_ref, cols, send, recv):
+        self.own, self.out, self.cols, self.send, self.recv = own_ref, out_ref, cols, send, recv
         self.rows = own_ref.shape[0]
         z, x, y, c, ax, ay, bx, by = neighbours()
         self.at_me = (z, x, y, c, ax, ay, bx, by)
@@ -40,25 +41,19 @@
         self.A, self.B, self.C = dev(z, ax, ay, c), dev(z, bx, by, c), dev(z, x, y, 1 - c)
 
     def place(self, p):
-        return self.out.at[pl.ds(pl.multiple_of(p * self.rows, self.rows), self.rows)]
+        return self.out.at[pl.ds(pl.multiple_of(p * self.rows, self.rows), self.rows), self.cols]
 
     def copy(self, p, to, k, own=False):
         return pltpu.make_async_remote_copy(
-            src_ref=self.own if own else self.place(p), dst_ref=self.place(p),
+            src_ref=self.own.at[:, self.cols] if own else self.place(p), dst_ref=self.place(p),
             send_sem=self.send.at[k, p], recv_sem=self.recv.at[p], device_id=to, device_id_type=MESH)
 
     def wait(self, p):
         self.copy(p, self.C, 4).wait_recv()
-
-    def local(self):
-        z, x, y, c = self.at_me[:4]
-        return pltpu.make_async_copy(self.own, self.place(pid(z, x, y, c)), self.lsem)
 
     def start(self):
         z, x, y, c = self.at_me[:4]
         me = pid(z, x, y, c)
-        self.local().start()
-
         @pl.when(z < 3)
         def _():
             self.copy(me, self.up, 0, True).start()
@@ -173,6 +168,12 @@
             src_ref=part_rows(slot, yy, 1 - c), dst_ref=cbuf.at[i], send_sem=csend.at[slot, yy],
             recv_sem=crecv.at[i], device_id=C, device_id_type=MESH)
 
+    weights = [pltpu.make_async_copy(r, mats.at[n], msem.at[n]) for n, r in enumerate((wd_ref, wg_ref, wu_ref))]
+    for cp in weights:
+        cp.start()
+    for cp in loads(0):
+        cp.start()
+
     def products(u):
         slot = u % 2
         zz, xx = place_of(u)
@@ -190,6 +191,11 @@
                 ccopy(zz, xx, yy, slot).wait_send()
 
         blk[slot, :, :width] = nn(low[slot, 0], mats[0]).astype(blk.dtype)
+        @pl.when(u == 0)
+        def _():
+            weights[1].wait()
+            weights[2].wait()
+
         blk[slot, :, width : 2 * width] = (
             nn(low[slot, 1], mats[1]) + nn(low[slot, 2], mats[2])
         ).astype(blk.dtype)
@@ -282,20 +288,18 @@
                 zcopy(z, down, 4).wait_recv()
                 out_ref[...] += zbuf[4].astype(f32)
 
-    weights = [pltpu.make_async_copy(r, mats.at[n], msem.at[n]) for n, r in enumerate((wd_ref, wg_ref, wu_ref))]
-    for cp in weights:
-        cp.start()
-    for cp in loads(0):
-        cp.start()
     line = Line(lambda zz: line_ref.at[zz], nsend, nrecv, att_ref)
     mine = pltpu.make_async_copy(att_ref, line_ref.at[z], nsem)
     mine.start()
     barrier_all()
     line.start()
-    for cp in weights:
-        cp.wait()
+    weights[0].wait()
 
     def step(u, carry):
+        @pl.when(u == 1)
+        def _():
+            stage_b(0, 1)
+
         @pl.when(u < 8)
         def _():
             products(u)
@@ -307,7 +311,7 @@
 
         k = (u - 1) // 2
 
-        @pl.when((u > 0) & (u < 9) & (u % 2 == 1))
+        @pl.when((u > 1) & (u < 9) & (u % 2 == 1))
         def _():
             stage_b(k, 1)
 
@@ -580,10 +584,10 @@
 
 
 def front_kernel(
-    x_ref, g1_ref, wq_ref, wk_ref, wv_ref, qg_ref, kg_ref, cos_ref, sin_ref, qpos_ref, kpos_ref,
-    wo_ref, g2_ref, wr_ref, routes_ref, cot_ref,
+    x_ref, g1_in, wq_ref, wk_ref, wv_ref, qg_in, kg_in, cos_ref, sin_ref, qpos_ref, kpos_ref,
+    wo_ref, g2_in, wr_in, routes_in, cot_ref,
     first_ref, qraw_ref, kraw_ref, qrot_ref, kv_ref, att_ref, log_ref, res_ref, gates_ref, piece_ref, cols_ref,
-    xs, wk, wv, turned, wq, wo, part, cbuf, ybuf, stage, csrc,
+    xs, g1_ref, qg_ref, kg_ref, g2_ref, wr_ref, routes_ref, wk, wv, turned, wq, wo, part, cbuf, ybuf, stage, csrc,
     wsem, ksend, krecv, csend, crecv, ysend, yrecv, psend, precv, tsend, trecv,
 ):
     f32, bf = jnp.float32, jnp.bfloat16
@@ -593,25 +597,28 @@
     head = qg_ref.shape[1]
     heads = wq_ref.shape[1] // head
     half = x_ref.shape[0] // 2
-    xc, wkc, wvc, wqc, woc = (
+    fetched = [
         pltpu.make_async_copy(src, dst, wsem.at[n])
-        for n, (src, dst) in enumerate(((x_ref, xs), (wk_ref, wk), (wv_ref, wv), (wq_ref, wq), (wo_ref, wo)))
-    )
-    for cp in (xc, wkc, wvc, wqc, woc):
+        for n, (src, dst) in enumerate((
+            (x_ref, xs), (g1_in, g1_ref), (qg_in, qg_ref), (kg_in, kg_ref), (g2_in, g2_ref),
+            (wr_in, wr_ref), (routes_in, routes_ref), (wk_ref, wk), (wv_ref, wv), (wq_ref, wq), (wo_ref, wo),
+        ))
+    ]
+    for cp in fetched:
         cp.start()
+    wqc, woc = fetched[9:]
     own = pl.ds(pl.multiple_of((y * 2 + c) * rows, rows), rows)
     Y, C = dev(z, x, 1 - y, c), dev(z, x, y, 1 - c)
     barrier_wide()
-    cotc = pltpu.make_async_copy(cot_ref.at[own], piece_ref.at[:, x_ref.shape[1] : 2 * x_ref.shape[1]], wsem.at[5])
+    cotc = pltpu.make_async_copy(cot_ref.at[own], piece_ref.at[:, x_ref.shape[1] : 2 * x_ref.shape[1]], wsem.at[11])
     cotc.start()
+    for cp in fetched[:9]:
+        cp.wait()
     turned[...] = routes_ref[...].T
-    xc.wait()
     value = xs[...].astype(f32)
     first = (value * row_norm(value) * g1_ref[...]).astype(bf)
     first_ref[...] = first
     cos, sin = cos_ref[...], sin_ref[...]
-    wkc.wait()
-    wvc.wait()
     kraw = nn(first, wk[...])
     kraw_ref[...] = kraw
     krot = turn(kraw * row_norm(kraw) * kg_ref[...], cos, sin).astype(bf)
@@ -751,7 +758,7 @@
 
     return pl.pallas_call(
         front_kernel,
-        in_specs=[anywhere, vm] + [anywhere] * 3 + [vm] * 6 + [anywhere] + [vm] * 3 + [anywhere],
+        in_specs=[anywhere] * 7 + [vm] * 4 + [anywhere] * 5,
         out_specs=[vm] * 11,
         out_shape=[
             out((tok, width), bf), out((tok, cols), f32), out((tok, head), f32),
@@ -760,12 +767,14 @@
             out((rows, 2 * width + 128), bf), out((4, 4, rows, width // 4), bf),
         ],
         scratch_shapes=[
-            pltpu.VMEM((tok, width), bf), pltpu.VMEM((width, head), bf), pltpu.VMEM((width, head), bf),
+            pltpu.VMEM((tok, width), bf), pltpu.VMEM(g1.shape, f32), pltpu.VMEM(qg.shape, f32),
+            pltpu.VMEM(kg.shape, f32), pltpu.VMEM(g2.shape, f32), pltpu.VMEM(wr.shape, bf),
+            pltpu.VMEM(routes.shape, jnp.int32), pltpu.VMEM((width, head), bf), pltpu.VMEM((width, head), bf),
             pltpu.VMEM(routes.shape[::-1], jnp.int32),
             pltpu.VMEM((width, cols), bf), pltpu.VMEM((cols, width), bf), pltpu.VMEM((tok, width), bf),
             pltpu.VMEM((2, rows, width), bf), pltpu.VMEM((rows, width), bf), pltpu.VMEM((rows, width), bf),
             pltpu.VMEM((4, rows, width // 4), bf),
-            dma((6,)), dma((3, 8)), dma((8,)), dma((2,)), dma((2,)), dma, dma,
+            dma((12,)), dma((3, 8)), dma((8,)), dma((2,)), dma((2,)), dma, dma,
             dma((4,)), dma((4,)), dma((3,)), dma((4,)),
         ],
         compiler_params=pltpu.CompilerParams(
@@ -776,26 +785,35 @@
 
 
 def middle_kernel(
-    sums_ref, res_ref, gates_ref, cot_ref, g2_ref, wr_ref, wo_ref, qrot_ref, kv_ref, log_ref,
-    qraw_ref, qg_ref, cos_ref, sin_ref, qpos_ref, kpos_ref,
+    sums_ref, res_ref, gates_ref, cot_in, g2_in, wr_in, wo_ref, qrot_ref, kv_ref, log_ref,
+    qraw_ref, qg_in, cos_ref, sin_ref, qpos_ref, kpos_ref,
     layer_ref, gres_ref, gn2_ref, cols_ref, qlow_ref, dkv_ref, qgain_ref,
-    wo, back, mixed, dk, dv, csrc, wsem, send, recv, psend, precv, tsend, trecv,
+    cot_ref, g2_ref, wr_ref, qg_ref, wo, back, mixed, dk, dv, csrc, wsem, send, recv, psend, precv, tsend, trecv,
 ):
     f32, bf = jnp.float32, jnp.bfloat16
     z, x, y, c = coords()
     rows, width = res_ref.shape
-    experts = wr_ref.shape[0]
-    head = qg_ref.shape[1]
+    experts = wr_in.shape[0]
+    head = qg_in.shape[1]
     heads = qraw_ref.shape[1] // head
     half = qraw_ref.shape[0] // 2
-    woc = pltpu.make_async_copy(wo_ref, wo, wsem)
-    woc.start()
+    mine = pl.ds(pl.multiple_of((y * 2 + c) * rows, rows), rows)
+    fetched = [
+        pltpu.make_async_copy(src, dst, wsem.at[n])
+        for n, (src, dst) in enumerate((
+            (cot_in.at[mine], cot_ref), (g2_in, g2_ref), (wr_in, wr_ref), (qg_in, qg_ref), (wo_ref, wo)))
+    ]
+    for item in fetched:
+        item.start()
+    woc = fetched[4]
     barrier_wide()
     Y, C = dev(z, x, 1 - y, c), dev(z, x, y, 1 - c)
 
     def at(yy, cc):
         return back.at[pl.ds(pl.multiple_of((yy * 2 + cc) * rows, rows), rows)]
 
+    for item in fetched[:4]:
+        item.wait()
     res = res_ref[...]
     layer_ref[...] = (res + sums_ref[:, :width]).astype(bf)
     gates = gates_ref[...]
@@ -808,7 +826,6 @@
     cg = gsec * g2_ref[...]
     gres = cot_ref[...].astype(f32) + rs * (cg - unit * jnp.mean(cg * unit, axis=1, keepdims=True))
     gres_ref[...] = gres
-    mine = pl.ds(pl.multiple_of((y * 2 + c) * rows, rows), rows)
     glow = gres.astype(bf)
     back[mine] = glow
 
@@ -905,7 +922,7 @@
 
     return pl.pallas_call(
         middle_kernel,
-        in_specs=[vm] * 6 + [anywhere] + [vm] * 9,
+        in_specs=[vm] * 3 + [anywhere] * 4 + [vm] * 4 + [anywhere] + [vm] * 4,
         out_specs=[vm] * 7,
         out_shape=[
             out((rows, width), bf), out((rows, width), f32), out((1, width), f32),
@@ -913,10 +930,12 @@
             out((8, head), f32),
         ],
         scratch_shapes=[
+            pltpu.VMEM((rows, width), bf), pltpu.VMEM(g2.shape, f32), pltpu.VMEM(wr.shape, bf),
+            pltpu.VMEM(qg.shape, f32),
             pltpu.VMEM((cols, width), bf), pltpu.VMEM((tok, width), bf), pltpu.VMEM((2 * cols // head, half, head), bf),
             pltpu.VMEM((2, 8 * half, head), f32), pltpu.VMEM((2, 8 * half, head), f32),
             pltpu.VMEM((4, rows, width // 4 + 128), bf),
-            dma, dma((3,)), dma((4,)), dma((4,)), dma((4,)), dma((3,)), dma((4,)),
+            dma((5,)), dma((3,)), dma((4,)), dma((4,)), dma((4,)), dma((3,)), dma((4,)),
         ],
         compiler_params=pltpu.CompilerParams(
             collective_id=cid, has_side_effects=True, vmem_limit_bytes=52 * 2**20
@@ -926,10 +945,10 @@
 
 
 def tail_kernel(
-    dkv_ref, qlow_ref, kraw_ref, kg_ref, cos_ref, sin_ref, wq_ref, wk_ref, wv_ref, x_ref, g1_ref,
-    gres_ref, layer_ref, vec_ref, first_ref, out_part, router_part,
+    dkv_ref, qlow_ref, kraw_ref, kg_in, cos_ref, sin_ref, wq_ref, wk_in, wv_in, x_in, g1_in,
+    gres_ref, layer_ref, gn2_ref, qgain_ref, first_in, att_in, back_ref, rows_in,
     gin_ref, lout_ref, gq_ref, gkv_ref, gout_ref, grouter_ref, vo_ref,
-    wq, xbuf, zbuf, zst, part, cbuf, ybuf, stage, vbuf, vpart, tbuf, gin, qbuf, kvbuf, turned, osrc, obuf, rsrc, rbuf, qsrc, qgot, ksrc, kgot,
+    wq, kg_ref, wk_ref, wv_ref, x_ref, g1_ref, first_ref, att, second, att_t, xbuf, zbuf, zst, part, cbuf, ybuf, stage, vbuf, vpart, tbuf, gin, qbuf, kvbuf, turned, osrc, obuf, rsrc, rbuf, qsrc, qgot, ksrc, kgot, grouter_both,
     wsem, xsend, xrecv, zsend, zrecv, csend, crecv, ysend, yrecv, send, recv, vsend, vrecv, tsend, trecv,
     qsend, qrecv, ksend, krecv, esend, erecv,
 ):
@@ -938,8 +957,23 @@
     ctx, tp = lax.axis_index("ctx"), lax.axis_index("tp")
     rows, width = gres_ref.shape
     half, head = dkv_ref.shape[2:]
-    wqc = pltpu.make_async_copy(wq_ref, wq, wsem.at[0])
-    wqc.start()
+    line_cols = first_in.shape[1]
+    tok = x_in.shape[0]
+    fetched = [
+        pltpu.make_async_copy(src, dst, wsem.at[n])
+        for n, (src, dst) in enumerate((
+            (first_in, first_ref), (att_in, att), (wq_ref, wq), (kg_in, kg_ref), (wk_in, wk_ref),
+            (wv_in, wv_ref), (x_in, x_ref), (g1_in, g1_ref),
+            *(
+                (rows_in.at[pl.ds(pl.multiple_of((zz * 2 + x) * tok, tok), tok),
+                            pl.ds(pl.multiple_of(z * line_cols, line_cols), line_cols)],
+                 second.at[pl.ds(zz * tok, tok)])
+                for zz in range(4)
+            ),
+        ))
+    ]
+    for item in fetched:
+        item.start()
     X, Y, C, D = dev(z, 1 - x, y, c), dev(z, x, 1 - y, c), dev(z, x, y, 1 - c), dev(z, x, 1 - y, 1 - c)
     up, down = dev(z + 1, x, y, c), dev(z - 1, x, y, c)
     barrier_wide()
@@ -965,6 +999,21 @@
         xcopy(far_z(z, k)).start()
     queries[0].start()
 
+    pairs = [(gin, gin_ref), (layer_ref, lout_ref)]
+
+    def place(ref, yy, cc):
+        return ref.at[pl.ds(pl.multiple_of((yy * 2 + cc) * rows, rows), rows)]
+
+    def cp(n, src, yy, cc, to, k):
+        return pltpu.make_async_remote_copy(
+            src_ref=src, dst_ref=place(pairs[n][1], yy, cc), send_sem=send.at[n, k],
+            recv_sem=recv.at[n, yy * 2 + cc], device_id=to, device_id_type=MESH)
+
+    own = pl.ds(pl.multiple_of((y * 2 + c) * rows, rows), rows)
+    cp(1, layer_ref, y, c, Y, 0).start()
+    cp(1, layer_ref, y, c, C, 1).start()
+    lout_ref[own] = layer_ref[...]
+
     per = gq_ref.shape[0]
     own_cols = pl.ds(pl.multiple_of(x * per, per), per)
     far_cols = pl.ds(pl.multiple_of((1 - x) * per, per), per)
@@ -978,10 +1027,13 @@
         swap(0, osrc, obuf), swap(1, rsrc, rbuf), swap(2, qsrc.at[0], qgot.at[0]),
         swap(3, qsrc.at[1], qgot.at[1]), swap(4, ksrc, kgot),
     ]
-    osrc[...] = out_part[:, far_cols].astype(bf)
-    rsrc[...] = router_part[far_cols].astype(bf)
+    own_lanes = pl.ds(pl.multiple_of(x * per, 128), per)
+    far_lanes = pl.ds(pl.multiple_of((1 - x) * per, 128), per)
+    for item in fetched[:2]:
+        item.wait()
+    att_t[...] = att[...].T
+    osrc[...] = nn(att_t[...], back_ref[:, far_lanes]).astype(bf)
     swaps[0].start()
-    swaps[1].start()
     turned[...] = first_ref[...].T
 
     def query_part(n):
@@ -1026,13 +1078,19 @@
         return pl.ds(pl.multiple_of(yy * 2 * rows, 2 * rows), 2 * rows)
 
     sum_z(0)
-    wqc.wait()
+    for item in fetched[2:]:
+        item.wait()
     first_a = nt(qlow_ref[two(1 - y)], wq[...])
     sum_z(1)
     first_b = nt(qlow_ref[two(y)], wq[...])
     queries[0].pass_on(1)
     sum_z(2)
     queries[1].start()
+    router_part = tn(second[...], back_ref[:, line_cols:])
+    part_of = jnp.stack([router_part[:per], router_part[per:]])
+    grouter_both[...] = part_of
+    rsrc[...] = grouter_both[1 - x].astype(bf)
+    swaps[1].start()
     xcopy(z).wait_recv()
     dkv = dkv_ref[:, ctx].astype(f32) + xbuf[z].astype(f32)
 
@@ -1087,7 +1145,6 @@
     queries[1].pass_on(1)
     ccopy(y).wait_recv()
     gfirst = at(y, c)[...].astype(f32) + cbuf[y].astype(f32)
-    own = pl.ds(pl.multiple_of((y * 2 + c) * rows, rows), rows)
     value = x_ref[own].astype(f32)
     rs = row_norm(value)
     unit = value * rs
@@ -1100,27 +1157,18 @@
     queries[0].pass_on(3)
     query_part(0)
     keys.pass_on(1)
-    pairs = [(gin, gin_ref), (layer_ref, lout_ref)]
-
-    def place(ref, yy, cc):
-        return ref.at[pl.ds(pl.multiple_of((yy * 2 + cc) * rows, rows), rows)]
-
-    def cp(n, src, yy, cc, to, k):
-        return pltpu.make_async_remote_copy(
-            src_ref=src, dst_ref=place(pairs[n][1], yy, cc), send_sem=send.at[n, k],
-            recv_sem=recv.at[n, yy * 2 + cc], device_id=to, device_id_type=MESH)
-
-    for n, (src, dst) in enumerate(pairs):
-        cp(n, src, y, c, Y, 0).start()
-        cp(n, src, y, c, C, 1).start()
-        dst[own] = src[...]
+    cp(0, gin, y, c, Y, 0).start()
+    cp(0, gin, y, c, C, 1).start()
+    gin_ref[own] = gin[...]
     part_width = width // 8
+    qgain = jnp.sum(qgain_ref[...], axis=0, keepdims=True)
     for i in range(8):
         for j in range(part_width // 128):
             lo = i * part_width + j * 128
             vpart[i, j : j + 1] = gn1[:, lo : lo + 128]
-        vpart[i, part_width // 128 : 8] = vec_ref[i, part_width // 128 : 8]
-        vpart[i, 7:8] = jnp.broadcast_to(kgain, (1, head))
+            vpart[i, part_width // 128 + j : part_width // 128 + j + 1] = gn2_ref[:, lo : lo + 128]
+        vpart[i, 2 * part_width // 128 : 7] = jnp.broadcast_to(qgain, (7 - 2 * part_width // 128, head))
+        vpart[i, 7:8] = kgain
 
     def vcopy(i):
         to = (ctx + i) % 8
@@ -1150,9 +1198,9 @@
         cp(n, src, 1 - y, c, Y, 0).wait_recv()
         cp(n, place(dst, 1 - y, c), 1 - y, c, C, 2).start()
     swaps[0].wait_recv()
-    gout_ref[...] = out_part[:, own_cols] + obuf[...].astype(f32)
+    gout_ref[...] = nn(att_t[...], back_ref[:, own_lanes]) + obuf[...].astype(f32)
     swaps[1].wait_recv()
-    grouter_ref[...] = router_part[own_cols] + rbuf[...].astype(f32)
+    grouter_ref[...] = grouter_both[x] + rbuf[...].astype(f32)
     queries[1].pass_on(3)
     query_part(1)
     keys.pass_on(3)
@@ -1193,7 +1241,7 @@
             zcopy(zz, up, zz).wait_send()
 
 
-def tail(dkv, qlow, kraw, kg, cos, sin, wq, wk, wv, x, g1, gres, layer, vec, first, out_part, router_part, cid):
+def tail(dkv, qlow, kraw, kg, cos, sin, wq, wk, wv, x, g1, gres, layer, gn2, qgain, first, att, back, rows_all, cid):
     tok, width = x.shape
     rows = gres.shape[0]
     half, head = dkv.shape[2:]
@@ -1210,23 +1258,25 @@
 
     return pl.pallas_call(
         tail_kernel,
-        in_specs=[vm] * 6 + [anywhere] + [vm] * 10,
+        in_specs=[vm] * 3 + [anywhere] + [vm] * 2 + [anywhere] * 5 + [vm] * 4 + [anywhere] * 2 + [vm] + [anywhere],
         out_specs=[vm] * 7,
         out_shape=[
             out((tok, width), bf), out((tok, width), bf), out((per, qlow.shape[1]), f32),
-            out((per, 2 * head), f32), out((out_part.shape[0], per), f32),
-            out((per, router_part.shape[1]), f32), out((8, 128), f32),
+            out((per, 2 * head), f32), out((att.shape[1], per), f32),
+            out((per, 128), f32), out((8, 128), f32),
         ],
         scratch_shapes=[
-            mem(*wq.shape), mem(4, 4, half, head), mem(5, 4, half, head), mem(4, 4, half, head),
+            mem(*wq.shape), mem(*kg.shape, kind=f32), mem(*wk.shape), mem(*wv.shape), mem(*x.shape),
+            mem(*g1.shape, kind=f32), mem(*first.shape), mem(*att.shape), mem(*first.shape),
+            mem(att.shape[1], att.shape[0]), mem(4, 4, half, head), mem(5, 4, half, head), mem(4, 4, half, head),
             mem(tok, width), mem(2, rows, width), mem(rows, width), mem(rows, width),
             mem(8, 8, 128, kind=f32), mem(8, 8, 128, kind=f32), mem(4, 8, 128, kind=f32), mem(rows, width),
             mem(2, 4, tok, qlow.shape[1] // 2), mem(4, tok, 2 * head), mem(2 * per, first.shape[0]),
-            mem(out_part.shape[0], per), mem(out_part.shape[0], per),
-            mem(per, router_part.shape[1]), mem(per, router_part.shape[1]),
+            mem(att.shape[1], per), mem(att.shape[1], per),
+            mem(per, 128), mem(per, 128),
             mem(2, per, qlow.shape[1] // 2), mem(2, per, qlow.shape[1] // 2),
-            mem(per, 2 * head), mem(per, 2 * head),
-            dma((1,)), dma((4,)), dma((4,)), dma((4,)), dma((5,)), dma((2,)), dma((2,)), dma, dma,
+            mem(per, 2 * head), mem(per, 2 * head), mem(2, per, 128, kind=f32),
+            dma((12,)), dma((4,)), dma((4,)), dma((4,)), dma((5,)), dma((2,)), dma((2,)), dma, dma,
             dma((2, 3)), dma((2, 4)), dma((8,)), dma((8,)), dma((3,)), dma((3,)),
             dma((2, 2, 4)), dma((2, 4)), dma((2, 4)), dma((4,)), dma((5,)), dma((5,)),
         ],
@@ -1234,26 +1284,51 @@
             collective_id=cid, has_side_effects=True, vmem_limit_bytes=52 * 2**20
         ),
         name="tail",
-    )(dkv, qlow, kraw, kg, cos, sin, wq, wk, wv, x, g1, gres, layer, vec, first, out_part, router_part)
+    )(dkv, qlow, kraw, kg, cos, sin, wq, wk, wv, x, g1, gres, layer, gn2, qgain, first, att, back, rows_all)
 
 
 def experts_kernel(
-    piece_ref, wg_ref, wu_ref, wd_ref, s_ref, t_ref,
+    own,
+    piece_ref, wg_ref, wu_ref, wd_ref,
     all_ref, pair_ref, hs_ref, gl_ref, ul_ref, hst_ref, glt_ref, ult_ref,
-    land, mats, pairs, lows, turns,
+    land, mats, s_ref, t_ref, pairs, lows, turns,
     gsem, gsend, grecv, msem, asem, psem, lsem, tsem,
 ):
     bf, f32 = jnp.bfloat16, jnp.float32
     width = wg_ref.shape[1]
     extra = t_ref.shape[1]
+    hid = wg_ref.shape[0]
     tok = 4 * piece_ref.shape[0]
     weights = [pltpu.make_async_copy(r, mats.at[n], msem.at[n]) for n, r in enumerate((wg_ref, wu_ref, wd_ref))]
     for cp in weights:
         cp.start()
+    named = lax.axis_index("ctx") * own
+
+    def expert_of(index):
+        return named + sum((index >= e * hid // own).astype(jnp.int32) for e in range(1, own))
+
+    shape = s_ref.shape
+    expert = expert_of(lax.broadcasted_iota(jnp.int32, shape, 1))
+    place = lax.broadcasted_iota(jnp.int32, shape, 0)
+    s_ref[...] = ((place == expert) | (place == expert + extra // 4)).astype(f32).astype(bf)
+    expert = expert_of(lax.broadcasted_iota(jnp.int32, shape[::-1], 0))
+    place = lax.broadcasted_iota(jnp.int32, shape[::-1], 1)
+    t_ref[...] = (place == expert).astype(f32).astype(bf)
     barrier_all()
-    gather = Gather(piece_ref, land, gsem, gsend, grecv)
-    gather.start()
-    z, x, y, c, ax, ay, bx, by = gather.at_me
+    wide = piece_ref.shape[1]
+    cut = wide // 256 * 128
+    gathers = [
+        Gather(piece_ref, land, pl.ds(0, cut), gsend.at[0], grecv.at[0]),
+        Gather(piece_ref, land, pl.ds(cut, wide - cut), gsend.at[1], grecv.at[1]),
+    ]
+    for gather in gathers:
+        gather.start()
+    z, x, y, c, ax, ay, bx, by = gathers[0].at_me
+    rows = piece_ref.shape[0]
+    me = pid(z, x, y, c)
+    local = pltpu.make_async_copy(
+        piece_ref, land.at[pl.ds(pl.multiple_of(me * rows, rows), rows)], gsem)
+    local.start()
 
     def place_of(u):
         return far_z(z, 3 - u // 2), x + (u % 2) * (1 - 2 * x)
@@ -1275,7 +1350,7 @@
         span = block_rows(u)
         return pltpu.make_async_copy(land.at[span], all_ref.at[span], asem.at[u])
 
-    gather.local().wait()
+    local.wait()
 
     def step(u, carry):
         zz, xx = place_of(u)
@@ -1283,20 +1358,25 @@
 
         @pl.when(u % 2 == 0)
         def _():
-            gather.from_a(zz)
+            for gather in gathers:
+                gather.from_a(zz)
 
             @pl.when(u < 6)
             def _():
-                gather.from_line(far_z(z, 2 - u // 2))
-
-            gather.from_b(zz, bx, by)
+                for gather in gathers:
+                    gather.from_line(far_z(z, 2 - u // 2))
+
+            for gather in gathers:
+                gather.from_b(zz, bx, by)
 
         @pl.when(u % 2 == 1)
         def _():
-            gather.from_b(zz, 1 - x, 1 - y)
+            for gather in gathers:
+                gather.from_b(zz, 1 - x, 1 - y)
 
         for yy in range(2):
-            gather.wait(pid(zz, xx, yy, 1 - c))
+            for gather in gathers:
+                gather.wait(pid(zz, xx, yy, 1 - c))
 
         whole(u).start()
 
@@ -1340,31 +1420,33 @@
             cp.wait()
     for u in range(8):
         whole(u).wait()
-    gather.finish()
-
-
-def experts_forward(piece, wg, wu, wd, spread, pick, cid):
+    for gather in gathers:
+        gather.finish()
+
+
+def experts_forward(piece, wg, wu, wd, own, cid):
     rows, wide = piece.shape
     hid, width = wg.shape
     n = 32 * rows
     tok = 4 * rows
-    extra = pick.shape[1]
+    extra = wide - 2 * width
     bf = jnp.bfloat16
     dma = pltpu.SemaphoreType.DMA
-    vm, anywhere = pl.BlockSpec(memory_space=pltpu.VMEM), pl.BlockSpec(memory_space=pl.ANY)
+    anywhere = pl.BlockSpec(memory_space=pl.ANY)
 
     def out(*shape):
         return jax.ShapeDtypeStruct(shape, bf)
 
     return pl.pallas_call(
-        experts_kernel,
-        in_specs=[anywhere] * 4 + [vm] * 2,
+        functools.partial(experts_kernel, own),
+        in_specs=[anywhere] * 4,
         out_specs=[anywhere] * 8,
         out_shape=[out(n, wide), out(n, extra)] + [out(n, hid)] * 3 + [out(hid, n)] * 3,
         scratch_shapes=[
-            pltpu.VMEM((n, wide), bf), pltpu.VMEM((3, hid, width), bf), pltpu.VMEM((2, tok, extra), bf),
+            pltpu.VMEM((n, wide), bf), pltpu.VMEM((3, hid, width), bf), pltpu.VMEM((extra, hid), bf),
+            pltpu.VMEM((hid, extra), bf), pltpu.VMEM((2, tok, extra), bf),
             pltpu.VMEM((2, 3, tok, hid), bf), pltpu.VMEM((2, 3, hid, tok), bf),
-            dma, dma((5, 32)), dma((32,)), dma((3,)), dma((8,)), dma((2,)), dma((2, 3)), dma((2, 3)),
+            dma, dma((2, 5, 32)), dma((2, 32)), dma((3,)), dma((8,)), dma((2,)), dma((2, 3)), dma((2, 3)),
         ],
         compiler_params=pltpu.CompilerParams(
             collective_id=cid, has_side_effects=True, vmem_limit_bytes=56 * 2**20
@@ -1373,7 +1455,7 @@
             flops=6 * n * width * hid, bytes_accessed=10 * n * width, transcendentals=n * hid
         ),
         name="experts_forward",
-    )(piece, wg, wu, wd, spread, pick)
+    )(piece, wg, wu, wd)
 
 
 EPSILON = 1e-06
@@ -1840,13 +1922,9 @@
     own_experts, _, units = w_gate.shape
     hid = own_experts * units
 
-    def own_rows(v):
-        return lax.dynamic_slice_in_dim(v, tp_me * rows, rows, axis=0)
-
     def row(v):
         return v.reshape(1, -1)
 
-    cot_own = own_rows(cotangent)
 
     token_positions = positions_of(block_order, devices, block_len)
     query_pos = lax.dynamic_index_in_dim(token_positions, me, 0, keepdims=False).reshape(-1)
@@ -1862,51 +1940,28 @@
         routes.T, cotangent, 1,
     )
 
-    extra = 4 * experts
-    column = jnp.arange(extra, dtype=jnp.int32)[:, None]
-    named = me * own_experts + jnp.arange(hid, dtype=jnp.int32)[None, :] // units
-    pick = (column == named).astype(BF)
-    spread = pick + (column == named + experts).astype(BF)
     gate_mat = w_gate.transpose(0, 2, 1).reshape(hid, model_width)
     up_mat = w_up.transpose(0, 2, 1).reshape(hid, model_width)
     down_mat = w_down.reshape(hid, model_width)
     all_rows, pair, hidden, gate_low, up_low, hidden_turned, gate_turned, up_turned = experts_forward(
-        piece, gate_mat, up_mat, down_mat, spread, pick.T, 3
+        piece, gate_mat, up_mat, down_mat, own_experts, 3
     )
     sums_own, attended_line = reduce_experts(
         hidden, gate_low, up_low, pair, down_mat, gate_mat, up_mat, attended, 6
     )
     layer_piece, grad_residual, grad_norm2, back_cols, query_low, grad_kv, qgain_part = middle(
-        sums_own, residual, gates, cot_own, row(norm2_gain), router_rows, w_out, query_rot, kv_all,
+        sums_own, residual, gates, cotangent, row(norm2_gain), router_rows, w_out, query_rot, kv_all,
         logs, query_raw, row(query_gain), cos, sin, query_pos, key_pos, 7,
     )
 
     line_tok = 4 * tok_count
     back_cols = back_cols.reshape(line_tok, -1)
-    line_cols = model_width // 4
-    out_part = dotf(
-        attended_line.reshape(line_tok, -1), back_cols[:, :line_cols], ((0,), (0,))
-    )
-    second_line = all_rows.reshape(4, 2, tok_count, -1)
-    second_line = lax.dynamic_slice(
-        second_line, (0, me % 2, 0, me // 2 * line_cols), (4, 1, tok_count, line_cols)
-    ).reshape(line_tok, line_cols)
-    router_part = dotf(second_line, back_cols[:, line_cols:], ((0,), (0,)))
-    per = model_width // devices // 128
-    vectors = jnp.concatenate(
-        [
-            jnp.zeros((devices, per, 128), F32),
-            grad_norm2.reshape(devices, per, 128),
-            jnp.broadcast_to(jnp.sum(qgain_part, axis=0), (devices, 1, 128)),
-            jnp.zeros((devices, 7 - 2 * per, 128), F32),
-        ],
-        axis=1,
-    )
     grad_input, layer_out, grad_query, kv_grads, grad_out, grad_router, total = tail(
         grad_kv, query_low, key_raw, row(key_gain), cos, sin, w_query, key_weight, value_weight,
-        tokens_in, row(norm1_gain), grad_residual, layer_piece, vectors,
-        first_cols.reshape(line_tok, -1), out_part, router_part, 8,
-    )
+        tokens_in, row(norm1_gain), grad_residual, layer_piece, grad_norm2, qgain_part,
+        first_cols.reshape(line_tok, -1), attended_line.reshape(line_tok, -1), back_cols, all_rows, 8,
+    )
+    per = model_width // devices // 128
     grad_key = kv_grads[:, :head_size]
     grad_value = kv_grads[:, head_size:]
     total, gate_turned = lax.optimization_barrier((total, gate_turned))

time: 382 us -> 365 us (0.955)
  Pallas kernels: 355 us -> 348 us
  matrix products: 5.25 us -> 0 us
    pallas_call x4, Pallas kernels: 241 us -> 235 us  [the longest x1 91.2 us: experts_forward(): pl.pallas_call(functools.partial(experts_kernel, own), in_specs=[anywhere...]
    dot_general x2 -> x0, matrix products: 5.25 us -> none  [dotf(): return lax.dot_general(a, b, (dims, ((), ())), preferred_element_type=F32)]
    unnamed x46 -> x42, local copies, waits for them, and re-layouts: 11.3 us -> 11.3 us
where the time goes in v5:
time: 365 us
  Pallas kernels  348 us (95%)
  local copies, waits for them, and re-layouts  14.2 us (4%)
    pallas_call x1, Pallas kernels, experts_forward(): pl.pallas_call(functools.partial(experts_kernel, own), in_specs=[anywhere...  91.2 us
    pallas_call x1, Pallas kernels, reduce_experts(): pl.pallas_call(reduce_kernel, in_specs=[anywhere] * 8, out_specs=[pl.Bloc...  86 us
    pallas_call x1, Pallas kernels, tail(): pl.pallas_call(tail_kernel, in_specs=[vm] * 3 + [anywhere] + [vm] * 2 + [...  67.9 us
    pallas_call x1, Pallas kernels, front(): pl.pallas_call(front_kernel, in_specs=[anywhere] * 7 + [vm] * 4 + [anywhe...  46 us
    pallas_call x1, Pallas kernels, middle(): pl.pallas_call(middle_kernel, in_specs=[vm] * 3 + [anywhere] * 4 + [vm] *...  30.1 us
    pallas_call x1, Pallas kernels, expert_grads(): pl.pallas_call(expert_grad_kernel, grid=(width // block, n // span), in_s...  26.8 us
    unnamed x42, local copies, waits for them, and re-layouts  11.3 us

profile of v5, /device:TPU:0, one launch (start us, length us, event | category | flops | bytes accessed | tf_op | source)
XLA Modules:
  0.0 365.0 jit_solution(1668450671789657710)
XLA Ops:
  0.7 0.7 fusion.1
  1.3 0.7 add_multiply_fusion
  3.2 0.9 copy-done.1
  4.1 0.7 copy-done.4
  4.8 0.7 copy-done.6
  5.5 0.7 copy-done.8
  6.2 0.7 copy-done.9
  6.8 0.7 copy-done.11
  7.5 46.0 %front.1 = (bf16[256,2048]{1,0:T(8,128)(2,1)}, f32[256,1024]{1,0:T(8,128)}, f32[256,128]{1,0:T(8,128)S(1)}, bf16[16,128,128]{2,1,0:T(8,128)(2,1)S(1)}, bf16[4,8,...) custom-call(bf16[256,2048]{1,0:T(8,128)(2,1)} %x_in.1, ...), custom_call_target="tpu_custom_call" | custom-call | tf_op jit(solution)/shard_map/front/pallas_call | solution.py:759
  53.5 0.8 copy-done.3
  54.3 0.8 copy-done.13
  55.0 91.2 %experts_forward.1 = (bf16[2048,4224]{1,0:T(8,128)(2,1)}, bf16[2048,128]{1,0:T(8,128)(2,1)}, bf16[2048,768]{1,0:T(8,128)(2,1)}, bf16[2048,768]{1,0:T(8,128)(2,1)...) custom-call(bf16[64,4224]{1,0:T(8,128)(2,1)} %get-tuple-element.53.p, ...), custom_call_target="tpu_custom_call" | custom-call | flops 19327352832 | bytes 41943040 | tf_op jit(solution)/shard_map/experts_forward/pallas_call | solution.py:1440
  146.3 86.0 %reduce_experts.1 = (f32[64,4224]{1,0:T(8,128)}, bf16[4,256,1024]{2,1,0:T(8,128)(2,1)}) custom-call(bf16[2048,768]{1,0:T(8,128)(2,1)} %get-tuple-element.54.hs_ref, bf16[2048,768]{1,0:T(8,128)(2,1)} %get-tuple-element.55.gl_ref, bf16[2048,768]{1,0:T(8,128)(2,1)} %get-tuple-element.56.ul_ref, bf16[2048,128]{1,0:T(8,128)(2,1)} %get-tuple-element.57.pair_ref, ...), custom_call_target="tpu_custom_call" | custom-call | flops 19327352832 | bytes 41943040 | tf_op jit(solution)/shard_map/reduce_experts/pallas_call | solution.py:365
  232.3 30.1 %middle.1 = (bf16[64,2048]{1,0:T(8,128)(2,1)S(1)}, f32[64,2048]{1,0:T(8,128)S(1)}, f32[1,2048]{1,0:T(1,128)S(1)}, bf16[4,4,64,640]{3,2,1,0:T(8,128)(2,1)}, bf16[...) custom-call(f32[64,4224]{1,0:T(8,128)} %get-tuple-element.59.sums_ref, ...), custom_call_target="tpu_custom_call" | custom-call | tf_op jit(solution)/shard_map/middle/pallas_call | solution.py:923
  262.5 0.8 copy-done
  263.2 67.9 %tail.1 = (bf16[256,2048]{1,0:T(8,128)(2,1)}, bf16[256,2048]{1,0:T(8,128)(2,1)}, f32[256,1024]{1,0:T(8,128)}, f32[256,256]{1,0:T(8,128)S(1)}, f32[1024,256]{1,0:...) custom-call(bf16[4,8,128,128]{3,2,1,0:T(8,128)(2,1)} %get-tuple-element.66.dkv_ref, ...), custom_call_target="tpu_custom_call" | custom-call | tf_op jit(solution)/shard_map/tail/pallas_call | solution.py:1259
  331.7 0.7 fusion.4
  332.4 0.6 fusion.2
  333.6 0.7 copy.31
  334.3 26.8 %expert_grads.1 = (f32[768,2048]{1,0:T(8,128)}, f32[768,2048]{1,0:T(8,128)}, f32[768,2048]{1,0:T(8,128)}) custom-call(bf16[2048,4224]{1,0:T(8,128)(2,1)} %get-tuple-element.76.rows_in.x_ref.cot_ref, bf16[2048,4224]{1,0:T(8,128)(2,1)} %get-tuple-element.76.rows_in.x_ref.cot_ref, bf16[768,2048]{1,0:T(8,128)(2,1)} %get-tuple-element.86.gl_ref, ...), custom_call_target="tpu_custom_call" | custom-call | flops 19327352832 | bytes 41943040 | tf_op jit(solution)/shard_map/expert_grads/pallas_call | solution.py:1567
  361.1 1.0 copy.39
  362.1 1.0 copy.40
  363.1 1.0 copy.41
  364.0 1.0 copy.42
  (42 shorter events, 2.4 us)
Async XLA Ops:
  3.2 0.9 copy-start.1
  4.1 0.7 copy-start.4
  4.8 0.7 copy-start.6
  5.5 0.7 copy-start.8
  6.2 0.7 copy-start.9
  6.8 0.7 copy-start.11
  53.5 0.8 copy-start.3
  54.3 0.8 copy-start.13
  146.2 86.0 %copy-start.2 = (bf16[2048,32]{0,1:T(8,128)(2,1)S(1)}, bf16[2048,32]{0,1:T(8,128)(2,1)}, u32[]{:S(2)}) copy-start(bf16[2048,32]{0,1:T(8,128)(2,1)} %param.27) | copy-start | bytes 393220
  146.2 86.0 %copy-start.5 = (f32[2048]{0:T(1024)S(1)}, f32[2048]{0:T(1024)}, u32[]{:S(2)}) copy-start(f32[2048]{0:T(1024)} %param.26) | copy-start | bytes 24580
  146.3 86.0 %copy-start.10 = (f32[128]{0:T(128)S(1)}, f32[128]{0:T(128)}, u32[]{:S(2)}) copy-start(f32[128]{0:T(128)} %param.23) | copy-start | bytes 1540
  232.3 31.0 %copy-start.7 = (f32[2048]{0:T(1024)S(1)}, f32[2048]{0:T(1024)}, u32[]{:S(2)}) copy-start(f32[2048]{0:T(1024)} %param.19) | copy-start | bytes 24580
  232.3 31.0 %copy-start.12 = (f32[128]{0:T(128)S(1)}, f32[128]{0:T(128)}, u32[]{:S(2)}) copy-start(f32[128]{0:T(128)} %param.24) | copy-start | bytes 1540
  262.4 0.8 copy-start
  334.3 26.8 %copy-start.17 = (bf16[256,2048]{1,0:T(8,128)(2,1)S(1)}, bf16[256,2048]{1,0:T(8,128)(2,1)}, u32[]{:S(2)}) copy-start(bf16[256,2048]{1,0:T(8,128)(2,1)} %get-tuple-element.133) | copy-start | bytes 3145732
  334.3 27.8 %copy-start.16 = (bf16[256,2048]{1,0:T(8,128)(2,1)S(1)}, bf16[256,2048]{1,0:T(8,128)(2,1)}, u32[]{:S(2)}) copy-start(bf16[256,2048]{1,0:T(8,128)(2,1)} %get-tuple-element.134) | copy-start | bytes 3145732
  361.1 2.0 copy-start.15
  361.1 2.9 copy-start.14

commit v6 on v5

--- a/solution.py
+++ b/solution.py
@@ -37,7 +37,7 @@
         self.rows = own_ref.shape[0]
         z, x, y, c, ax, ay, bx, by = neighbours()
         self.at_me = (z, x, y, c, ax, ay, bx, by)
-        self.up, self.down = dev(z + 1, x, y, c), dev(z - 1, x, y, c)
+        self.up, self.down = dev(z + 1 - z // 3, x, y, c), dev(z - 1 + (3 - z) // 3, x, y, c)
         self.A, self.B, self.C = dev(z, ax, ay, c), dev(z, bx, by, c), dev(z, x, y, 1 - c)
 
     def place(self, p):
@@ -141,7 +141,7 @@
     z, x, y, c, ax, ay, bx, by = neighbours()
     dx, dy = 1 - x, 1 - y
     A, B, C = dev(z, ax, ay, c), dev(z, bx, by, c), dev(z, x, y, 1 - c)
-    up, down = dev(z + 1, x, y, c), dev(z - 1, x, y, c)
+    up, down = dev(z + 1 - z // 3, x, y, c), dev(z - 1 + (3 - z) // 3, x, y, c)
     tok = 4 * rows
 
     def q(zz, xx, yy):
@@ -451,7 +451,7 @@
         self.place, self.send, self.recv, self.first = place, send, recv, first
         z, x, y, c = coords()
         self.z = z
-        self.up, self.down = dev(z + 1, x, y, c), dev(z - 1, x, y, c)
+        self.up, self.down = dev(z + 1 - z // 3, x, y, c), dev(z - 1 + (3 - z) // 3, x, y, c)
 
     def copy(self, zz, to, k, own=False):
         src = self.first if own and self.first is not None else self.place(zz)
@@ -505,7 +505,7 @@
         z, x, y, c = coords()
         self.z, self.x = z, x
         self.X = dev(z, 1 - x, y, c)
-        self.up, self.down = dev(z + 1, x, y, c), dev(z - 1, x, y, c)
+        self.up, self.down = dev(z + 1 - z // 3, x, y, c), dev(z - 1 + (3 - z) // 3, x, y, c)
         self.me = z * 2 + x
 
     def copy(self, p, to, k, own=False):
@@ -778,7 +778,7 @@
             dma((4,)), dma((4,)), dma((3,)), dma((4,)),
         ],
         compiler_params=pltpu.CompilerParams(
-            collective_id=cid, has_side_effects=True, vmem_limit_bytes=52 * 2**20
+            collective_id=cid, has_side_effects=True, vmem_limit_bytes=60 * 2**20
         ),
         name="front",
     )(x, g1, wq, wk, wv, qg, kg, cos, sin, qpos, kpos, wo, g2, wr, routes, cot)
@@ -975,7 +975,7 @@
     for item in fetched:
         item.start()
     X, Y, C, D = dev(z, 1 - x, y, c), dev(z, x, 1 - y, c), dev(z, x, y, 1 - c), dev(z, x, 1 - y, 1 - c)
-    up, down = dev(z + 1, x, y, c), dev(z - 1, x, y, c)
+    up, down = dev(z + 1 - z // 3, x, y, c), dev(z - 1 + (3 - z) // 3, x, y, c)
     barrier_wide()
 
     def xcopy(zz):
@@ -1360,14 +1360,12 @@
         def _():
             for gather in gathers:
                 gather.from_a(zz)
+                gather.from_b(zz, bx, by)
 
             @pl.when(u < 6)
             def _():
                 for gather in gathers:
                     gather.from_line(far_z(z, 2 - u // 2))
-
-            for gather in gathers:
-                gather.from_b(zz, bx, by)
 
         @pl.when(u % 2 == 1)
         def _():
@@ -1449,7 +1447,7 @@
             dma, dma((2, 5, 32)), dma((2, 32)), dma((3,)), dma((8,)), dma((2,)), dma((2, 3)), dma((2, 3)),
         ],
         compiler_params=pltpu.CompilerParams(
-            collective_id=cid, has_side_effects=True, vmem_limit_bytes=56 * 2**20
+            collective_id=cid, has_side_effects=True, vmem_limit_bytes=60 * 2**20
         ),
         cost_estimate=pl.CostEstimate(
             flops=6 * n * width * hid, bytes_accessed=10 * n * width, transcendentals=n * hid

time: 365 us -> 363 us (level)
  local copies, waits for them, and re-layouts: 14.2 us -> 9.59 us
    unnamed x42 -> x38, local copies, waits for them, and re-layouts: 11.3 us -> 6.04 us
where the time goes in v6:
time: 363 us; the launch traced here: 362 us
  Pallas kernels  349 us (96%)
  local copies, waits for them, and re-layouts  9.59 us (3%)
    pallas_call x1, Pallas kernels, experts_forward(): pl.pallas_call(functools.partial(experts_kernel, own), in_specs=[anywhere...  90.6 us
    pallas_call x1, Pallas kernels, reduce_experts(): pl.pallas_call(reduce_kernel, in_specs=[anywhere] * 8, out_specs=[pl.Bloc...  85.6 us
    pallas_call x1, Pallas kernels, tail(): pl.pallas_call(tail_kernel, in_specs=[vm] * 3 + [anywhere] + [vm] * 2 + [...  67.2 us
    pallas_call x1, Pallas kernels, front(): pl.pallas_call(front_kernel, in_specs=[anywhere] * 7 + [vm] * 4 + [anywhe...  47.2 us
    pallas_call x1, Pallas kernels, middle(): pl.pallas_call(middle_kernel, in_specs=[vm] * 3 + [anywhere] * 4 + [vm] *...  31.7 us
    pallas_call x1, Pallas kernels, expert_grads(): pl.pallas_call(expert_grad_kernel, grid=(width // block, n // span), in_s...  26.8 us

profile of v6, /device:TPU:0, one launch (start us, length us, event | category | flops | bytes accessed | tf_op | source)
XLA Modules:
  0.0 362.3 jit_solution(9574108265547271294)
XLA Ops:
  0.7 0.7 fusion.1
  1.3 0.7 add_multiply_fusion
  2.0 0.1 copy.30
  2.2 0.1 add.29
  2.4 0.5 fusion
  2.9 0.8 pad_maximum_fusion
  3.8 0.8 broadcast_in_dim.2.qpos_ref
  4.5 0.6 copy.34
  5.1 47.2 %front.1 = (bf16[256,2048]{1,0:T(8,128)(2,1)}, f32[256,1024]{1,0:T(8,128)}, f32[256,128]{1,0:T(8,128)}, bf16[16,128,128]{2,1,0:T(8,128)(2,1)}, bf16[4,8,128,128]...) custom-call(bf16[256,2048]{1,0:T(8,128)(2,1)} %x_in.1, ...), custom_call_target="tpu_custom_call" | custom-call | tf_op jit(solution)/shard_map/front/pallas_call | solution.py:759
  52.3 90.6 %experts_forward.1 = (bf16[2048,4224]{1,0:T(8,128)(2,1)}, bf16[2048,128]{1,0:T(8,128)(2,1)}, bf16[2048,768]{1,0:T(8,128)(2,1)}, bf16[2048,768]{1,0:T(8,128)(2,1)...) custom-call(bf16[64,4224]{1,0:T(8,128)(2,1)} %get-tuple-element.53.p, ...), custom_call_target="tpu_custom_call" | custom-call | flops 19327352832 | bytes 41943040 | tf_op jit(solution)/shard_map/experts_forward/pallas_call | solution.py:1438
  143.0 85.6 %reduce_experts.1 = (f32[64,4224]{1,0:T(8,128)}, bf16[4,256,1024]{2,1,0:T(8,128)(2,1)}) custom-call(bf16[2048,768]{1,0:T(8,128)(2,1)} %get-tuple-element.54.hs_ref, bf16[2048,768]{1,0:T(8,128)(2,1)} %get-tuple-element.55.gl_ref, bf16[2048,768]{1,0:T(8,128)(2,1)} %get-tuple-element.56.ul_ref, bf16[2048,128]{1,0:T(8,128)(2,1)} %get-tuple-element.57.pair_ref, ...), custom_call_target="tpu_custom_call" | custom-call | flops 19327352832 | bytes 41943040 | tf_op jit(solution)/shard_map/reduce_experts/pallas_call | solution.py:365
  228.7 31.7 %middle.1 = (bf16[64,2048]{1,0:T(8,128)(2,1)S(1)}, f32[64,2048]{1,0:T(8,128)S(1)}, f32[1,2048]{1,0:T(1,128)S(1)}, bf16[4,4,64,640]{3,2,1,0:T(8,128)(2,1)}, bf16[...) custom-call(f32[64,4224]{1,0:T(8,128)} %get-tuple-element.59.sums_ref, ...), custom_call_target="tpu_custom_call" | custom-call | tf_op jit(solution)/shard_map/middle/pallas_call | solution.py:923
  260.4 0.8 copy-done.3
  261.2 67.2 %tail.1 = (bf16[256,2048]{1,0:T(8,128)(2,1)}, bf16[256,2048]{1,0:T(8,128)(2,1)}, f32[256,1024]{1,0:T(8,128)}, f32[256,256]{1,0:T(8,128)S(1)}, f32[1024,256]{1,0:...) custom-call(bf16[4,8,128,128]{3,2,1,0:T(8,128)(2,1)} %get-tuple-element.66.dkv_ref, ...), custom_call_target="tpu_custom_call" | custom-call | tf_op jit(solution)/shard_map/tail/pallas_call | solution.py:1259
  328.4 0.6 slice_bitcast_fusion
  329.0 0.7 fusion.4
  329.7 0.6 fusion.2
  330.3 0.6 fusion.3
  330.9 0.7 copy.31
  331.6 26.8 %expert_grads.1 = (f32[768,2048]{1,0:T(8,128)}, f32[768,2048]{1,0:T(8,128)}, f32[768,2048]{1,0:T(8,128)}) custom-call(bf16[2048,4224]{1,0:T(8,128)(2,1)} %get-tuple-element.76.rows_in.x_ref.cot_ref, bf16[2048,4224]{1,0:T(8,128)(2,1)} %get-tuple-element.76.rows_in.x_ref.cot_ref, bf16[768,2048]{1,0:T(8,128)(2,1)} %get-tuple-element.86.gl_ref, ...), custom_call_target="tpu_custom_call" | custom-call | flops 19327352832 | bytes 41943040 | tf_op jit(solution)/shard_map/expert_grads/pallas_call | solution.py:1565
  358.4 1.0 copy.39
  359.4 1.0 copy.40
  360.3 1.0 copy.41
  361.3 1.0 copy.42
  (38 shorter events, 0.3 us)
Async XLA Ops:
  142.9 85.7 %copy-start = (f32[256,128]{1,0:T(8,128)S(1)}, f32[256,128]{1,0:T(8,128)}, u32[]{:S(2)}) copy-start(f32[256,128]{1,0:T(8,128)} %get-tuple-element.117.cos_ref) | copy-start | bytes 393220
  142.9 85.7 %copy-start.1 = (f32[256,128]{1,0:T(8,128)S(1)}, f32[256,128]{1,0:T(8,128)}, u32[]{:S(2)}) copy-start(f32[256,128]{1,0:T(8,128)} %get-tuple-element.118.sin_ref) | copy-start | bytes 393220
  142.9 85.7 %copy-start.2 = (f32[256,128]{1,0:T(8,128)S(1)}, f32[256,128]{1,0:T(8,128)}, u32[]{:S(2)}) copy-start(f32[256,128]{1,0:T(8,128)} %broadcast_in_dim.2.qpos_ref) | copy-start | bytes 393220
  142.9 85.7 %copy-start.4 = (bf16[2048,32]{0,1:T(8,128)(2,1)S(1)}, bf16[2048,32]{0,1:T(8,128)(2,1)}, u32[]{:S(2)}) copy-start(bf16[2048,32]{0,1:T(8,128)(2,1)} %param.27) | copy-start | bytes 393220
  142.9 85.7 %copy-start.6 = (f32[1,2,8,128]{3,1,2,0:T(2,128)S(1)}, f32[1,2,8,128]{3,1,2,0:T(2,128)}, u32[]{:S(2)}) copy-start(f32[1,2,8,128]{3,1,2,0:T(2,128)} %copy.34) | copy-start | bytes 24580
  142.9 85.7 %copy-start.7 = (f32[64,128]{1,0:T(8,128)S(1)}, f32[64,128]{1,0:T(8,128)}, u32[]{:S(2)}) copy-start(f32[64,128]{1,0:T(8,128)} %get-tuple-element.61.gates_ref) | copy-start | bytes 98308
  142.9 85.7 %copy-start.8 = (f32[2048]{0:T(1024)S(1)}, f32[2048]{0:T(1024)}, u32[]{:S(2)}) copy-start(f32[2048]{0:T(1024)} %param.26) | copy-start | bytes 24580
  143.0 85.7 %copy-start.10 = (f32[128]{0:T(128)S(1)}, f32[128]{0:T(128)}, u32[]{:S(2)}) copy-start(f32[128]{0:T(128)} %param.23) | copy-start | bytes 1540
  228.7 32.5 %copy-start.5 = (f32[256,128]{1,0:T(8,128)S(1)}, f32[256,128]{1,0:T(8,128)}, u32[]{:S(2)}) copy-start(f32[256,128]{1,0:T(8,128)} %get-tuple-element.68.kraw_ref) | copy-start | bytes 393220
  228.7 32.5 %copy-start.9 = (f32[2048]{0:T(1024)S(1)}, f32[2048]{0:T(1024)}, u32[]{:S(2)}) copy-start(f32[2048]{0:T(1024)} %param.19) | copy-start | bytes 24580
  228.7 32.5 %copy-start.11 = (f32[128]{0:T(128)S(1)}, f32[128]{0:T(128)}, u32[]{:S(2)}) copy-start(f32[128]{0:T(128)} %param.24) | copy-start | bytes 1540
  260.4 0.8 copy-start.3
  331.6 26.8 %copy-start.15 = (bf16[256,2048]{1,0:T(8,128)(2,1)S(1)}, bf16[256,2048]{1,0:T(8,128)(2,1)}, u32[]{:S(2)}) copy-start(bf16[256,2048]{1,0:T(8,128)(2,1)} %get-tuple-element.133) | copy-start | bytes 3145732
  331.6 27.8 %copy-start.14 = (bf16[256,2048]{1,0:T(8,128)(2,1)S(1)}, bf16[256,2048]{1,0:T(8,128)(2,1)}, u32[]{:S(2)}) copy-start(bf16[256,2048]{1,0:T(8,128)(2,1)} %get-tuple-element.134) | copy-start | bytes 3145732
  358.4 2.0 copy-start.13
  358.4 2.9 copy-start.12

commit v7 on v6

--- a/solution.py
+++ b/solution.py
@@ -1200,7 +1200,7 @@
     swaps[0].wait_recv()
     gout_ref[...] = nn(att_t[...], back_ref[:, own_lanes]) + obuf[...].astype(f32)
     swaps[1].wait_recv()
-    grouter_ref[...] = grouter_both[x] + rbuf[...].astype(f32)
+    grouter_ref[...] = (grouter_both[x] + rbuf[...].astype(f32)).T[: grouter_ref.shape[0]]
     queries[1].pass_on(3)
     query_part(1)
     keys.pass_on(3)
@@ -1241,7 +1241,7 @@
             zcopy(zz, up, zz).wait_send()
 
 
-def tail(dkv, qlow, kraw, kg, cos, sin, wq, wk, wv, x, g1, gres, layer, gn2, qgain, first, att, back, rows_all, cid):
+def tail(dkv, qlow, kraw, kg, cos, sin, wq, wk, wv, x, g1, gres, layer, gn2, qgain, first, att, back, rows_all, experts, cid):
     tok, width = x.shape
     rows = gres.shape[0]
     half, head = dkv.shape[2:]
@@ -1263,7 +1263,7 @@
         out_shape=[
             out((tok, width), bf), out((tok, width), bf), out((per, qlow.shape[1]), f32),
             out((per, 2 * head), f32), out((att.shape[1], per), f32),
-            out((per, 128), f32), out((8, 128), f32),
+            out((experts, per), f32), out((8, 128), f32),
         ],
         scratch_shapes=[
             mem(*wq.shape), mem(*kg.shape, kind=f32), mem(*wk.shape), mem(*wv.shape), mem(*x.shape),
@@ -1957,7 +1957,7 @@
     grad_input, layer_out, grad_query, kv_grads, grad_out, grad_router, total = tail(
         grad_kv, query_low, key_raw, row(key_gain), cos, sin, w_query, key_weight, value_weight,
         tokens_in, row(norm1_gain), grad_residual, layer_piece, grad_norm2, qgain_part,
-        first_cols.reshape(line_tok, -1), attended_line.reshape(line_tok, -1), back_cols, all_rows, 8,
+        first_cols.reshape(line_tok, -1), attended_line.reshape(line_tok, -1), back_cols, all_rows, experts, 8,
     )
     per = model_width // devices // 128
     grad_key = kv_grads[:, :head_size]
@@ -1984,7 +1984,7 @@
         gain_of(7),
         grad_out,
         total[per : 2 * per].reshape(-1),
-        grad_router[:, :experts],
+        grad_router.T,
         grad_gate,
         grad_up,
         grad_down,

time: 363 us -> 363 us (level)
  no operation moved by 1% of the time
where the time goes in v7:
time: 363 us
  Pallas kernels  349 us (96%)
  local copies, waits for them, and re-layouts  9.52 us (3%)
    pallas_call x1, Pallas kernels, experts_forward(): pl.pallas_call(functools.partial(experts_kernel, own), in_specs=[anywhere...  90.5 us
    pallas_call x1, Pallas kernels, reduce_experts(): pl.pallas_call(reduce_kernel, in_specs=[anywhere] * 8, out_specs=[pl.Bloc...  85.4 us
    pallas_call x1, Pallas kernels, tail(): pl.pallas_call(tail_kernel, in_specs=[vm] * 3 + [anywhere] + [vm] * 2 + [...  67.5 us
    pallas_call x1, Pallas kernels, front(): pl.pallas_call(front_kernel, in_specs=[anywhere] * 7 + [vm] * 4 + [anywhe...  47.2 us
    pallas_call x1, Pallas kernels, middle(): pl.pallas_call(middle_kernel, in_specs=[vm] * 3 + [anywhere] * 4 + [vm] *...  32 us
    pallas_call x1, Pallas kernels, expert_grads(): pl.pallas_call(expert_grad_kernel, grid=(width // block, n // span), in_s...  26.8 us

profile of v7, /device:TPU:0, one launch (start us, length us, event | category | flops | bytes accessed | tf_op | source)
XLA Modules:
  0.0 362.6 jit_solution(11753961421083189087)
XLA Ops:
  0.7 0.7 fusion.1
  1.3 0.7 add_multiply_fusion
  2.0 0.1 copy.30
  2.2 0.1 add.29
  2.4 0.5 fusion
  2.9 0.8 pad_maximum_fusion
  3.8 0.8 broadcast_in_dim.2.qpos_ref
  4.5 0.6 copy.33
  5.1 47.2 %front.1 = (bf16[256,2048]{1,0:T(8,128)(2,1)}, f32[256,1024]{1,0:T(8,128)}, f32[256,128]{1,0:T(8,128)}, bf16[16,128,128]{2,1,0:T(8,128)(2,1)}, bf16[4,8,128,128]...) custom-call(bf16[256,2048]{1,0:T(8,128)(2,1)} %x_in.1, ...), custom_call_target="tpu_custom_call" | custom-call | tf_op jit(solution)/shard_map/front/pallas_call | solution.py:759
  52.3 90.5 %experts_forward.1 = (bf16[2048,4224]{1,0:T(8,128)(2,1)}, bf16[2048,128]{1,0:T(8,128)(2,1)}, bf16[2048,768]{1,0:T(8,128)(2,1)}, bf16[2048,768]{1,0:T(8,128)(2,1)...) custom-call(bf16[64,4224]{1,0:T(8,128)(2,1)} %get-tuple-element.53.p, ...), custom_call_target="tpu_custom_call" | custom-call | flops 19327352832 | bytes 41943040 | tf_op jit(solution)/shard_map/experts_forward/pallas_call | solution.py:1438
  142.9 85.4 %reduce_experts.1 = (f32[64,4224]{1,0:T(8,128)}, bf16[4,256,1024]{2,1,0:T(8,128)(2,1)}) custom-call(bf16[2048,768]{1,0:T(8,128)(2,1)} %get-tuple-element.54.hs_ref, bf16[2048,768]{1,0:T(8,128)(2,1)} %get-tuple-element.55.gl_ref, bf16[2048,768]{1,0:T(8,128)(2,1)} %get-tuple-element.56.ul_ref, bf16[2048,128]{1,0:T(8,128)(2,1)} %get-tuple-element.57.pair_ref, ...), custom_call_target="tpu_custom_call" | custom-call | flops 19327352832 | bytes 41943040 | tf_op jit(solution)/shard_map/reduce_experts/pallas_call | solution.py:365
  228.4 32.0 %middle.1 = (bf16[64,2048]{1,0:T(8,128)(2,1)S(1)}, f32[64,2048]{1,0:T(8,128)S(1)}, f32[1,2048]{1,0:T(1,128)S(1)}, bf16[4,4,64,640]{3,2,1,0:T(8,128)(2,1)}, bf16[...) custom-call(f32[64,4224]{1,0:T(8,128)} %get-tuple-element.59.sums_ref, ...), custom_call_target="tpu_custom_call" | custom-call | tf_op jit(solution)/shard_map/middle/pallas_call | solution.py:923
  260.5 0.8 copy-done.4
  261.3 67.5 %tail.1 = (bf16[256,2048]{1,0:T(8,128)(2,1)}, bf16[256,2048]{1,0:T(8,128)(2,1)}, f32[256,1024]{1,0:T(8,128)}, f32[256,256]{1,0:T(8,128)S(1)}, f32[1024,256]{1,0:...) custom-call(bf16[4,8,128,128]{3,2,1,0:T(8,128)(2,1)} %get-tuple-element.66.dkv_ref, ...), custom_call_target="tpu_custom_call" | custom-call | tf_op jit(solution)/shard_map/tail/pallas_call | solution.py:1259
  328.8 0.6 slice_bitcast_fusion
  329.4 0.7 fusion.4
  330.1 0.6 fusion.2
  330.7 0.6 fusion.3
  331.3 26.8 %expert_grads.1 = (f32[768,2048]{1,0:T(8,128)}, f32[768,2048]{1,0:T(8,128)}, f32[768,2048]{1,0:T(8,128)}) custom-call(bf16[2048,4224]{1,0:T(8,128)(2,1)} %get-tuple-element.76.rows_in.x_ref.cot_ref, bf16[2048,4224]{1,0:T(8,128)(2,1)} %get-tuple-element.76.rows_in.x_ref.cot_ref, bf16[768,2048]{1,0:T(8,128)(2,1)} %get-tuple-element.86.gl_ref, ...), custom_call_target="tpu_custom_call" | custom-call | flops 19327352832 | bytes 41943040 | tf_op jit(solution)/shard_map/expert_grads/pallas_call | solution.py:1565
  358.1 1.0 copy.39
  359.1 1.0 copy.40
  360.0 1.0 copy.41
  361.0 1.0 copy.42
  362.0 0.6 copy.43
  (40 shorter events, 0.3 us)
Async XLA Ops:
  142.8 85.5 %copy-start = (f32[256,128]{1,0:T(8,128)S(1)}, f32[256,128]{1,0:T(8,128)}, u32[]{:S(2)}) copy-start(f32[256,128]{1,0:T(8,128)} %get-tuple-element.103.cos_ref) | copy-start | bytes 393220
  142.8 85.5 %copy-start.1 = (f32[256,128]{1,0:T(8,128)S(1)}, f32[256,128]{1,0:T(8,128)}, u32[]{:S(2)}) copy-start(f32[256,128]{1,0:T(8,128)} %get-tuple-element.104.sin_ref) | copy-start | bytes 393220
  142.8 85.5 %copy-start.3 = (f32[256,128]{1,0:T(8,128)S(1)}, f32[256,128]{1,0:T(8,128)}, u32[]{:S(2)}) copy-start(f32[256,128]{1,0:T(8,128)} %broadcast_in_dim.2.qpos_ref) | copy-start | bytes 393220
  142.8 85.5 %copy-start.5 = (bf16[2048,32]{0,1:T(8,128)(2,1)S(1)}, bf16[2048,32]{0,1:T(8,128)(2,1)}, u32[]{:S(2)}) copy-start(bf16[2048,32]{0,1:T(8,128)(2,1)} %param.27) | copy-start | bytes 393220
  142.8 85.5 %copy-start.7 = (f32[1,2,8,128]{3,1,2,0:T(2,128)S(1)}, f32[1,2,8,128]{3,1,2,0:T(2,128)}, u32[]{:S(2)}) copy-start(f32[1,2,8,128]{3,1,2,0:T(2,128)} %copy.33) | copy-start | bytes 24580
  142.8 85.5 %copy-start.8 = (f32[64,128]{1,0:T(8,128)S(1)}, f32[64,128]{1,0:T(8,128)}, u32[]{:S(2)}) copy-start(f32[64,128]{1,0:T(8,128)} %get-tuple-element.61.gates_ref) | copy-start | bytes 98308
  142.9 85.5 %copy-start.9 = (f32[2048]{0:T(1024)S(1)}, f32[2048]{0:T(1024)}, u32[]{:S(2)}) copy-start(f32[2048]{0:T(1024)} %param.26) | copy-start | bytes 24580
  142.9 85.5 %copy-start.11 = (f32[128]{0:T(128)S(1)}, f32[128]{0:T(128)}, u32[]{:S(2)}) copy-start(f32[128]{0:T(128)} %param.23) | copy-start | bytes 1540
  228.4 32.9 %copy-start.2 = (bf16[2048,128]{1,0:T(8,128)(2,1)S(1)}, bf16[2048,128]{1,0:T(8,128)(2,1)}, u32[]{:S(2)}) copy-start(bf16[2048,128]{1,0:T(8,128)(2,1)} %wk_in.1) | copy-start | bytes 1572868
  228.4 32.9 %copy-start.6 = (f32[256,128]{1,0:T(8,128)S(1)}, f32[256,128]{1,0:T(8,128)}, u32[]{:S(2)}) copy-start(f32[256,128]{1,0:T(8,128)} %get-tuple-element.68.kraw_ref) | copy-start | bytes 393220
  228.4 32.9 %copy-start.10 = (f32[2048]{0:T(1024)S(1)}, f32[2048]{0:T(1024)}, u32[]{:S(2)}) copy-start(f32[2048]{0:T(1024)} %param.19) | copy-start | bytes 24580
  228.4 32.9 %copy-start.12 = (f32[128]{0:T(128)S(1)}, f32[128]{0:T(128)}, u32[]{:S(2)}) copy-start(f32[128]{0:T(128)} %param.24) | copy-start | bytes 1540
  260.5 0.8 copy-start.4
  331.3 26.8 %copy-start.16 = (bf16[256,2048]{1,0:T(8,128)(2,1)S(1)}, bf16[256,2048]{1,0:T(8,128)(2,1)}, u32[]{:S(2)}) copy-start(bf16[256,2048]{1,0:T(8,128)(2,1)} %get-tuple-element.119) | copy-start | bytes 3145732
  331.3 27.8 %copy-start.15 = (bf16[256,2048]{1,0:T(8,128)(2,1)S(1)}, bf16[256,2048]{1,0:T(8,128)(2,1)}, u32[]{:S(2)}) copy-start(bf16[256,2048]{1,0:T(8,128)(2,1)} %get-tuple-element.120) | copy-start | bytes 3145732
  358.1 2.0 copy-start.14
  358.1 2.9 copy-start.13
